TPU v7x, 32 devices: a whole 2x2x4 slice. The times are simulated.
32 devices in a mesh: rows: 2 (over core), seq: 16 (over z, y, x).
Axes of the slice: x: 2, y: 2, z: 4, core: 2. Of those that a mesh axis runs over, the one named last changes fastest.
Arguments:
- tokens: bfloat16 [2, 2048, 2048], P('rows', 'seq'), may hold values from -6 to 6
- out_grad: bfloat16 [2, 2048, 2048], P('rows', 'seq'), may hold values from -6 to 6
- doc_lengths: int32 [2, 2], P('rows'), may hold values from 1 to 1536, 2048 in all within a row
- norm_attn: bfloat16 [2048], P(('rows', 'seq')), may hold values from 0.099609375 to 1.8984375
- w_qdown: bfloat16 [2048, 1024], P(('rows', 'seq')), may hold values from -0.125 to 0.125
- norm_query: bfloat16 [1024], P(('rows', 'seq')), may hold values from 0.099609375 to 1.8984375
- w_qup: bfloat16 [1024, 4096], P(('rows', 'seq')), may hold values from -0.1875 to 0.1875
- w_key: bfloat16 [2048, 256], P(('rows', 'seq')), may hold values from -0.125 to 0.125
- w_value: bfloat16 [2048, 256], P(('rows', 'seq')), may hold values from -0.125 to 0.125
- w_out: bfloat16 [4096, 2048], P(None, ('rows', 'seq')), may hold values from -0.375 to 0.375
- norm_ffn: bfloat16 [2048], P(('rows', 'seq')), may hold values from 0.099609375 to 1.8984375
- w_gate: bfloat16 [2048, 5632], P('rows', 'seq'), may hold values from -0.125 to 0.125
- w_up: bfloat16 [2048, 5632], P('rows', 'seq'), may hold values from -0.125 to 0.125
- w_down: bfloat16 [5632, 2048], P('seq', 'rows'), may hold values from -0.078125 to 0.078125
Outputs:
- output: bfloat16 [2, 2048, 2048], P('rows', 'seq')
- grad_tokens: bfloat16 [2, 2048, 2048], P('rows', 'seq')
- grad_norm_attn: float32 [2048], P(('rows', 'seq'))
- grad_w_qdown: float32 [2048, 1024], P(('rows', 'seq'))
- grad_norm_query: float32 [1024], P(('rows', 'seq'))
- grad_w_qup: float32 [1024, 4096], P(('rows', 'seq'))
- grad_w_key: float32 [2048, 256], P(('rows', 'seq'))
- grad_w_value: float32 [2048, 256], P(('rows', 'seq'))
- grad_w_out: float32 [4096, 2048], P(None, ('rows', 'seq'))
- grad_norm_ffn: float32 [2048], P(('rows', 'seq'))
- grad_w_gate: float32 [2048, 5632], P('rows', 'seq')
- grad_w_up: float32 [2048, 5632], P('rows', 'seq')
- grad_w_down: float32 [5632, 2048], P('seq', 'rows')
Inputs may be any that keep to these rules, and one draw needn't show every extreme that they name: `doc_lengths`: in each row the 2 document lengths add up to 2048; the longest document of every row has at most 1536 tokens.
All inputs are finite; a program needn't handle non-finite values.
Results may differ from a plain program's by a relative error of at most 0.02.
Values may be sent and summed in bfloat16 or wider, within the bound.
No kernel may reach another device: no remote copies, remote signals or barrier semaphores. Data moves between devices by JAX's collectives and lax.ppermute only.
A program may use at most 512 MiB of HBM per device.

v0:
```python
import jax
import jax.numpy as jnp
from jax import lax
from jax.sharding import PartitionSpec as P

HEADS = 16
HD = 256


masked = -1e30
epsilon = 1e-05


def rms_norm(values, gain_vec):
    return (
        values * lax.rsqrt(jnp.mean(values * values, axis=-1, keepdims=True) + epsilon) * gain_vec
    )


def rope_tables(relative, half_dim):
    frequency = 1.0 / 10000.0 ** (jnp.arange(half_dim, dtype=jnp.float32) / half_dim)
    angles = relative.astype(jnp.float32)[..., None] * frequency
    return (jnp.cos(angles), jnp.sin(angles))


def rotate(values, cosine, sine_table):
    half_dim = values.shape[-1] // 2
    front_part = values[..., :half_dim]
    back_part = values[..., half_dim:]
    return jnp.concatenate(
        [
            front_part * cosine - back_part * sine_table,
            back_part * cosine + front_part * sine_table,
        ],
        axis=-1,
    )


def doc_layout(lengths, positions):
    doc_ends = jnp.cumsum(lengths)
    passed = positions[:, None] >= doc_ends[None, :]
    segment = jnp.sum(passed.astype(jnp.int32), axis=1)
    doc_start = jnp.sum(jnp.where(passed, lengths[None, :], 0), axis=1)
    return (segment, positions - doc_start)


def matmul_f32(left, right):
    return jnp.dot(left, right, preferred_element_type=jnp.float32)


def contract_last(left, right):
    return jnp.einsum("ik,jk->ij", left, right, preferred_element_type=jnp.float32)


def contract_first(left, right):
    return jnp.einsum("ki,kj->ij", left, right, preferred_element_type=jnp.float32)


def gated_unit(gate_act, upward):
    return jax.nn.silu(gate_act) * upward


def reduce_ffn(gradient):
    partial_sum = lax.psum_scatter(
        gradient.astype(jnp.bfloat16), "seq", scatter_dimension=1, tiled=True
    )
    return lax.psum_scatter(partial_sum, "rows", scatter_dimension=0, tiled=True).astype(
        jnp.float32
    )


def shards(
    tokens,
    out_grad,
    doc_lengths,
    norm_attn,
    w_qdown,
    norm_query,
    w_qup,
    w_key,
    w_value,
    w_out,
    norm_ffn,
    w_gate,
    w_up,
    w_down,
):
    row_tokens = tokens[0].astype(jnp.float32)
    count_local = row_tokens.shape[0]
    row_length = count_local * lax.axis_size("seq")
    offset = lax.axis_index("seq") * count_local
    key_positions = jnp.arange(row_length, dtype=jnp.int32)
    key_segment, key_relative = doc_layout(doc_lengths[0], key_positions)
    query_positions = offset + jnp.arange(count_local, dtype=jnp.int32)
    query_segment = lax.dynamic_slice_in_dim(key_segment, offset, count_local)
    query_relative = lax.dynamic_slice_in_dim(key_relative, offset, count_local)
    cosine, sine_table = rope_tables(query_relative, HD // 2)
    allowed = (query_segment[:, None] == key_segment[None, :]) & (
        key_positions[None, :] <= query_positions[:, None]
    )
    score_scale = HD ** (-0.5)
    gathered = (
        lax.all_gather(norm_attn, ("rows", "seq"), axis=0, tiled=True),
        lax.all_gather(w_qdown, ("rows", "seq"), axis=0, tiled=True),
        lax.all_gather(norm_query, ("rows", "seq"), axis=0, tiled=True),
        lax.all_gather(w_qup, ("rows", "seq"), axis=0, tiled=True),
        lax.all_gather(w_key, ("rows", "seq"), axis=0, tiled=True),
        lax.all_gather(w_value, ("rows", "seq"), axis=0, tiled=True),
        lax.all_gather(w_out, ("rows", "seq"), axis=1, tiled=True),
        lax.all_gather(norm_ffn, ("rows", "seq"), axis=0, tiled=True),
    )
    gain_attn = gathered[0].astype(jnp.float32)
    down_query = gathered[1]
    gain_query = gathered[2].astype(jnp.float32)
    up_query = gathered[3]
    key_proj = gathered[4]
    value_proj = gathered[5]
    out_proj = gathered[6]
    gain_ffn = gathered[7].astype(jnp.float32)
    normed_f, pull_attn_norm = jax.vjp(rms_norm, row_tokens, gain_attn)
    normed = normed_f.astype(jnp.bfloat16)
    latent = matmul_f32(normed, down_query)
    latent_f, pull_latent = jax.vjp(rms_norm, latent, gain_query)
    latent_normed = latent_f.astype(jnp.bfloat16)
    query_raw = matmul_f32(latent_normed, up_query).reshape(count_local, HEADS, HD)
    query_rot, pull_query = jax.vjp(
        lambda field: rotate(field, cosine[:, None, :], sine_table[:, None, :]), query_raw
    )
    queries = query_rot.astype(jnp.bfloat16).reshape(count_local * HEADS, HD)
    key_rot, pull_key = jax.vjp(
        lambda field: rotate(field, cosine, sine_table), matmul_f32(normed, key_proj)
    )
    key_local = key_rot.astype(jnp.bfloat16)
    value_local = matmul_f32(normed, value_proj).astype(jnp.bfloat16)
    all_keys, all_values = (
        lax.all_gather(key_local, "seq", axis=0, tiled=True),
        lax.all_gather(value_local, "seq", axis=0, tiled=True),
    )

    def masked_scores():
        raw_scores = (
            jnp.einsum("rd,kd->rk", queries, all_keys, preferred_element_type=jnp.float32)
            * score_scale
        )
        return jnp.where(
            allowed[:, None, :], raw_scores.reshape(count_local, HEADS, row_length), masked
        )

    scores = masked_scores()
    row_peak = jnp.max(scores, axis=-1, keepdims=True)
    log_total = row_peak + jnp.log(jnp.sum(jnp.exp(scores - row_peak), axis=-1, keepdims=True))
    probs_bf = (
        jnp.exp(scores - log_total).astype(jnp.bfloat16).reshape(count_local * HEADS, row_length)
    )
    attended = (
        matmul_f32(probs_bf, all_values).reshape(count_local, HEADS * HD).astype(jnp.bfloat16)
    )
    middle = row_tokens + matmul_f32(attended, out_proj)
    normed2_f, pull_ffn_norm = jax.vjp(rms_norm, middle, gain_ffn)
    normed_ffn = normed2_f.astype(jnp.bfloat16)
    upstream = out_grad[0]
    upstream_f = upstream.astype(jnp.float32)
    middle_w = (
        lax.all_gather(w_gate, "seq", axis=1, tiled=True),
        lax.all_gather(w_up, "seq", axis=1, tiled=True),
        lax.all_gather(w_down, "seq", axis=0, tiled=True),
    )
    gate_w, up_w, down_w = (
        lax.all_gather(middle_w[0], "rows", axis=0, tiled=True),
        lax.all_gather(middle_w[1], "rows", axis=0, tiled=True),
        lax.all_gather(middle_w[2], "rows", axis=1, tiled=True),
    )
    gate_act = matmul_f32(normed_ffn, gate_w)
    upward = matmul_f32(normed_ffn, up_w)
    hidden_f, pull_gated = jax.vjp(gated_unit, gate_act, upward)
    hidden = hidden_f.astype(jnp.bfloat16)
    output = middle + matmul_f32(hidden, down_w)
    grad_hidden = contract_last(upstream, down_w)
    down_grad = jnp.transpose(reduce_ffn(contract_first(upstream, hidden)))
    grad_gate_in, grad_up_in = pull_gated(grad_hidden)
    gate_b = grad_gate_in.astype(jnp.bfloat16)
    up_b = grad_up_in.astype(jnp.bfloat16)
    grad_normed_ffn = contract_last(gate_b, gate_w) + contract_last(up_b, up_w)
    gate_grad = reduce_ffn(contract_first(normed_ffn, gate_b))
    up_grad = reduce_ffn(contract_first(normed_ffn, up_b))
    ffn_grads = (gate_grad, up_grad, down_grad)
    grad_middle_norm, grad_gain_ffn = pull_ffn_norm(grad_normed_ffn)
    grad_middle = upstream_f + grad_middle_norm
    branch_grad = grad_middle.astype(jnp.bfloat16)
    grad_out_w = contract_first(attended, branch_grad)
    grad_attended = (
        contract_last(branch_grad, out_proj).astype(jnp.bfloat16).reshape(count_local * HEADS, HD)
    )
    scores = masked_scores()
    probs_f = jnp.exp(scores - log_total)
    probs_again = probs_f.astype(jnp.bfloat16).reshape(count_local * HEADS, row_length)
    grad_probs = jnp.einsum(
        "rd,kd->rk", grad_attended, all_values, preferred_element_type=jnp.float32
    ).reshape(count_local, HEADS, row_length)
    grad_scores = probs_f * (grad_probs - jnp.sum(grad_probs * probs_f, axis=-1, keepdims=True))
    grad_scores = grad_scores.astype(jnp.bfloat16).reshape(count_local * HEADS, row_length)
    grad_queries = matmul_f32(grad_scores, all_keys) * score_scale
    key_part = contract_first(grad_scores, queries) * score_scale
    value_part = contract_first(probs_again, grad_attended)
    grad_keys, grad_values = (
        lax.psum_scatter(
            key_part.astype(jnp.bfloat16), "seq", scatter_dimension=0, tiled=True
        ).astype(jnp.float32),
        lax.psum_scatter(
            value_part.astype(jnp.bfloat16), "seq", scatter_dimension=0, tiled=True
        ).astype(jnp.float32),
    )
    grad_query_raw = pull_query(grad_queries.reshape(count_local, HEADS, HD))[0]
    grad_query_raw = grad_query_raw.reshape(count_local, HEADS * HD).astype(jnp.bfloat16)
    grad_up_query = contract_first(latent_normed, grad_query_raw)
    grad_latent_normed = contract_last(grad_query_raw, up_query)
    grad_latent, grad_gain_query = pull_latent(grad_latent_normed)
    latent_b = grad_latent.astype(jnp.bfloat16)
    grad_down_query = contract_first(normed, latent_b)
    key_b = pull_key(grad_keys)[0].astype(jnp.bfloat16)
    value_b = grad_values.astype(jnp.bfloat16)
    grad_key_w = contract_first(normed, key_b)
    grad_value_w = contract_first(normed, value_b)
    grad_normed = (
        contract_last(latent_b, down_query)
        + contract_last(key_b, key_proj)
        + contract_last(value_b, value_proj)
    )
    grad_input_norm, grad_gain_attn = pull_attn_norm(grad_normed)
    grad_input = grad_middle + grad_input_norm
    attn_grads = (
        lax.psum_scatter(grad_gain_attn, ("rows", "seq"), scatter_dimension=0, tiled=True),
        lax.psum_scatter(grad_down_query, ("rows", "seq"), scatter_dimension=0, tiled=True),
        lax.psum_scatter(grad_gain_query, ("rows", "seq"), scatter_dimension=0, tiled=True),
        lax.psum_scatter(grad_up_query, ("rows", "seq"), scatter_dimension=0, tiled=True),
        lax.psum_scatter(grad_key_w, ("rows", "seq"), scatter_dimension=0, tiled=True),
        lax.psum_scatter(grad_value_w, ("rows", "seq"), scatter_dimension=0, tiled=True),
        lax.psum_scatter(grad_out_w, ("rows", "seq"), scatter_dimension=1, tiled=True),
        lax.psum_scatter(grad_gain_ffn, ("rows", "seq"), scatter_dimension=0, tiled=True),
    )
    return (
        output.astype(jnp.bfloat16)[None],
        grad_input.astype(jnp.bfloat16)[None],
        attn_grads[0],
        attn_grads[1],
        attn_grads[2],
        attn_grads[3],
        attn_grads[4],
        attn_grads[5],
        attn_grads[6],
        attn_grads[7],
        ffn_grads[0],
        ffn_grads[1],
        ffn_grads[2],
    )


def solution(mesh):
    placed = (
        P("rows", "seq", None),
        P("rows", "seq", None),
        P("rows", None),
        P(("rows", "seq")),
        P(("rows", "seq"), None),
        P(("rows", "seq")),
        P(("rows", "seq"), None),
        P(("rows", "seq"), None),
        P(("rows", "seq"), None),
        P(None, ("rows", "seq")),
        P(("rows", "seq")),
        P("rows", "seq"),
        P("rows", "seq"),
        P("seq", "rows"),
    )
    return jax.shard_map(
        shards,
        mesh=mesh,
        in_specs=placed,
        out_specs=(
            P("rows", "seq", None),
            P("rows", "seq", None),
            P(("rows", "seq")),
            P(("rows", "seq"), None),
            P(("rows", "seq")),
            P(("rows", "seq"), None),
            P(("rows", "seq"), None),
            P(("rows", "seq"), None),
            P(None, ("rows", "seq")),
            P(("rows", "seq")),
            P("rows", "seq"),
            P("rows", "seq"),
            P("seq", "rows"),
        ),
        check_vma=False,
    )
```

profile of v0, /device:TPU:0, one launch (start us, length us, event | category | flops | bytes accessed | tf_op | source)
XLA Modules:
  0.0 4258.8 jit_solution(3798030836438086052)
XLA Ops:
  15.3 42.1 all-reduce.11
  70.4 53.3 %all-gather.22.cloned.1.call-done = bf16[2048,256]{1,0:T(8,128)(2,1)} async-done(((bf16[64,256]{1,0:T(8,128)(2,1)}), bf16[2048,256]{1,0:T(8,128)(2,1)}) %all-gather.22.cloned.1.call-update) | async-done | bytes 1048592 | tf_op jit(solution)/shard_map/all_gather | solution.py:108
  126.7 140.8 %all-gather.32.cloned.1.call-done = bf16[1024,5632]{0,1:T(8,128)(2,1)} async-done(((bf16[1024,352]{0,1:T(8,128)(2,1)}), bf16[1024,5632]{0,1:T(8,128)(2,1)}) %all-gather.32.cloned.1.call-update) | async-done | bytes 11534352 | tf_op jit(solution)/shard_map/all_gather | solution.py:165
  267.6 142.9 %all-gather.28.cloned.1.call-done = bf16[1024,5632]{0,1:T(8,128)(2,1)} async-done(((bf16[1024,352]{0,1:T(8,128)(2,1)}), bf16[1024,5632]{0,1:T(8,128)(2,1)}) %all-gather.28.cloned.1.call-update) | async-done | bytes 11534352 | tf_op jit(solution)/shard_map/all_gather | solution.py:164
  410.6 142.9 %all-gather.36.cloned.1.call-done = bf16[5632,1024]{1,0:T(8,128)(2,1)} async-done(((bf16[352,1024]{1,0:T(8,128)(2,1)}), bf16[5632,1024]{1,0:T(8,128)(2,1)}) %all-gather.36.cloned.1.call-update) | async-done | bytes 11534352 | tf_op jit(solution)/shard_map/all_gather | solution.py:166
  554.1 62.5 %all-gather.14.cloned.1.call-done = bf16[2048,1024]{1,0:T(8,128)(2,1)} async-done(((bf16[64,1024]{1,0:T(8,128)(2,1)}), bf16[2048,1024]{1,0:T(8,128)(2,1)}) %all-gather.14.cloned.1.call-update) | async-done | bytes 4194320 | tf_op jit(solution)/shard_map/all_gather | solution.py:104
  619.7 75.9 %all-gather.16.cloned.1.call-done = bf16[1024,4096]{1,0:T(8,128)(2,1)} async-done(((bf16[32,4096]{1,0:T(8,128)(2,1)}), bf16[1024,4096]{1,0:T(8,128)(2,1)}) %all-gather.16.cloned.1.call-update) | async-done | bytes 8388624 | tf_op jit(solution)/shard_map/all_gather | solution.py:106
  703.4 49.4 %all-gather.20.cloned.1.call-done = bf16[2048,256]{1,0:T(8,128)(2,1)} async-done(((bf16[128,256]{1,0:T(8,128)(2,1)}), bf16[2048,256]{1,0:T(8,128)(2,1)}) %all-gather.20.cloned.1.call-update) | async-done | bytes 1048592 | tf_op jit(solution)/shard_map/all_gather | solution.py:136
  769.0 41.2 all-gather.24.cloned.1.call-done
  816.8 110.0 %all-gather.26.cloned.1.call-done = bf16[4096,2048]{0,1:T(8,128)(2,1)} async-done(((bf16[4096,64]{0,1:T(8,128)(2,1)}), bf16[4096,2048]{0,1:T(8,128)(2,1)}) %all-gather.26.cloned.1.call-update) | async-done | bytes 16777232 | tf_op jit(solution)/shard_map/all_gather | solution.py:109
  938.6 25.8 all-gather.34.cloned.1.call-done
  964.5 14.3 fusion.79
  978.8 26.2 all-gather.30.cloned.1.call-done
  1005.0 14.6 fusion.78
  1019.6 26.0 all-gather.38.cloned.1.call-done
  1045.7 14.9 multiply_convert_fusion.1
  1072.8 12.9 convolution_convert_fusion.1
  1108.4 13.1 multiply_reduce_fusion.1
  1136.3 23.6 multiply_reduce_fusion
  1159.9 20.9 multiply_convert_fusion
  1187.8 359.3 %reduce-scatter.32.cloned.1.call-done = bf16[2048,352]{0,1:T(8,128)(2,1)} async-done(((bf16[2048,5632]{0,1:T(8,128)(2,1)}), bf16[2048,352]{0,1:T(8,128)(2,1)}) %reduce-scatter.32.cloned.1.call-update) | async-done | bytes 1441808 | tf_op jit(solution)/shard_map/reduce_scatter | solution.py:64
  1547.2 481.9 %reduce-scatter.28.cloned.1.call-done = bf16[2048,352]{0,1:T(8,128)(2,1)} async-done(((bf16[2048,5632]{0,1:T(8,128)(2,1)}), bf16[2048,352]{0,1:T(8,128)(2,1)}) %reduce-scatter.28.cloned.1.call-update) | async-done | bytes 1441808 | tf_op jit(solution)/shard_map/reduce_scatter | solution.py:64
  2029.1 481.9 %reduce-scatter.36.cloned.1.call-done = bf16[2048,352]{0,1:T(8,128)(2,1)} async-done(((bf16[2048,5632]{0,1:T(8,128)(2,1)}), bf16[2048,352]{0,1:T(8,128)(2,1)}) %reduce-scatter.36.cloned.1.call-update) | async-done | bytes 1441808 | tf_op jit(solution)/shard_map/reduce_scatter | solution.py:64
  2511.2 87.1 %reduce-scatter.16.cloned.1.call-done = bf16[128,256]{1,0:T(8,128)(2,1)} async-done(((bf16[2048,256]{1,0:T(8,128)(2,1)}), bf16[128,256]{1,0:T(8,128)(2,1)}) %reduce-scatter.16.cloned.1.call-update) | async-done | bytes 65552 | tf_op jit(solution)/shard_map/reduce_scatter | solution.py:209
  2601.0 74.3 %reduce-scatter.14.cloned.1.call-done = bf16[128,256]{1,0:T(8,128)(2,1)} async-done(((bf16[2048,256]{1,0:T(8,128)(2,1)}), bf16[128,256]{1,0:T(8,128)(2,1)}) %reduce-scatter.14.cloned.1.call-update) | async-done | bytes 65552 | tf_op jit(solution)/shard_map/reduce_scatter | solution.py:206
  2724.6 14.5 fusion.37
  2754.1 37.4 all-reduce.10
  2801.5 52.3 %reduce-scatter.24.cloned.1.call-done = f32[64,256]{1,0:T(8,128)} async-done(((f32[2048,256]{1,0:T(8,128)}), f32[64,256]{1,0:T(8,128)}) %reduce-scatter.24.cloned.1.call-update) | async-done | bytes 65552 | tf_op jit(solution)/shard_map/reduce_scatter | solution.py:237
  2853.8 142.3 %reduce-scatter.22.cloned.1.call-done = f32[64,256]{1,0:T(8,128)} async-done(((f32[2048,256]{1,0:T(8,128)}), f32[64,256]{1,0:T(8,128)}) %reduce-scatter.22.cloned.1.call-update) | async-done | bytes 65552 | tf_op jit(solution)/shard_map/reduce_scatter | solution.py:236
  2996.1 183.4 %reduce-scatter.18.cloned.1.call-done = f32[64,1024]{1,0:T(8,128)} async-done(((f32[2048,1024]{1,0:T(8,128)}), f32[64,1024]{1,0:T(8,128)}) %reduce-scatter.18.cloned.1.call-update) | async-done | bytes 262160 | tf_op jit(solution)/shard_map/reduce_scatter | solution.py:233
  3179.6 361.0 %reduce-scatter.20.cloned.1.call-done = f32[32,4096]{1,0:T(8,128)} async-done(((f32[1024,4096]{1,0:T(8,128)}), f32[32,4096]{1,0:T(8,128)}) %reduce-scatter.20.cloned.1.call-update) | async-done | bytes 524304 | tf_op jit(solution)/shard_map/reduce_scatter | solution.py:235
  3540.6 711.5 %reduce-scatter.26.cloned.1.call-done = f32[4096,64]{0,1:T(8,128)} async-done(((f32[4096,2048]{0,1:T(8,128)}), f32[4096,64]{0,1:T(8,128)}) %reduce-scatter.26.cloned.1.call-update) | async-done | bytes 1048592 | tf_op jit(solution)/shard_map/reduce_scatter | solution.py:238
  (220 shorter events, 203.4 us)
Async XLA Ops:
  7.2 60.4 %all-gather.18.cloned.1.call-start = ((), (), s32[]{:S(2)}) async-start(), calls=%async_computation.15 | async-start | bytes 1081344 | tf_op jit(solution)/shard_map/all_gather | solution.py:107
  7.9 115.8 %all-gather.22.cloned.1.call-start = ((), (), s32[]{:S(2)}) async-start(), calls=%async_computation.17 | async-start | bytes 1081344 | tf_op jit(solution)/shard_map/all_gather | solution.py:108
  8.7 258.8 %all-gather.32.cloned.1.call-start = ((), (), s32[]{:S(2)}) async-start(), calls=%async_computation.22 | async-start | bytes 12255232 | tf_op jit(solution)/shard_map/all_gather | solution.py:165
  9.4 401.1 %all-gather.28.cloned.1.call-start = ((), (), s32[]{:S(2)}) async-start(), calls=%async_computation.20 | async-start | bytes 12255232 | tf_op jit(solution)/shard_map/all_gather | solution.py:164
  10.0 543.5 %all-gather.36.cloned.1.call-start = ((), (), s32[]{:S(2)}) async-start(), calls=%async_computation.24 | async-start | bytes 12255232 | tf_op jit(solution)/shard_map/all_gather | solution.py:166
  10.6 606.0 %all-gather.14.cloned.1.call-start = ((), (), s32[]{:S(2)}) async-start(), calls=%async_computation.13 | async-start | bytes 4325376 | tf_op jit(solution)/shard_map/all_gather | solution.py:104
  11.1 684.5 %all-gather.16.cloned.1.call-start = ((), (), s32[]{:S(2)}) async-start(), calls=%async_computation.14 | async-start | bytes 8650752 | tf_op jit(solution)/shard_map/all_gather | solution.py:106
  11.9 740.9 %all-gather.20.cloned.1.call-start = ((), (), s32[]{:S(2)}) async-start(), calls=%async_computation.16 | async-start | bytes 1114112 | tf_op jit(solution)/shard_map/all_gather | solution.py:136
  69.7 631.5 %copy-start.18 = (f32[128,128]{1,0:T(8,128)}, f32[128,128]{1,0:T(8,128)S(1)}, u32[]{:S(2)}) copy-start(f32[128,128]{1,0:T(8,128)S(1)} %get-tuple-element.42) | copy-start | bytes 196612
  69.7 631.5 %copy-start.20 = (f32[128,128]{1,0:T(8,128)}, f32[128,128]{1,0:T(8,128)S(1)}, u32[]{:S(2)}) copy-start(f32[128,128]{1,0:T(8,128)S(1)} %get-tuple-element.43) | copy-start | bytes 196612
  70.3 739.9 %all-gather.24.cloned.1.call-start = ((), (), s32[]{:S(2)}) async-start(), calls=%async_computation.18 | async-start | bytes 1114112 | tf_op jit(solution)/shard_map/all_gather | solution.py:137
  126.1 800.7 %all-gather.26.cloned.1.call-start = ((), (), s32[]{:S(2)}) async-start(), calls=%async_computation.19 | async-start | bytes 17301504 | tf_op jit(solution)/shard_map/all_gather | solution.py:109
  126.7 837.8 %all-gather.34.cloned.1.call-start = ((), (), s32[]{:S(2)}) async-start(), calls=%async_computation.23 | async-start | bytes 34603008 | tf_op jit(solution)/shard_map/all_gather | solution.py:170
  267.5 737.4 %all-gather.30.cloned.1.call-start = ((), (), s32[]{:S(2)}) async-start(), calls=%async_computation.21 | async-start | bytes 34603008 | tf_op jit(solution)/shard_map/all_gather | solution.py:169
  410.5 635.1 %all-gather.38.cloned.1.call-start = ((), (), s32[]{:S(2)}) async-start(), calls=%async_computation.25 | async-start | bytes 34603008 | tf_op jit(solution)/shard_map/all_gather | solution.py:171
  553.5 993.6 %reduce-scatter.32.cloned.1.call-start = ((), (), s32[]{:S(2)}) async-start(), calls=%async_computation.35 | async-start | bytes 24510464 | tf_op jit(solution)/shard_map/reduce_scatter | solution.py:64
  1072.8 956.3 %reduce-scatter.28.cloned.1.call-start = ((), (), s32[]{:S(2)}) async-start(), calls=%async_computation.33 | async-start | bytes 24510464 | tf_op jit(solution)/shard_map/reduce_scatter | solution.py:64
  1085.8 1425.3 %reduce-scatter.36.cloned.1.call-start = ((), (), s32[]{:S(2)}) async-start(), calls=%async_computation.37 | async-start | bytes 24510464 | tf_op jit(solution)/shard_map/reduce_scatter | solution.py:64
  1098.2 1500.0 %reduce-scatter.16.cloned.1.call-start = ((), (), s32[]{:S(2)}) async-start(), calls=%async_computation.27 | async-start | bytes 1114112 | tf_op jit(solution)/shard_map/reduce_scatter | solution.py:209
  1136.2 1539.1 %reduce-scatter.14.cloned.1.call-start = ((), (), s32[]{:S(2)}) async-start(), calls=%async_computation.26 | async-start | bytes 1114112 | tf_op jit(solution)/shard_map/reduce_scatter | solution.py:206
  1184.1 1414.1 %copy-start.17 = (f32[2048]{0:T(1024)S(1)}, f32[2048]{0:T(1024)}, u32[]{:S(2)}) copy-start(f32[2048]{0:T(1024)} %copy-done.16) | copy-start | bytes 24580
  1184.1 1414.1 %copy-start.27 = (f32[128]{0:T(128)S(1)}, f32[128]{0:T(128)}, u32[]{:S(2)}) copy-start(f32[128]{0:T(128)} %copy-done.26) | copy-start | bytes 1540
  1187.7 1488.4 %copy-start.32 = (f32[128]{0:T(128)S(1)}, f32[128]{0:T(128)}, u32[]{:S(2)}) copy-start(f32[128]{0:T(128)} %copy-done.31) | copy-start | bytes 1540
  1187.7 1488.4 %copy-start.34 = (f32[128]{0:T(128)S(1)}, f32[128]{0:T(128)}, u32[]{:S(2)}) copy-start(f32[128]{0:T(128)} %copy-done.33) | copy-start | bytes 1540
  1187.8 1606.6 %reduce-scatter.34.cloned.1.call-start = ((), (), s32[]{:S(2)}) async-start(), calls=%async_computation.36 | async-start | bytes 2162688 | tf_op jit(solution)/shard_map/reduce_scatter | solution.py:67
  1547.1 1249.6 %reduce-scatter.30.cloned.1.call-start = ((), (), s32[]{:S(2)}) async-start(), calls=%async_computation.34 | async-start | bytes 2162688 | tf_op jit(solution)/shard_map/reduce_scatter | solution.py:67
  2029.1 770.0 %reduce-scatter.38.cloned.1.call-start = ((), (), s32[]{:S(2)}) async-start(), calls=%async_computation.38 | async-start | bytes 2162688 | tf_op jit(solution)/shard_map/reduce_scatter | solution.py:67
  2511.1 342.7 %reduce-scatter.24.cloned.1.call-start = ((), (), s32[]{:S(2)}) async-start(), calls=%async_computation.31 | async-start | bytes 2162688 | tf_op jit(solution)/shard_map/reduce_scatter | solution.py:237
  2600.9 395.2 %reduce-scatter.22.cloned.1.call-start = ((), (), s32[]{:S(2)}) async-start(), calls=%async_computation.30 | async-start | bytes 2162688 | tf_op jit(solution)/shard_map/reduce_scatter | solution.py:236
  2678.4 501.1 %reduce-scatter.18.cloned.1.call-start = ((), (), s32[]{:S(2)}) async-start(), calls=%async_computation.28 | async-start | bytes 8650752 | tf_op jit(solution)/shard_map/reduce_scatter | solution.py:233
  2714.7 825.8 %reduce-scatter.20.cloned.1.call-start = ((), (), s32[]{:S(2)}) async-start(), calls=%async_computation.29 | async-start | bytes 17301504 | tf_op jit(solution)/shard_map/reduce_scatter | solution.py:235
  2724.5 1527.5 %reduce-scatter.26.cloned.1.call-start = ((), (), s32[]{:S(2)}) async-start(), calls=%async_computation.32 | async-start | bytes 34603008 | tf_op jit(solution)/shard_map/reduce_scatter | solution.py:238
  (37 other events, 2967.9 us)
Sparse Core Ops, SparseCore 0:
  11.1 56.4 all-gather.17
  70.7 52.9 all-gather.21
  126.4 141.0 all-gather.31
  270.1 140.3 all-gather.27
  413.1 140.3 all-gather.35
  556.3 60.2 all-gather.13
  619.4 76.0 all-gather.15
  698.9 53.8 all-gather.19
  756.2 54.0 all-gather.23
  813.1 113.6 all-gather.25
  928.4 36.0 all-gather.33
  965.9 39.0 all-gather.29
  1006.5 39.0 all-gather.37
  1072.9 474.1 reduce-scatter.31
  1549.3 479.7 reduce-scatter.27
  2031.2 479.8 reduce-scatter.35
  2513.8 84.4 reduce-scatter.15
  2601.0 74.2 reduce-scatter.13
  2677.5 5.2 reduce-scatter.33
  2685.0 10.1 reduce-scatter.29
  2697.4 10.1 reduce-scatter.37
  2710.5 143.2 reduce-scatter.23
  2856.7 139.3 reduce-scatter.21
  2998.9 180.5 reduce-scatter.17
  3182.5 357.9 reduce-scatter.19
  3543.4 708.5 reduce-scatter.25
where the time goes:
time: 4270 us; the launch traced here: 4260 us
  waiting for transfers between devices  3850 us (90%)
  matrix products  239 us (6%)
  blocking collectives  79.5 us (2%)
  other arithmetic  50.6 us (1%)
    reduce_scatter x3, waiting for transfers between devices, reduce_ffn(): lax.psum_scatter(gradient.astype(jnp.bfloat16), 'seq', scatter_dimension=...  1320 us
    reduce_scatter x1, waiting for transfers between devices, shards(): lax.psum_scatter(grad_out_w, ('rows', 'seq'), scatter_dimension=1, tiled=...  711 us
    reduce_scatter x1, waiting for transfers between devices, shards(): lax.psum_scatter(grad_up_query, ('rows', 'seq'), scatter_dimension=0, til...  361 us
    reduce_scatter x1, waiting for transfers between devices, shards(): lax.psum_scatter(grad_down_query, ('rows', 'seq'), scatter_dimension=0, t...  183 us
    all_gather x1, waiting for transfers between devices, shards(): lax.all_gather(w_gate, 'seq', axis=1, tiled=True)  143 us
    all_gather x1, waiting for transfers between devices, shards(): lax.all_gather(w_down, 'seq', axis=0, tiled=True)  143 us
    reduce_scatter x1, waiting for transfers between devices, shards(): lax.psum_scatter(grad_key_w, ('rows', 'seq'), scatter_dimension=0, tiled=...  142 us
    all_gather x1, waiting for transfers between devices, shards(): lax.all_gather(w_up, 'seq', axis=1, tiled=True)  141 us
  transfers between devices with their start and end apart: 26, of which 23 were waited for; matrix products, arithmetic and copies ran while one was open for 7% of the time, Pallas kernels for 0%

commit v1 on v0

v1 whole, which is shorter than its diff:
```python
import jax
import jax.numpy as jnp
import numpy as np
from jax import lax
from jax.sharding import Mesh, PartitionSpec as P

HEADS = 16
HD = 256
PLANE = 4

masked = -1e30
epsilon = 1e-05
BF = jnp.bfloat16
F32 = jnp.float32


def rms_norm(values, gain_vec):
    return (
        values * lax.rsqrt(jnp.mean(values * values, axis=-1, keepdims=True) + epsilon) * gain_vec
    )


def rope_tables(relative, half_dim):
    frequency = 1.0 / 10000.0 ** (jnp.arange(half_dim, dtype=F32) / half_dim)
    angles = relative.astype(F32)[..., None] * frequency
    return (jnp.cos(angles), jnp.sin(angles))


def rotate(values, cosine, sine_table):
    half_dim = values.shape[-1] // 2
    front = values[..., :half_dim]
    back = values[..., half_dim:]
    return jnp.concatenate(
        [front * cosine - back * sine_table, back * cosine + front * sine_table], axis=-1
    )


def doc_layout(lengths, positions):
    doc_ends = jnp.cumsum(lengths)
    passed = positions[:, None] >= doc_ends[None, :]
    segment = jnp.sum(passed.astype(jnp.int32), axis=1)
    doc_start = jnp.sum(jnp.where(passed, lengths[None, :], 0), axis=1)
    return (segment, positions - doc_start)


def mm(left, right):
    return jnp.dot(left, right, preferred_element_type=F32)


def mm_nt(left, right):
    return jnp.einsum("ik,jk->ij", left, right, preferred_element_type=F32)


def mm_tn(left, right):
    return jnp.einsum("ki,kj->ij", left, right, preferred_element_type=F32)


def shift(value, axis, by=1):
    count = lax.axis_size(axis)
    return lax.ppermute(value, axis, [(i, (i + by) % count) for i in range(count)])


def ring_gather(value, axis):
    pieces = [value]
    for _ in range(lax.axis_size(axis) - 1):
        pieces.append(shift(pieces[-1], axis))
    return pieces


def ring_spread(value, axis):
    return [value] + [shift(value, axis, k) for k in range(1, lax.axis_size(axis))]


def ring_scatter(parts, axis):
    total = parts[1]
    for k in range(2, len(parts) + 1):
        total = shift(total.astype(BF), axis).astype(F32) + parts[k % len(parts)]
    return total


def flip(value, by):
    if by == 3:
        return lax.ppermute(value, ("py", "px"), [(i, i ^ 3) for i in range(PLANE)])
    return lax.ppermute(value, "px" if by == 1 else "py", [(0, 1), (1, 0)])


def halves(value, axis=0):
    half = value.shape[axis] // 2
    return (
        lax.slice_in_dim(value, 0, half, axis=axis),
        lax.slice_in_dim(value, half, 2 * half, axis=axis),
    )


def plane_gather(value, axis=0):
    over_x = flip(value, 1)
    over_y = flip(value, 2)
    first = flip(halves(over_x, axis)[0], 2)
    second = flip(halves(over_y, axis)[1], 1)
    return [value, over_x, over_y, jnp.concatenate([first, second], axis=axis)]


def plane_scatter(parts, axis=0):
    own_a, own_b = halves(parts[0], axis)
    x_a, x_b = halves(parts[1], axis)
    y_a, y_b = halves(parts[2], axis)
    d_a, d_b = halves(parts[3], axis)
    got_xa = flip(d_a.astype(BF), 2)
    got_yb = flip(d_b.astype(BF), 1)
    got_xb = flip(x_b.astype(BF), 1)
    got_ya = flip(y_a.astype(BF), 2)
    fin_a = flip((x_a + got_xa.astype(F32)).astype(BF), 1)
    fin_b = flip((y_b + got_yb.astype(F32)).astype(BF), 2)
    return jnp.concatenate(
        [
            own_a + got_ya.astype(F32) + fin_a.astype(F32),
            own_b + got_xb.astype(F32) + fin_b.astype(F32),
        ],
        axis=axis,
    )


def plane_swap(parts):
    return [parts[0]] + [flip(parts[k], k) for k in range(1, PLANE)]


def pick(stacked, index):
    return lax.dynamic_index_in_dim(stacked, index, 0, keepdims=False)


def plane_order(pieces, place, axis=0):
    stacked = jnp.stack(pieces)
    return jnp.concatenate([pick(stacked, place ^ i) for i in range(PLANE)], axis=axis)


def ring_order(pieces, place, axis=0):
    count = len(pieces)
    stacked = jnp.stack(pieces)
    return jnp.concatenate([pick(stacked, (place - i) % count) for i in range(count)], axis=axis)


def block_of(value, index, size, axis=0):
    return lax.dynamic_slice_in_dim(value, index * size, size, axis)


def swap_features(value, place, count):
    if count == 1:
        return value
    size = value.shape[1] // count
    return jnp.concatenate(
        [block_of(value, (place - k) % count, size, 1) for k in range(count)], axis=1
    )


def plane_ring_weight(parts, spot):
    row, ring, plane = spot
    got = plane_order(plane_swap([pick(parts, plane ^ k) for k in range(PLANE)]), plane)
    got = ring_order(ring_spread(got, "ring"), ring)
    return ring_order(ring_spread(got, "rows"), row)


def plane_ring_gradient(gradient, spot):
    row, ring, plane = spot
    rows, rings = lax.axis_size("rows"), lax.axis_size("ring")
    size = gradient.shape[0] // rows
    total = ring_scatter([block_of(gradient, (row - k) % rows, size) for k in range(rows)], "rows")
    size //= rings
    total = ring_scatter([block_of(total, (ring - k) % rings, size) for k in range(rings)], "ring")
    size //= PLANE
    total = total.astype(BF)
    got = plane_swap([block_of(total, plane ^ k, size) for k in range(PLANE)])
    stacked = jnp.stack(got)
    return [pick(stacked, plane ^ i).astype(F32) for i in range(PLANE)]


def shards(
    tokens,
    out_grad,
    doc_lengths,
    norm_attn,
    w_qdown,
    norm_query,
    w_qup,
    w_key,
    w_value,
    w_out,
    norm_ffn,
    w_gate,
    w_up,
    w_down,
):
    rows, rings = lax.axis_size("rows"), lax.axis_size("ring")
    devices = rows * rings * PLANE
    row = lax.axis_index("rows")
    ring = lax.axis_index("ring")
    plane = lax.axis_index("py") * 2 + lax.axis_index("px")
    spot = (row, ring, plane)
    own_tokens = tokens[0]
    count_local, width = own_tokens.shape
    group = count_local * PLANE
    row_length = group * rings
    heads = HEADS // PLANE
    score_scale = HD ** (-0.5)

    group_tokens = plane_order(plane_gather(own_tokens), plane).astype(F32)

    gains = jnp.concatenate([norm_attn, norm_query, norm_ffn])[None]
    gains = ring_order(ring_spread(gains, "rows"), row)
    part_a, part_q = norm_attn.shape[0], norm_query.shape[0]
    gains = plane_order(plane_swap([gains] * PLANE), plane)
    gains = ring_order(ring_spread(gains, "ring"), ring)
    gains = gains.reshape(rings, PLANE, rows, -1).transpose(2, 0, 1, 3).reshape(devices, -1)
    gains = gains.astype(F32)
    gain_attn = gains[:, :part_a].reshape(-1)
    gain_query = gains[:, part_a : part_a + part_q].reshape(-1)
    gain_ffn = gains[:, part_a + part_q :].reshape(-1)

    latent_width = w_qdown.shape[1] // PLANE
    kv_width = 2 * HD // PLANE
    kv_w = jnp.concatenate([w_key, w_value], axis=1)
    down_parts = jnp.stack(
        [
            jnp.concatenate(
                [
                    w_qdown[:, i * latent_width : (i + 1) * latent_width],
                    kv_w[:, i * kv_width : (i + 1) * kv_width],
                ],
                axis=1,
            )
            for i in range(PLANE)
        ]
    )
    down_w = plane_ring_weight(down_parts, spot)
    up_query = plane_ring_weight(
        w_qup.reshape(w_qup.shape[0], PLANE, -1).transpose(1, 0, 2), spot
    )
    out_t = jnp.transpose(w_out)
    out_proj = plane_ring_weight(
        out_t.reshape(out_t.shape[0], PLANE, -1).transpose(1, 0, 2), spot
    )

    key_positions = jnp.arange(row_length, dtype=jnp.int32)
    key_segment, key_relative = doc_layout(doc_lengths[0], key_positions)
    offset = ring * group
    query_positions = offset + jnp.arange(group, dtype=jnp.int32)
    query_segment = lax.dynamic_slice_in_dim(key_segment, offset, group)
    key_cos, key_sin = rope_tables(key_relative, HD // 2)
    cosine = lax.dynamic_slice_in_dim(key_cos, offset, group)[:, None, :]
    sine_table = lax.dynamic_slice_in_dim(key_sin, offset, group)[:, None, :]
    allowed = (query_segment[:, None] == key_segment[None, :]) & (
        key_positions[None, :] <= query_positions[:, None]
    )

    hidden_w = jnp.stack([jnp.transpose(w_gate), jnp.transpose(w_up), w_down])
    hidden_w = jnp.concatenate(plane_gather(hidden_w, 1), axis=1)
    ffn_w = ring_gather(hidden_w, "rows")
    hidden_units = hidden_w.shape[1]
    feat = hidden_w.shape[2]
    gate_up_w = [w[:2].reshape(2 * hidden_units, feat) for w in ffn_w]
    down_ffn_w = [w[2] for w in ffn_w]

    upstream = out_grad[0]
    upstream_f = upstream.astype(F32)
    ring_upstream = jnp.concatenate(ring_gather(swap_features(upstream, row, rows), "ring"))

    normed_f = rms_norm(group_tokens, gain_attn)
    normed = normed_f.astype(BF)
    projected = mm(normed, down_w).astype(BF)
    key_value = projected[:, latent_width:]
    key_value = ring_order(ring_gather(key_value, "ring"), ring)
    key_value = jnp.stack(plane_gather(key_value))
    key_value = [pick(key_value, plane ^ i) for i in range(PLANE)]
    key_raw = jnp.concatenate(key_value[:2], axis=1).astype(F32)
    all_keys = rotate(key_raw, key_cos, key_sin).astype(BF)
    all_values = jnp.concatenate(key_value[2:], axis=1)

    latent = plane_order(plane_gather(projected[:, :latent_width]), plane, axis=1).astype(F32)
    latent_normed = rms_norm(latent, gain_query).astype(BF)
    query_raw = mm(latent_normed, up_query).reshape(group, heads, HD)
    queries = rotate(query_raw, cosine, sine_table).astype(BF).reshape(group * heads, HD)

    def masked_scores():
        raw_scores = mm_nt(queries, all_keys) * score_scale
        return jnp.where(
            allowed[:, None, :], raw_scores.reshape(group, heads, row_length), masked
        )

    scores = masked_scores()
    row_peak = jnp.max(scores, axis=-1, keepdims=True)
    log_total = row_peak + jnp.log(jnp.sum(jnp.exp(scores - row_peak), axis=-1, keepdims=True))
    probs_bf = jnp.exp(scores - log_total).astype(BF).reshape(group * heads, row_length)
    attended = mm(probs_bf, all_values).reshape(group, heads * HD).astype(BF)
    branch = mm_nt(attended, out_proj)
    branch = plane_scatter([block_of(branch, plane ^ k, count_local) for k in range(PLANE)])
    middle = own_tokens.astype(F32) + branch

    normed2_f, pull_ffn_norm = jax.vjp(rms_norm, middle, gain_ffn)
    normed_ffn = swap_features(normed2_f.astype(BF), row, rows)
    ring_normed = jnp.concatenate(ring_gather(normed_ffn, "ring"))

    def feature_blocks(value):
        return [value[:, k * feat : (k + 1) * feat] for k in range(rows)]

    h2_blocks = feature_blocks(ring_normed)
    dy_blocks = feature_blocks(ring_upstream)
    gate_up = sum(mm_nt(h, w) for h, w in zip(h2_blocks, gate_up_w))
    grad_hidden = sum(mm_nt(d, w) for d, w in zip(dy_blocks, down_ffn_w))

    def gated_unit(both):
        return jax.nn.silu(both[:, :hidden_units]) * both[:, hidden_units:]

    hidden_f, pull_gated = jax.vjp(gated_unit, gate_up)
    hidden = hidden_f.astype(BF)
    grad_gate_up = pull_gated(grad_hidden)[0].astype(BF)

    def ring_parts(blocks):
        whole = jnp.concatenate(blocks, axis=1)
        return [whole[k * count_local : (k + 1) * count_local] for k in range(rings)]

    grad_normed_ffn = ring_scatter(ring_parts([mm(grad_gate_up, w) for w in gate_up_w]), "ring")
    grad_normed_ffn = swap_features(grad_normed_ffn, row, rows)
    output = ring_scatter(ring_parts([mm(hidden, w) for w in down_ffn_w]), "ring")
    output = middle + swap_features(output, row, rows)

    ffn_grad = [
        jnp.concatenate([mm_tn(grad_gate_up, h), mm_tn(hidden, d)])
        for h, d in zip(h2_blocks, dy_blocks)
    ]
    ffn_grad = ring_scatter(ffn_grad, "rows")
    ffn_grad = ffn_grad.reshape(3, PLANE, hidden_units // PLANE, feat)
    ffn_grad = plane_scatter([ffn_grad[:, k] for k in range(PLANE)], axis=1)
    gate_grad = jnp.transpose(ffn_grad[0])
    up_grad = jnp.transpose(ffn_grad[1])
    down_grad = ffn_grad[2]

    grad_middle_norm, grad_gain_ffn = pull_ffn_norm(grad_normed_ffn)
    grad_middle = upstream_f + grad_middle_norm

    branch_grad = plane_order(plane_gather(grad_middle.astype(BF)), plane)
    grad_out_w = plane_ring_gradient(mm_tn(branch_grad, attended), spot)
    grad_out_w = jnp.transpose(jnp.concatenate(grad_out_w, axis=1))
    grad_attended = mm(branch_grad, out_proj).astype(BF).reshape(group * heads, HD)
    scores = masked_scores()
    probs_f = jnp.exp(scores - log_total)
    probs_again = probs_f.astype(BF).reshape(group * heads, row_length)
    grad_probs = mm_nt(grad_attended, all_values).reshape(group, heads, row_length)
    grad_scores = probs_f * (grad_probs - jnp.sum(grad_probs * probs_f, axis=-1, keepdims=True))
    grad_scores = grad_scores.astype(BF).reshape(group * heads, row_length)
    grad_queries = mm(grad_scores, all_keys) * score_scale
    key_part = mm_tn(grad_scores, queries) * score_scale
    value_part = mm_tn(probs_again, grad_attended)
    key_part = rotate(key_part, key_cos, -key_sin)
    kv_parts = jnp.stack(
        [key_part[:, :kv_width], key_part[:, kv_width:]]
        + [value_part[:, :kv_width], value_part[:, kv_width:]]
    )
    kv_grad = plane_scatter([pick(kv_parts, plane ^ k) for k in range(PLANE)])
    kv_grad = ring_scatter(
        [block_of(kv_grad, (ring - k) % rings, group) for k in range(rings)], "ring"
    )

    grad_query_raw = rotate(grad_queries.reshape(group, heads, HD), cosine, -sine_table)
    grad_query_raw = grad_query_raw.reshape(group, heads * HD).astype(BF)
    grad_up_query = plane_ring_gradient(mm_tn(latent_normed, grad_query_raw), spot)
    grad_latent_normed = mm_nt(grad_query_raw, up_query)
    grad_latent_normed = plane_scatter(
        [block_of(grad_latent_normed, plane ^ k, count_local) for k in range(PLANE)]
    )
    own_latent = block_of(latent, plane, count_local)
    pull_latent = jax.vjp(rms_norm, own_latent, gain_query)[1]
    grad_latent, grad_gain_query = pull_latent(grad_latent_normed)
    grad_latent = grad_latent.astype(BF)
    grad_latent = plane_order(
        plane_swap([block_of(grad_latent, plane ^ k, latent_width, 1) for k in range(PLANE)]),
        plane,
    )
    grad_projected = jnp.concatenate([grad_latent, kv_grad.astype(BF)], axis=1)
    grad_down = plane_ring_gradient(mm_tn(normed, grad_projected), spot)
    grad_down_query = jnp.concatenate([p[:, :latent_width] for p in grad_down], axis=1)
    grad_kv_w = jnp.concatenate([p[:, latent_width:] for p in grad_down], axis=1)
    grad_normed = mm_nt(grad_projected, down_w)
    pull_attn_norm = jax.vjp(rms_norm, own_tokens.astype(F32), gain_attn)[1]
    scale = lax.rsqrt(jnp.mean(group_tokens * group_tokens, axis=-1, keepdims=True) + epsilon)
    grad_gain_attn = jnp.sum(grad_normed * group_tokens * scale, axis=0)
    grad_normed = plane_scatter(
        [block_of(grad_normed, plane ^ k, count_local) for k in range(PLANE)]
    )
    grad_input = grad_middle + pull_attn_norm(grad_normed)[0]

    gain_grads = jnp.concatenate(
        [g.reshape(devices, -1) for g in (grad_gain_attn, grad_gain_query, grad_gain_ffn)], axis=1
    ).reshape(rows, rings, PLANE, -1)
    got = ring_scatter_small([pick(gain_grads, (row - k) % rows) for k in range(rows)], "rows")
    got = ring_scatter_small([pick(got, (ring - k) % rings) for k in range(rings)], "ring")
    got = sum(plane_swap([pick(got, plane ^ k) for k in range(PLANE)]))

    return (
        output.astype(BF)[None],
        grad_input.astype(BF)[None],
        got[:part_a],
        grad_down_query,
        got[part_a : part_a + part_q],
        jnp.concatenate(grad_up_query, axis=1),
        grad_kv_w[:, :HD],
        grad_kv_w[:, HD:],
        grad_out_w,
        got[part_a + part_q :],
        gate_grad,
        up_grad,
        down_grad,
    )


def ring_scatter_small(parts, axis):
    return parts[0] + sum(shift(parts[k], axis, -k) for k in range(1, len(parts)))


def solution(mesh):
    rows = mesh.shape["rows"]
    chips = mesh.shape["seq"]
    inner = Mesh(
        np.asarray(mesh.devices).reshape(rows, chips // PLANE, 2, 2), ("rows", "ring", "py", "px")
    )
    seq = ("ring", "py", "px")
    every = ("rows",) + seq
    placed = (
        P("rows", seq, None),
        P("rows", seq, None),
        P("rows", None),
        P(every),
        P(every, None),
        P(every),
        P(every, None),
        P(every, None),
        P(every, None),
        P(None, every),
        P(every),
        P("rows", seq),
        P("rows", seq),
        P(seq, "rows"),
    )
    return jax.shard_map(
        shards,
        mesh=inner,
        in_specs=placed,
        out_specs=(
            P("rows", seq, None),
            P("rows", seq, None),
            P(every),
            P(every, None),
            P(every),
            P(every, None),
            P(every, None),
            P(every, None),
            P(None, every),
            P(every),
            P("rows", seq),
            P("rows", seq),
            P(seq, "rows"),
        ),
        check_vma=False,
    )
```

time: 4270 us -> 913 us (0.21)
  waiting for transfers between devices: 3850 us -> 348 us
  starting transfers between devices: 1.41 us -> 138 us
  local copies, waits for them, and re-layouts: 28.5 us -> 163 us
  matrix products: 239 us -> 126 us
  blocking collectives: 79.5 us -> 0 us
  other arithmetic: 50.6 us -> 125 us
    reduce_scatter x13 -> x0, waiting for transfers between devices: 2930 us -> none  [the longest x3 1320 us: reduce_ffn(): lax.psum_scatter(gradient.astype(jnp.bfloat16), 'seq', scatter_dimension=...]
    all_gather x13 -> x0, waiting for transfers between devices: 905 us -> none  [the longest x1 143 us: shards(): lax.all_gather(w_gate, 'seq', axis=1, tiled=True)]
    ppermute x0 -> x129, waiting for transfers between devices: none -> 348 us  [the longest x52 214 us: shift(): lax.ppermute(value, axis, [(i, (i + by) % count) for i in range(count)])]
    ppermute x0 -> x129, starting transfers between devices: none -> 138 us  [the longest x68 85.9 us: flip(): return lax.ppermute(value, 'px' if by == 1 else 'py', [(0, 1), (1, 0)])]
    dot_general x30 -> x27, matrix products: 239 us -> 126 us  [the longest x9 64.2 us: mm_nt(): return jnp.einsum('ik,jk->ij', left, right, preferred_element_type=F32)]
    unnamed x2 -> x0, blocking collectives: 79.5 us -> none
  transfers between devices with their start and end apart: 26 -> 129, of which waited for: 23 -> 62; matrix products, arithmetic and copies ran while one was open for 7% -> 25% of each run, Pallas kernels for 0% -> 0%
where the time goes in v1:
time: 913 us; the launch traced here: 904 us
  waiting for transfers between devices  348 us (38%)
  local copies, waits for them, and re-layouts  163 us (18%)
  starting transfers between devices  138 us (15%)
  matrix products  126 us (14%)
  other arithmetic  125 us (14%)
    ppermute x52, waiting for transfers between devices, shift(): lax.ppermute(value, axis, [(i, (i + by) % count) for i in range(count)])  214 us
    ppermute x68, waiting for transfers between devices, flip(): return lax.ppermute(value, 'px' if by == 1 else 'py', [(0, 1), (1, 0)])  129 us
    ppermute x68, starting transfers between devices, flip(): return lax.ppermute(value, 'px' if by == 1 else 'py', [(0, 1), (1, 0)])  85.9 us
    dot_general x9, matrix products, mm_nt(): return jnp.einsum('ik,jk->ij', left, right, preferred_element_type=F32)  64.2 us
    ppermute x52, starting transfers between devices, shift(): lax.ppermute(value, axis, [(i, (i + by) % count) for i in range(count)])  41.8 us
    dot_general x9, matrix products, mm(): return jnp.dot(left, right, preferred_element_type=F32)  33.8 us
    dot_general x9, matrix products, mm_tn(): return jnp.einsum('ki,kj->ij', left, right, preferred_element_type=F32)  28.2 us
    unnamed x255, local copies, waits for them, and re-layouts  28.2 us
  transfers between devices with their start and end apart: 129, of which 62 were waited for; matrix products, arithmetic and copies ran while one was open for 25% of the time, Pallas kernels for 0%

profile of v1, /device:TPU:0, one launch (start us, length us, event | category | flops | bytes accessed | tf_op | source)
XLA Modules:
  0.0 904.3 jit_solution(5310917683889245437)
XLA Ops:
  39.0 12.2 %broadcast_in_dim.72 = pred[2048,2048]{1,0:T(32,128)(4,1)} reshape(pred[512,4,2048]{2,1,0:T(4,128)(4,1)} %broadcast_in_dim.71.clone) | data formatting | bytes 8388608 | tf_op jit(solution)/shard_map/jit(_where)/broadcast_in_dim | solution.py:284
  81.0 12.9 %collective-permute-done.15 = bf16[256,384]{1,0:T(8,128)(2,1)S(1)} collective-permute-done((bf16[256,384]{1,0:T(8,128)(2,1)S(1)}, bf16[256,384]{1,0:T(8,128)(2,1)S(1)}, u32[]{:S(2)}, u32[]{:S(2)}) %collective-permute-start.15) | collective-permute-done | bytes 196640 | tf_op jit(solution)/shard_map/ppermute | solution.py:60
  98.0 15.9 %collective-permute-done.26 = bf16[128,1024]{1,0:T(8,128)(2,1)S(1)} collective-permute-done((bf16[128,1024]{1,0:T(8,128)(2,1)S(1)}, bf16[128,1024]{1,0:T(8,128)(2,1)S(1)}, u32[]{:S(2)}, u32[]{:S(2)}) %collective-permute-start.26) | collective-permute-done | bytes 262176 | tf_op jit(solution)/shard_map/ppermute | solution.py:60
  113.9 18.4 %collective-permute-start.39 = (bf16[256,1024]{1,0:T(8,128)(2,1)S(1)}, bf16[256,1024]{1,0:T(8,128)(2,1)S(1)}, u32[]{:S(2)}, u32[]{:S(2)}) collective-permute-start(bf16[256,1024]{1,0:T(8,128)(2,1)S(1)} %get-tuple-element.133), channel_id=1, source_target_pairs={{0,4},{4,8},{8,12},{12,0},{1,5},{5,9},{9,13},{13,1},{2,6},{6,10},{... | collective-permute-start | bytes 1572872 | tf_op jit(solution)/shard_map/ppermute | solution.py:60
  136.0 16.3 %collective-permute-done.40 = bf16[256,1024]{1,0:T(8,128)(2,1)S(1)} collective-permute-done((bf16[256,1024]{1,0:T(8,128)(2,1)S(1)}, bf16[256,1024]{1,0:T(8,128)(2,1)S(1)}, u32[]{:S(2)}, u32[]{:S(2)}) %collective-permute-start.40) | collective-permute-done | bytes 524320 | tf_op jit(solution)/shard_map/ppermute | solution.py:60
  159.7 6.7 collective-permute-done.29
  175.0 15.6 %collective-permute-done.18 = bf16[512,256]{1,0:T(8,128)(2,1)S(1)} collective-permute-done((bf16[512,256]{1,0:T(8,128)(2,1)S(1)}, bf16[512,256]{1,0:T(8,128)(2,1)S(1)}, u32[]{:S(2)}, u32[]{:S(2)}) %collective-permute-start.18) | collective-permute-done | bytes 262176 | tf_op jit(solution)/shard_map/ppermute | solution.py:84
  200.6 18.8 %collective-permute-done.20 = bf16[256,256]{1,0:T(8,128)(2,1)S(1)} collective-permute-done((bf16[256,256]{1,0:T(8,128)(2,1)S(1)}, bf16[256,256]{1,0:T(8,128)(2,1)S(1)}, u32[]{:S(2)}, u32[]{:S(2)}) %collective-permute-start.20) | collective-permute-done | bytes 131104 | tf_op jit(solution)/shard_map/ppermute | solution.py:84
  268.5 6.8 exponential_convert_fusion
  275.4 6.7 convolution_convert_fusion.2
  323.9 10.3 %collective-permute-done.60 = bf16[128,2048]{1,0:T(8,128)(2,1)} collective-permute-done((bf16[128,2048]{1,0:T(8,128)(2,1)}, bf16[128,2048]{1,0:T(8,128)(2,1)}, u32[]{:S(2)}, u32[]{:S(2)}) %collective-permute-start.60) | collective-permute-done | bytes 524320 | tf_op jit(solution)/shard_map/ppermute | solution.py:60
  334.2 11.2 %collective-permute-done.49 = bf16[128,2048]{1,0:T(8,128)(2,1)} collective-permute-done((bf16[128,2048]{1,0:T(8,128)(2,1)S(1)}, bf16[128,2048]{1,0:T(8,128)(2,1)}, u32[]{:S(2)}, u32[]{:S(2)}) %collective-permute-start.49) | collective-permute-done | bytes 524320 | tf_op jit(solution)/shard_map/ppermute | solution.py:60
  345.4 11.2 %collective-permute-done.61 = bf16[128,2048]{1,0:T(8,128)(2,1)} collective-permute-done((bf16[128,2048]{1,0:T(8,128)(2,1)}, bf16[128,2048]{1,0:T(8,128)(2,1)}, u32[]{:S(2)}, u32[]{:S(2)}) %collective-permute-start.61) | collective-permute-done | bytes 524320 | tf_op jit(solution)/shard_map/ppermute | solution.py:60
  356.7 11.2 %collective-permute-done.50 = bf16[128,2048]{1,0:T(8,128)(2,1)} collective-permute-done((bf16[128,2048]{1,0:T(8,128)(2,1)}, bf16[128,2048]{1,0:T(8,128)(2,1)}, u32[]{:S(2)}, u32[]{:S(2)}) %collective-permute-start.50) | collective-permute-done | bytes 524320 | tf_op jit(solution)/shard_map/ppermute | solution.py:60
  370.2 9.0 collective-permute-done.62
  383.3 19.0 %reshape.522 = f32[512,4,2048]{2,1,0:T(4,128)} reshape(f32[2048,2048]{1,0:T(8,128)} %copy-done) | data formatting | bytes 33554432 | tf_op jit(solution)/shard_map/reshape | solution.py:285
  413.4 7.1 fusion.101
  420.5 7.5 convolution_add_fusion
  433.6 7.5 fusion.131
  469.7 8.8 collective-permute-done.63
  489.9 11.0 %collective-permute-done.64 = bf16[128,2048]{1,0:T(8,128)(2,1)S(1)} collective-permute-done((bf16[128,2048]{1,0:T(8,128)(2,1)S(1)}, bf16[128,2048]{1,0:T(8,128)(2,1)S(1)}, u32[]{:S(2)}, u32[]{:S(2)}) %collective-permute-start.64) | collective-permute-done | bytes 524320 | tf_op jit(solution)/shard_map/ppermute | solution.py:60
  505.5 6.7 collective-permute-done.58
  548.1 23.0 %multiply_reduce_fusion = (f32[512,4]{0,1:T(4,128)S(1)}, f32[512,4,2048]{2,0,1:T(8,128)}) fusion(f32[512,4,2048]{2,1,0:T(4,128)} %reshape.522, f32[512,4]{0,1:T(4,128)S(1)} %copy.81, pred[512,2048]{1,0:T(8,128)(4,1)S(1)} %copy-done.7, bf16[2048,128]{1,0:T(8,128)(2,1)} %get-tuple-element.80, bf16[2048,128]{1,0:T(8,128)(2,1)S(1)} %copy-done.78, ...), kind=kOutput, calls=%fused_computation.5 | convolution fusion | flops 2166355968 | bytes 36716544 | tf_op jit(solution)/shard_map/ik,jk->ij/dot_general | solution.py:51
  571.1 20.6 %multiply_convert_fusion = bf16[512,4,2048]{2,0,1:T(8,128)(2,1)S(1)} fusion(f32[512,4,2048]{2,0,1:T(8,128)} %get-tuple-element.236, f32[512,4,2048]{2,1,0:T(4,128)} %reshape.522, f32[512,4]{0,1:T(4,128)S(1)} %get-tuple-element.235, f32[512,4]{0,1:T(4,128)S(1)} %copy.81, pred[512,2048]{1,0:T(8,128)(4,1)S(1)} %copy-done.7), kind=kLoop, calls=%fused_computation.4 | loop fusion | flops 20971520 | bytes 43008000 | tf_op jit(solution)/shard_map/convert_element_type | solution.py:348
  595.7 20.4 %copy.83 = bf16[512,4,2048]{2,1,0:T(4,128)(2,1)} copy(bf16[512,4,2048]{2,0,1:T(8,128)(2,1)S(1)} %multiply_convert_fusion) | data formatting | bytes 16777216 | tf_op jit(solution)/shard_map/convert_element_type | solution.py:348
  616.1 12.6 %reshape.523 = bf16[2048,2048]{1,0:T(8,128)(2,1)} reshape(bf16[512,4,2048]{2,1,0:T(4,128)(2,1)} %copy.83) | data formatting | bytes 16777216 | tf_op jit(solution)/shard_map/reshape | solution.py:348
  628.7 7.2 convolution_multiply_fusion.1
  774.5 15.1 %collective-permute-done.103 = bf16[256,384]{1,0:T(8,128)(2,1)S(1)} collective-permute-done((bf16[256,384]{1,0:T(8,128)(2,1)S(1)}, bf16[256,384]{1,0:T(8,128)(2,1)S(1)}, u32[]{:S(2)}, u32[]{:S(2)}) %collective-permute-start.103) | collective-permute-done | bytes 196640 | tf_op jit(solution)/shard_map/ppermute | solution.py:60
  791.4 8.0 collective-permute-done.104
  806.5 9.5 %maximum_add_fusion = f32[4224,1024]{1,0:T(8,128)S(1)} fusion(f32[1408,1024]{1,0:T(8,128)} %fusion.97, f32[2816,1024]{1,0:T(8,128)} %fusion.103, bf16[4224,1024]{1,0:T(8,128)(2,1)} %collective-permute-done.122), kind=kLoop, calls=%fused_computation | loop fusion | flops 12976128 | bytes 43253760 | tf_op jit(solution)/shard_map/add | solution.py:77
  829.9 10.6 %slice_bitcast_fusion.2 = (f32[3,352,1024]{2,1,0:T(8,128)}, f32[3,352,1024]{2,1,0:T(8,128)}, f32[3,352,1024]{2,1,0:T(8,128)S(1)}) fusion(f32[3,4,352,1024]{3,2,1,0:T(8,128)} %bitcast.474), kind=kLoop, calls=%fused_computation.41 | loop fusion | bytes 25952256 | tf_op jit(solution)/shard_map/squeeze | solution.py:331
  863.5 34.1 %collective-permute-done.119 = bf16[64,1024]{1,0:T(8,128)(2,1)S(1)} collective-permute-done((bf16[64,1024]{1,0:T(8,128)(2,1)S(1)}, bf16[64,1024]{1,0:T(8,128)(2,1)S(1)}, u32[]{:S(2)}, u32[]{:S(2)}) %collective-permute-start.119) | collective-permute-done | bytes 131104 | tf_op jit(solution)/shard_map/ppermute | solution.py:84
  (763 shorter events, 488.4 us)
Async XLA Ops:
  0.7 132.0 %collective-permute-start.1 = (bf16[128,2048]{1,0:T(8,128)(2,1)}, bf16[128,2048]{1,0:T(8,128)(2,1)S(1)}, u32[]{:S(2)}, u32[]{:S(2)}) collective-permute-start(bf16[128,2048]{1,0:T(8,128)(2,1)} %bitcast.475), channel_id=1, source_target_pairs={{0,2},{2,0},{1,3},{3,1},{4,6},{6,4},{5,7},{7,5},{8,10},{10,8},{9,1... | collective-permute-start | bytes 1572872 | tf_op jit(solution)/shard_map/ppermute | solution.py:84
  3.7 130.6 %collective-permute-start = (bf16[128,2048]{1,0:T(8,128)(2,1)}, bf16[128,2048]{1,0:T(8,128)(2,1)S(1)}, u32[]{:S(2)}, u32[]{:S(2)}) collective-permute-start(bf16[128,2048]{1,0:T(8,128)(2,1)} %bitcast.476), channel_id=1, source_target_pairs={{0,1},{1,0},{2,3},{3,2},{4,5},{5,4},{6,7},{7,6},{8,9},{9,8},{10,11... | collective-permute-start | bytes 1572872 | tf_op jit(solution)/shard_map/ppermute | solution.py:84
  95.5 39.6 %collective-permute-start.41 = (bf16[256,1024]{1,0:T(8,128)(2,1)S(1)}, bf16[256,1024]{1,0:T(8,128)(2,1)S(1)}, u32[]{:S(2)}, u32[]{:S(2)}) collective-permute-start(bf16[256,1024]{1,0:T(8,128)(2,1)S(1)} %get-tuple-element.133), channel_id=1, source_target_pairs={{0,12},{4,0},{8,4},{12,8},{1,13},{5,1},{9,5},{13,9},{2,14},{6,2},{... | collective-permute-start | bytes 1572872 | tf_op jit(solution)/shard_map/ppermute | solution.py:60
  113.9 38.4 %collective-permute-start.40 = (bf16[256,1024]{1,0:T(8,128)(2,1)S(1)}, bf16[256,1024]{1,0:T(8,128)(2,1)S(1)}, u32[]{:S(2)}, u32[]{:S(2)}) collective-permute-start(bf16[256,1024]{1,0:T(8,128)(2,1)S(1)} %get-tuple-element.133), channel_id=1, source_target_pairs={{0,8},{4,12},{8,0},{12,4},{1,9},{5,13},{9,1},{13,5},{2,10},{6,14},... | collective-permute-start | bytes 1572872 | tf_op jit(solution)/shard_map/ppermute | solution.py:60
  113.9 38.4 %collective-permute-start.39 = (bf16[256,1024]{1,0:T(8,128)(2,1)S(1)}, bf16[256,1024]{1,0:T(8,128)(2,1)S(1)}, u32[]{:S(2)}, u32[]{:S(2)}) collective-permute-start(bf16[256,1024]{1,0:T(8,128)(2,1)S(1)} %get-tuple-element.133), channel_id=1, source_target_pairs={{0,4},{4,8},{8,12},{12,0},{1,5},{5,9},{9,13},{13,1},{2,6},{6,10},{... | collective-permute-start | bytes 1572872 | tf_op jit(solution)/shard_map/ppermute | solution.py:60
  135.1 99.0 %collective-permute-start.52 = (bf16[3,352,1024]{2,1,0:T(8,128)(2,1)}, bf16[3,352,1024]{2,1,0:T(8,128)(2,1)}, u32[]{:S(2)}, u32[]{:S(2)}) collective-permute-start(bf16[3,352,1024]{2,1,0:T(8,128)(2,1)} %get-tuple-element.55), channel_id=1, source_target_pairs={{0,1},{1,0},{2,3},{3,2},{4,5},{5,4},{6,7},{7,6},{8,9},{9,8},{10,11... | collective-permute-start | bytes 6488072 | tf_op jit(solution)/shard_map/ppermute | solution.py:84
  152.3 40.8 %collective-permute-start.28 = (bf16[512,1024]{1,0:T(8,128)(2,1)S(1)}, bf16[512,1024]{1,0:T(8,128)(2,1)S(1)}, u32[]{:S(2)}, u32[]{:S(2)}) collective-permute-start(bf16[512,1024]{1,0:T(8,128)(2,1)S(1)} %get-tuple-element.102), channel_id=1, source_target_pairs={{0,16},{16,0},{1,17},{17,1},{2,18},{18,2},{3,19},{19,3},{4,20},{20... | collective-permute-start | bytes 3145736 | tf_op jit(solution)/shard_map/ppermute | solution.py:60
  157.8 32.9 %collective-permute-start.18 = (bf16[512,256]{1,0:T(8,128)(2,1)S(1)}, bf16[512,256]{1,0:T(8,128)(2,1)S(1)}, u32[]{:S(2)}, u32[]{:S(2)}) collective-permute-start(bf16[512,256]{1,0:T(8,128)(2,1)S(1)} %get-tuple-element.151), channel_id=1, source_target_pairs={{0,1},{1,0},{2,3},{3,2},{4,5},{5,4},{6,7},{7,6},{8,9},{9,8},{10,11... | collective-permute-start | bytes 786440 | tf_op jit(solution)/shard_map/ppermute | solution.py:84
  166.4 69.2 %collective-permute-start.53 = (bf16[3,352,1024]{2,1,0:T(8,128)(2,1)}, bf16[3,352,1024]{2,1,0:T(8,128)(2,1)}, u32[]{:S(2)}, u32[]{:S(2)}) collective-permute-start(bf16[3,352,1024]{2,1,0:T(8,128)(2,1)} %get-tuple-element.55), channel_id=1, source_target_pairs={{0,2},{2,0},{1,3},{3,1},{4,6},{6,4},{5,7},{7,5},{8,10},{10,8},{9,1... | collective-permute-start | bytes 6488072 | tf_op jit(solution)/shard_map/ppermute | solution.py:84
  175.0 109.6 %collective-permute-start.42 = (bf16[1024,1024]{1,0:T(8,128)(2,1)}, bf16[1024,1024]{1,0:T(8,128)(2,1)}, u32[]{:S(2)}, u32[]{:S(2)}) collective-permute-start(bf16[1024,1024]{1,0:T(8,128)(2,1)} %get-tuple-element.73), channel_id=1, source_target_pairs={{0,16},{16,0},{1,17},{17,1},{2,18},{18,2},{3,19},{19,3},{4,20},{20... | collective-permute-start | bytes 6291464 | tf_op jit(solution)/shard_map/ppermute | solution.py:60
  199.6 28.8 %collective-permute-start.33 = (bf16[2048,128]{1,0:T(8,128)(2,1)}, bf16[2048,128]{1,0:T(8,128)(2,1)}, u32[]{:S(2)}, u32[]{:S(2)}) collective-permute-start(bf16[2048,128]{1,0:T(8,128)(2,1)} %get-tuple-element.143), channel_id=1, source_target_pairs={{0,2},{2,0},{1,3},{3,1},{4,6},{6,4},{5,7},{7,5},{8,10},{10,8},{9,1... | collective-permute-start | bytes 1572872 | tf_op jit(solution)/shard_map/ppermute | solution.py:84
  235.3 30.9 %collective-permute-start.54 = (bf16[3,176,1024]{2,1,0:T(8,128)(2,1)S(1)}, bf16[3,176,1024]{2,1,0:T(8,128)(2,1)S(1)}, u32[]{:S(2)}, u32[]{:S(2)}) collective-permute-start(bf16[3,176,1024]{2,1,0:T(8,128)(2,1)S(1)} %slice.500), channel_id=1, source_target_pairs={{0,2},{2,0},{1,3},{3,1},{4,6},{6,4},{5,7},{7,5},{8,10},{10,8},{9,1... | collective-permute-start | bytes 3244040 | tf_op jit(solution)/shard_map/ppermute | solution.py:84
  236.9 30.5 %collective-permute-start.55 = (bf16[3,176,1024]{2,1,0:T(8,128)(2,1)S(1)}, bf16[3,176,1024]{2,1,0:T(8,128)(2,1)S(1)}, u32[]{:S(2)}, u32[]{:S(2)}) collective-permute-start(bf16[3,176,1024]{2,1,0:T(8,128)(2,1)S(1)} %slice.501), channel_id=1, source_target_pairs={{0,1},{1,0},{2,3},{3,2},{4,5},{5,4},{6,7},{7,6},{8,9},{9,8},{10,11... | collective-permute-start | bytes 3244040 | tf_op jit(solution)/shard_map/ppermute | solution.py:84
  268.5 141.6 %collective-permute-start.56 = (bf16[3,1408,1024]{2,1,0:T(8,128)(2,1)}, bf16[3,1408,1024]{2,1,0:T(8,128)(2,1)}, u32[]{:S(2)}, u32[]{:S(2)}) collective-permute-start(bf16[3,1408,1024]{2,1,0:T(8,128)(2,1)} %constant_dynamic-update-slice_fusion), channel_id=1, source_target_pairs={{0,16},{16,0},{1,17},{17,1},{2,18},{18,2},{3,19},{19,3},{4,20},{20... | collective-permute-start | bytes 25952264 | tf_op jit(solution)/shard_map/ppermute | solution.py:60
  367.9 38.1 %collective-permute-start.51 = (bf16[128,2048]{1,0:T(8,128)(2,1)}, bf16[128,2048]{1,0:T(8,128)(2,1)}, u32[]{:S(2)}, u32[]{:S(2)}) collective-permute-start(bf16[128,2048]{1,0:T(8,128)(2,1)} %collective-permute-done.50), channel_id=1, source_target_pairs={{0,4},{4,8},{8,12},{12,0},{1,5},{5,9},{9,13},{13,1},{2,6},{6,10},{... | collective-permute-start | bytes 1572872 | tf_op jit(solution)/shard_map/ppermute | solution.py:60
  465.6 24.2 %collective-permute-start.57 = (bf16[128,2048]{1,0:T(8,128)(2,1)S(1)}, bf16[128,2048]{1,0:T(8,128)(2,1)S(1)}, u32[]{:S(2)}, u32[]{:S(2)}) collective-permute-start(bf16[128,2048]{1,0:T(8,128)(2,1)S(1)} %fusion.75), channel_id=1, source_target_pairs={{0,4},{4,8},{8,12},{12,0},{1,5},{5,9},{9,13},{13,1},{2,6},{6,10},{... | collective-permute-start | bytes 1572872 | tf_op jit(solution)/shard_map/ppermute | solution.py:60
  660.9 24.0 %collective-permute-start.82 = (bf16[1024,128]{1,0:T(8,128)(2,1)S(1)}, bf16[1024,128]{1,0:T(8,128)(2,1)S(1)}, u32[]{:S(2)}, u32[]{:S(2)}) collective-permute-start(bf16[1024,128]{1,0:T(8,128)(2,1)S(1)} %get-tuple-element.41), channel_id=1, source_target_pairs={{0,1},{1,0},{2,3},{3,2},{4,5},{5,4},{6,7},{7,6},{8,9},{9,8},{10,11... | collective-permute-start | bytes 786440 | tf_op jit(solution)/shard_map/ppermute | solution.py:84
  661.7 23.2 %collective-permute-start.80 = (bf16[1024,128]{1,0:T(8,128)(2,1)S(1)}, bf16[1024,128]{1,0:T(8,128)(2,1)S(1)}, u32[]{:S(2)}, u32[]{:S(2)}) collective-permute-start(bf16[1024,128]{1,0:T(8,128)(2,1)S(1)} %get-tuple-element.125), channel_id=1, source_target_pairs={{0,2},{2,0},{1,3},{3,1},{4,6},{6,4},{5,7},{7,5},{8,10},{10,8},{9,1... | collective-permute-start | bytes 786440 | tf_op jit(solution)/shard_map/ppermute | solution.py:84
  678.5 128.1 %collective-permute-start.122 = (bf16[4224,1024]{1,0:T(8,128)(2,1)}, bf16[4224,1024]{1,0:T(8,128)(2,1)}, u32[]{:S(2)}, u32[]{:S(2)}) collective-permute-start(bf16[4224,1024]{1,0:T(8,128)(2,1)} %pad_maximum_fusion), channel_id=1, source_target_pairs={{0,16},{16,0},{1,17},{17,1},{2,18},{18,2},{3,19},{19,3},{4,20},{20... | collective-permute-start | bytes 25952264 | tf_op jit(solution)/shard_map/ppermute | solution.py:60
  684.9 24.0 %collective-permute-start.108 = (bf16[512,1024]{1,0:T(8,128)(2,1)}, bf16[512,1024]{1,0:T(8,128)(2,1)}, u32[]{:S(2)}, u32[]{:S(2)}) collective-permute-start(bf16[512,1024]{1,0:T(8,128)(2,1)} %dynamic-slice_convert_fusion.1), channel_id=1, source_target_pairs={{0,16},{16,0},{1,17},{17,1},{2,18},{18,2},{3,19},{19,3},{4,20},{20... | collective-permute-start | bytes 3145736 | tf_op jit(solution)/shard_map/ppermute | solution.py:60
  711.2 25.5 %collective-permute-start.109 = (bf16[128,1024]{1,0:T(8,128)(2,1)S(1)}, bf16[128,1024]{1,0:T(8,128)(2,1)}, u32[]{:S(2)}, u32[]{:S(2)}) collective-permute-start(bf16[128,1024]{1,0:T(8,128)(2,1)S(1)} %dynamic-slice_convert_fusion.13), channel_id=1, source_target_pairs={{0,4},{4,8},{8,12},{12,0},{1,5},{5,9},{9,13},{13,1},{2,6},{6,10},{... | collective-permute-start | bytes 786440 | tf_op jit(solution)/shard_map/ppermute | solution.py:60
  799.4 25.2 %collective-permute-start.107 = (bf16[64,384]{1,0:T(8,128)(2,1)S(1)}, bf16[64,384]{1,0:T(8,128)(2,1)S(1)}, u32[]{:S(2)}, u32[]{:S(2)}) collective-permute-start(bf16[64,384]{1,0:T(8,128)(2,1)S(1)} %get-tuple-element.185), channel_id=1, source_target_pairs={{0,3},{1,2},{2,1},{3,0},{4,7},{5,6},{6,5},{7,4},{8,11},{9,10},{10,... | collective-permute-start | bytes 147464 | tf_op jit(solution)/shard_map/ppermute | solution.py:83
  801.5 23.1 %collective-permute-start.106 = (bf16[64,384]{1,0:T(8,128)(2,1)S(1)}, bf16[64,384]{1,0:T(8,128)(2,1)S(1)}, u32[]{:S(2)}, u32[]{:S(2)}) collective-permute-start(bf16[64,384]{1,0:T(8,128)(2,1)S(1)} %get-tuple-element.186), channel_id=1, source_target_pairs={{0,2},{2,0},{1,3},{3,1},{4,6},{6,4},{5,7},{7,5},{8,10},{10,8},{9,1... | collective-permute-start | bytes 147464 | tf_op jit(solution)/shard_map/ppermute | solution.py:84
  823.8 27.1 %collective-permute-start.127 = (bf16[3,176,1024]{2,1,0:T(8,128)(2,1)}, bf16[3,176,1024]{2,1,0:T(8,128)(2,1)}, u32[]{:S(2)}, u32[]{:S(2)}) collective-permute-start(bf16[3,176,1024]{2,1,0:T(8,128)(2,1)} %get-tuple-element.53), channel_id=1, source_target_pairs={{0,1},{1,0},{2,3},{3,2},{4,5},{5,4},{6,7},{7,6},{8,9},{9,8},{10,11... | collective-permute-start | bytes 3244040 | tf_op jit(solution)/shard_map/ppermute | solution.py:84
  824.8 30.7 %collective-permute-start.124 = (bf16[3,176,1024]{2,1,0:T(8,128)(2,1)}, bf16[3,176,1024]{2,1,0:T(8,128)(2,1)}, u32[]{:S(2)}, u32[]{:S(2)}) collective-permute-start(bf16[3,176,1024]{2,1,0:T(8,128)(2,1)} %get-tuple-element.54), channel_id=1, source_target_pairs={{0,2},{2,0},{1,3},{3,1},{4,6},{6,4},{5,7},{7,5},{8,10},{10,8},{9,1... | collective-permute-start | bytes 3244040 | tf_op jit(solution)/shard_map/ppermute | solution.py:84
  828.4 30.8 %collective-permute-start.121 = (bf16[64,1024]{1,0:T(8,128)(2,1)}, bf16[64,1024]{1,0:T(8,128)(2,1)S(1)}, u32[]{:S(2)}, u32[]{:S(2)}) collective-permute-start(bf16[64,1024]{1,0:T(8,128)(2,1)} %get-tuple-element.119), channel_id=1, source_target_pairs={{0,3},{1,2},{2,1},{3,0},{4,7},{5,6},{6,5},{7,4},{8,11},{9,10},{10,... | collective-permute-start | bytes 393224 | tf_op jit(solution)/shard_map/ppermute | solution.py:83
  828.4 31.7 %collective-permute-start.120 = (bf16[64,1024]{1,0:T(8,128)(2,1)}, bf16[64,1024]{1,0:T(8,128)(2,1)S(1)}, u32[]{:S(2)}, u32[]{:S(2)}) collective-permute-start(bf16[64,1024]{1,0:T(8,128)(2,1)} %get-tuple-element.120), channel_id=1, source_target_pairs={{0,2},{2,0},{1,3},{3,1},{4,6},{6,4},{5,7},{7,5},{8,10},{10,8},{9,1... | collective-permute-start | bytes 393224 | tf_op jit(solution)/shard_map/ppermute | solution.py:84
  842.4 56.3 %collective-permute-start.126 = (bf16[3,176,1024]{2,1,0:T(8,128)(2,1)S(1)}, bf16[3,176,1024]{2,1,0:T(8,128)(2,1)S(1)}, u32[]{:S(2)}, u32[]{:S(2)}) collective-permute-start(bf16[3,176,1024]{2,1,0:T(8,128)(2,1)S(1)} %slice.699), channel_id=1, source_target_pairs={{0,1},{1,0},{2,3},{3,2},{4,5},{5,4},{6,7},{7,6},{8,9},{9,8},{10,11... | collective-permute-start | bytes 3244040 | tf_op jit(solution)/shard_map/ppermute | solution.py:84
  850.9 47.8 %collective-permute-start.123 = (bf16[3,176,1024]{2,1,0:T(8,128)(2,1)S(1)}, bf16[3,176,1024]{2,1,0:T(8,128)(2,1)S(1)}, u32[]{:S(2)}, u32[]{:S(2)}) collective-permute-start(bf16[3,176,1024]{2,1,0:T(8,128)(2,1)S(1)} %slice.700), channel_id=1, source_target_pairs={{0,2},{2,0},{1,3},{3,1},{4,6},{6,4},{5,7},{7,5},{8,10},{10,8},{9,1... | collective-permute-start | bytes 3244040 | tf_op jit(solution)/shard_map/ppermute | solution.py:84
  855.6 44.8 %collective-permute-start.128 = (bf16[3,176,1024]{2,1,0:T(8,128)(2,1)S(1)}, bf16[3,176,1024]{2,1,0:T(8,128)(2,1)S(1)}, u32[]{:S(2)}, u32[]{:S(2)}) collective-permute-start(bf16[3,176,1024]{2,1,0:T(8,128)(2,1)S(1)} %fusion.20), channel_id=1, source_target_pairs={{0,2},{2,0},{1,3},{3,1},{4,6},{6,4},{5,7},{7,5},{8,10},{10,8},{9,1... | collective-permute-start | bytes 3244040 | tf_op jit(solution)/shard_map/ppermute | solution.py:84
  859.3 41.1 %collective-permute-start.125 = (bf16[3,176,1024]{2,1,0:T(8,128)(2,1)S(1)}, bf16[3,176,1024]{2,1,0:T(8,128)(2,1)S(1)}, u32[]{:S(2)}, u32[]{:S(2)}) collective-permute-start(bf16[3,176,1024]{2,1,0:T(8,128)(2,1)S(1)} %fusion.22), channel_id=1, source_target_pairs={{0,1},{1,0},{2,3},{3,2},{4,5},{5,4},{6,7},{7,6},{8,9},{9,8},{10,11... | collective-permute-start | bytes 3244040 | tf_op jit(solution)/shard_map/ppermute | solution.py:84
  860.1 37.5 %collective-permute-start.119 = (bf16[64,1024]{1,0:T(8,128)(2,1)S(1)}, bf16[64,1024]{1,0:T(8,128)(2,1)S(1)}, u32[]{:S(2)}, u32[]{:S(2)}) collective-permute-start(bf16[64,1024]{1,0:T(8,128)(2,1)S(1)} %get-tuple-element.121), channel_id=1, source_target_pairs={{0,1},{1,0},{2,3},{3,2},{4,5},{5,4},{6,7},{7,6},{8,9},{9,8},{10,11... | collective-permute-start | bytes 393224 | tf_op jit(solution)/shard_map/ppermute | solution.py:84
  (219 other events, 2833.7 us)

commit v2 on v1

--- a/solution.py
+++ b/solution.py
@@ -2,6 +2,8 @@
 import jax.numpy as jnp
 import numpy as np
 from jax import lax
+from jax.experimental import pallas as pl
+from jax.experimental.pallas import tpu as pltpu
 from jax.sharding import Mesh, PartitionSpec as P
 
 HEADS = 16
@@ -24,15 +26,6 @@
     frequency = 1.0 / 10000.0 ** (jnp.arange(half_dim, dtype=F32) / half_dim)
     angles = relative.astype(F32)[..., None] * frequency
     return (jnp.cos(angles), jnp.sin(angles))
-
-
-def rotate(values, cosine, sine_table):
-    half_dim = values.shape[-1] // 2
-    front = values[..., :half_dim]
-    back = values[..., half_dim:]
-    return jnp.concatenate(
-        [front * cosine - back * sine_table, back * cosine + front * sine_table], axis=-1
-    )
 
 
 def doc_layout(lengths, positions):
@@ -171,6 +164,258 @@
     got = plane_swap([block_of(total, plane ^ k, size) for k in range(PLANE)])
     stacked = jnp.stack(got)
     return [pick(stacked, plane ^ i).astype(F32) for i in range(PLANE)]
+
+
+def after(value, *deps):
+    return lax.optimization_barrier((value,) + deps)[0]
+
+
+def params():
+    return pltpu.CompilerParams(vmem_limit_bytes=56 * 1024 * 1024)
+
+
+def dot_nn(left, right):
+    return lax.dot_general(left, right, (((1,), (0,)), ((), ())), preferred_element_type=F32)
+
+
+def dot_nt(left, right):
+    return lax.dot_general(left, right, (((1,), (1,)), ((), ())), preferred_element_type=F32)
+
+
+def dot_tn(left, right):
+    return lax.dot_general(left, right, (((0,), (0,)), ((), ())), preferred_element_type=F32)
+
+
+QB = 256
+KB = 512
+HALF = HD // 2
+
+
+def query_bounds(scal, ndoc, block):
+    first = scal[1] + block * QB
+    positions = first + lax.broadcasted_iota(jnp.int32, (QB, 1), 0)
+    starts = jnp.zeros((QB, 1), jnp.int32)
+    low_start, end = 0, 0
+    for n in range(ndoc):
+        end = end + scal[2 + n]
+        starts = jnp.where(positions >= end, end, starts)
+        low_start = jnp.where(first >= end, end, low_start)
+    return positions, starts, lax.div(low_start, KB), lax.div(first + QB - 1, KB) + 1
+
+
+def attend_kernel(ndoc, scal, q_raw, p0, p1, p2, p3, cos, sin, att, q_out, lse, keys, values):
+    head, block = pl.program_id(0), pl.program_id(1)
+
+    @pl.when((head == 0) & (block == 0))
+    def _():
+        plane = scal[0]
+        for i in range(PLANE):
+            dest = keys if i < 2 else values
+            side = slice((i % 2) * HALF, (i % 2 + 1) * HALF)
+            for j, piece in enumerate((p0, p1, p2, p3)):
+
+                @pl.when(plane == (i ^ j))
+                def _(dest=dest, side=side, piece=piece):
+                    dest[:, side] = piece[...]
+
+        front, back = keys[:, :HALF].astype(F32), keys[:, HALF:].astype(F32)
+        keys[:, :HALF] = (front * cos[...] - back * sin[...]).astype(BF)
+        keys[:, HALF:] = (back * cos[...] + front * sin[...]).astype(BF)
+
+    rows = pl.ds(pl.multiple_of(scal[1] + block * QB, QB), QB)
+    q_cos, q_sin = cos[rows, :], sin[rows, :]
+    front, back = q_raw[:, :HALF], q_raw[:, HALF:]
+    query = jnp.concatenate(
+        [front * q_cos - back * q_sin, back * q_cos + front * q_sin], axis=1
+    ).astype(BF)
+    query = query * jnp.asarray(HD**-0.5, BF)
+    q_out[...] = query
+    positions, starts, low, high = query_bounds(scal, ndoc, block)
+
+    def step(kb, carry):
+        peak, total, mixed = carry
+        span = pl.ds(pl.multiple_of(kb * KB, KB), KB)
+        scores = dot_nt(query, keys[span, :])
+        where = kb * KB + lax.broadcasted_iota(jnp.int32, (QB, KB), 1)
+        scores = jnp.where((where <= positions) & (where >= starts), scores, masked)
+        new_peak = jnp.maximum(peak, jnp.max(scores, axis=1, keepdims=True))
+        weights = jnp.exp(scores - new_peak)
+        keep = jnp.exp(peak - new_peak)
+        total = total * keep + jnp.sum(weights, axis=1, keepdims=True)
+        mixed = mixed * keep + dot_nn(weights.astype(BF), values[span, :])
+        return new_peak, total, mixed
+
+    peak, total, mixed = lax.fori_loop(
+        low,
+        high,
+        step,
+        (jnp.full((QB, 1), -3e38, F32), jnp.zeros((QB, 1), F32), jnp.zeros((QB, HD), F32)),
+    )
+    att[...] = (mixed / total).astype(BF)
+    lse[...] = jnp.broadcast_to(peak + jnp.log(total), (QB, 128))
+
+
+def attend(scal, query_raw, pieces, cos, sin):
+    group, wide = query_raw.shape
+    length = cos.shape[0]
+    heads = wide // HD
+    whole = pl.BlockSpec((length, HALF), lambda h, i, s: (0, 0))
+    token = pl.BlockSpec((QB, HD), lambda h, i, s: (i, h))
+    return pl.pallas_call(
+        lambda *refs: attend_kernel(scal.shape[0] - 2, *refs),
+        grid_spec=pltpu.PrefetchScalarGridSpec(
+            num_scalar_prefetch=1,
+            grid=(heads, group // QB),
+            in_specs=[token] + [whole] * 6,
+            out_specs=[
+                token,
+                token,
+                pl.BlockSpec((QB, 128), lambda h, i, s: (i, h)),
+                pl.BlockSpec((length, HD), lambda h, i, s: (0, 0)),
+                pl.BlockSpec((length, HD), lambda h, i, s: (0, 0)),
+            ],
+        ),
+        out_shape=[
+            jax.ShapeDtypeStruct((group, wide), BF),
+            jax.ShapeDtypeStruct((group, wide), BF),
+            jax.ShapeDtypeStruct((group, heads * 128), F32),
+            jax.ShapeDtypeStruct((length, HD), BF),
+            jax.ShapeDtypeStruct((length, HD), BF),
+        ],
+        compiler_params=params(),
+        cost_estimate=pl.CostEstimate(
+            flops=4 * group * wide * length, bytes_accessed=8 << 20, transcendentals=0
+        ),
+        name="attend",
+    )(scal, query_raw, *pieces, cos, sin)
+
+
+def attend_back_kernel(
+    ndoc, scal, query, keys, values, lse, att, d_att, cos, sin, d_raw, parts, d_keys, d_values
+):
+    head, block = pl.program_id(0), pl.program_id(1)
+
+    @pl.when((head == 0) & (block == 0))
+    def _():
+        d_keys[...] = jnp.zeros_like(d_keys)
+        d_values[...] = jnp.zeros_like(d_values)
+
+    positions, starts, low, high = query_bounds(scal, ndoc, block)
+    peak = lse[:, :1]
+    grad = d_att[...]
+    shared = jnp.sum(grad.astype(F32) * att[...].astype(F32), axis=1, keepdims=True)
+
+    def step(kb, d_query):
+        span = pl.ds(pl.multiple_of(kb * KB, KB), KB)
+        key, value = keys[span, :], values[span, :]
+        scores = dot_nt(query[...], key)
+        where = kb * KB + lax.broadcasted_iota(jnp.int32, (QB, KB), 1)
+        scores = jnp.where((where <= positions) & (where >= starts), scores, masked)
+        probs = jnp.exp(scores - peak)
+        d_probs = dot_nt(grad, value)
+        d_scores = (probs * (d_probs - shared)).astype(BF)
+        d_keys[span, :] += dot_tn(d_scores, query[...])
+        d_values[span, :] += dot_tn(probs.astype(BF), grad)
+        return d_query + dot_nn(d_scores, key)
+
+    d_query = lax.fori_loop(low, high, step, jnp.zeros((QB, HD), F32)) * HD**-0.5
+    rows = pl.ds(pl.multiple_of(scal[1] + block * QB, QB), QB)
+    q_cos, q_sin = cos[rows, :], sin[rows, :]
+    front, back = d_query[:, :HALF], d_query[:, HALF:]
+    d_raw[:, :HALF] = (front * q_cos + back * q_sin).astype(BF)
+    d_raw[:, HALF:] = (back * q_cos - front * q_sin).astype(BF)
+
+    @pl.when((head == pl.num_programs(0) - 1) & (block == pl.num_programs(1) - 1))
+    def _():
+        plane = scal[0]
+        front, back = d_keys[:, :HALF], d_keys[:, HALF:]
+        parts[plane] = front * cos[...] + back * sin[...]
+        parts[plane ^ 1] = back * cos[...] - front * sin[...]
+        parts[plane ^ 2] = d_values[:, :HALF]
+        parts[plane ^ 3] = d_values[:, HALF:]
+
+
+def attend_back(scal, query, keys, values, lse, att, d_att, cos, sin):
+    group, wide = query.shape
+    length = cos.shape[0]
+    heads = wide // HD
+    token = pl.BlockSpec((QB, HD), lambda h, i, s: (i, h))
+    table = pl.BlockSpec((length, HALF), lambda h, i, s: (0, 0))
+    whole = pl.BlockSpec((length, HD), lambda h, i, s: (0, 0))
+    return pl.pallas_call(
+        lambda *refs: attend_back_kernel(scal.shape[0] - 2, *refs),
+        grid_spec=pltpu.PrefetchScalarGridSpec(
+            num_scalar_prefetch=1,
+            grid=(heads, group // QB),
+            in_specs=[token, whole, whole, pl.BlockSpec((QB, 128), lambda h, i, s: (i, h))]
+            + [token, token, table, table],
+            out_specs=[token, pl.BlockSpec((PLANE, length, HALF), lambda h, i, s: (0, 0, 0))],
+            scratch_shapes=[pltpu.VMEM((length, HD), F32), pltpu.VMEM((length, HD), F32)],
+        ),
+        out_shape=[
+            jax.ShapeDtypeStruct((group, wide), BF),
+            jax.ShapeDtypeStruct((PLANE, length, HALF), F32),
+        ],
+        compiler_params=params(),
+        cost_estimate=pl.CostEstimate(
+            flops=10 * group * wide * length, bytes_accessed=12 << 20, transcendentals=0
+        ),
+        name="attend_back",
+    )(scal, query, keys, values, lse, att, d_att, cos, sin)
+
+
+def ffn_kernel(blocks, *refs):
+    h_ref, dy_ref = refs[0], refs[1]
+    gate_up = refs[2 : 2 + blocks]
+    down = refs[2 + blocks : 2 + 2 * blocks]
+    hidden, d_gate_up, d_h, out = refs[2 + 2 * blocks :]
+    units = hidden.shape[1]
+    feat = h_ref.shape[1] // blocks
+
+    def cols(ref, k):
+        return ref[:, k * feat : (k + 1) * feat]
+
+    gate = sum(dot_nt(cols(h_ref, k), gate_up[k][:units, :]) for k in range(blocks))
+    up = sum(dot_nt(cols(h_ref, k), gate_up[k][units:, :]) for k in range(blocks))
+    d_hidden = sum(dot_nt(cols(dy_ref, k), down[k][...]) for k in range(blocks))
+    sig = 1.0 / (1.0 + jnp.exp(-gate))
+    silu = gate * sig
+    hid = (silu * up).astype(BF)
+    hidden[...] = hid
+    d_gate = (d_hidden * up * (sig + silu * (1.0 - sig))).astype(BF)
+    d_up = (d_hidden * silu).astype(BF)
+    d_gate_up[:, :units] = d_gate
+    d_gate_up[:, units:] = d_up
+    for k in range(blocks):
+        span = slice(k * feat, (k + 1) * feat)
+        d_h[:, span] = dot_nn(d_gate, gate_up[k][:units, :]) + dot_nn(d_up, gate_up[k][units:, :])
+        out[:, span] = dot_nn(hid, down[k][...])
+
+
+def feed_forward(h, dy, gate_up, down):
+    count, width = h.shape
+    blocks = len(gate_up)
+    units, feat = down[0].shape
+    tile = min(count, 128)
+    token = lambda size: pl.BlockSpec((tile, size), lambda i: (i, 0))
+    fixed = lambda size: pl.BlockSpec((size, feat), lambda i: (0, 0), pipeline_mode=pl.Buffered(1))
+    return pl.pallas_call(
+        lambda *refs: ffn_kernel(blocks, *refs),
+        grid=(count // tile,),
+        in_specs=[token(width)] * 2 + [fixed(2 * units)] * blocks + [fixed(units)] * blocks,
+        out_specs=[token(units), token(2 * units), token(width), token(width)],
+        out_shape=[
+            jax.ShapeDtypeStruct((count, units), BF),
+            jax.ShapeDtypeStruct((count, 2 * units), BF),
+            jax.ShapeDtypeStruct((count, width), F32),
+            jax.ShapeDtypeStruct((count, width), F32),
+        ],
+        compiler_params=params(),
+        cost_estimate=pl.CostEstimate(
+            flops=12 * count * width * units, bytes_accessed=24 << 20, transcendentals=0
+        ),
+        name="feed_forward",
+    )(h, dy, *gate_up, *down)
 
 
 def shards(
@@ -199,8 +444,6 @@
     count_local, width = own_tokens.shape
     group = count_local * PLANE
     row_length = group * rings
-    heads = HEADS // PLANE
-    score_scale = HD ** (-0.5)
 
     group_tokens = plane_order(plane_gather(own_tokens), plane).astype(F32)
 
@@ -240,98 +483,77 @@
     )
 
     key_positions = jnp.arange(row_length, dtype=jnp.int32)
-    key_segment, key_relative = doc_layout(doc_lengths[0], key_positions)
-    offset = ring * group
-    query_positions = offset + jnp.arange(group, dtype=jnp.int32)
-    query_segment = lax.dynamic_slice_in_dim(key_segment, offset, group)
+    key_relative = doc_layout(doc_lengths[0], key_positions)[1]
     key_cos, key_sin = rope_tables(key_relative, HD // 2)
-    cosine = lax.dynamic_slice_in_dim(key_cos, offset, group)[:, None, :]
-    sine_table = lax.dynamic_slice_in_dim(key_sin, offset, group)[:, None, :]
-    allowed = (query_segment[:, None] == key_segment[None, :]) & (
-        key_positions[None, :] <= query_positions[:, None]
-    )
-
-    hidden_w = jnp.stack([jnp.transpose(w_gate), jnp.transpose(w_up), w_down])
-    hidden_w = jnp.concatenate(plane_gather(hidden_w, 1), axis=1)
-    ffn_w = ring_gather(hidden_w, "rows")
-    hidden_units = hidden_w.shape[1]
-    feat = hidden_w.shape[2]
-    gate_up_w = [w[:2].reshape(2 * hidden_units, feat) for w in ffn_w]
-    down_ffn_w = [w[2] for w in ffn_w]
+    scal = jnp.concatenate([jnp.stack([plane, ring * group]), doc_lengths[0]]).astype(jnp.int32)
+
+    gate_w = plane_gather(jnp.stack([jnp.transpose(w_gate), jnp.transpose(w_up)]))
+    gate_w = jnp.concatenate(gate_w, axis=1)
+    hidden_units, feat = gate_w.shape[1:]
+    gate_up_w = ring_gather(gate_w.reshape(2 * hidden_units, feat), "rows")
+    down_ffn_w = ring_gather(jnp.concatenate(plane_gather(w_down)), "rows")
 
     upstream = out_grad[0]
     upstream_f = upstream.astype(F32)
-    ring_upstream = jnp.concatenate(ring_gather(swap_features(upstream, row, rows), "ring"))
+    ring_upstream = ring_gather(swap_features(upstream, row, rows), "ring")
 
     normed_f = rms_norm(group_tokens, gain_attn)
     normed = normed_f.astype(BF)
     projected = mm(normed, down_w).astype(BF)
     key_value = projected[:, latent_width:]
     key_value = ring_order(ring_gather(key_value, "ring"), ring)
-    key_value = jnp.stack(plane_gather(key_value))
-    key_value = [pick(key_value, plane ^ i) for i in range(PLANE)]
-    key_raw = jnp.concatenate(key_value[:2], axis=1).astype(F32)
-    all_keys = rotate(key_raw, key_cos, key_sin).astype(BF)
-    all_values = jnp.concatenate(key_value[2:], axis=1)
+    key_value = plane_gather(key_value)
 
     latent = plane_order(plane_gather(projected[:, :latent_width]), plane, axis=1).astype(F32)
     latent_normed = rms_norm(latent, gain_query).astype(BF)
-    query_raw = mm(latent_normed, up_query).reshape(group, heads, HD)
-    queries = rotate(query_raw, cosine, sine_table).astype(BF).reshape(group * heads, HD)
-
-    def masked_scores():
-        raw_scores = mm_nt(queries, all_keys) * score_scale
-        return jnp.where(
-            allowed[:, None, :], raw_scores.reshape(group, heads, row_length), masked
-        )
-
-    scores = masked_scores()
-    row_peak = jnp.max(scores, axis=-1, keepdims=True)
-    log_total = row_peak + jnp.log(jnp.sum(jnp.exp(scores - row_peak), axis=-1, keepdims=True))
-    probs_bf = jnp.exp(scores - log_total).astype(BF).reshape(group * heads, row_length)
-    attended = mm(probs_bf, all_values).reshape(group, heads * HD).astype(BF)
+    query_raw = mm(latent_normed, up_query)
+    attended, queries, log_total, all_keys, all_values = attend(
+        scal, query_raw, key_value, key_cos, key_sin
+    )
     branch = mm_nt(attended, out_proj)
     branch = plane_scatter([block_of(branch, plane ^ k, count_local) for k in range(PLANE)])
     middle = own_tokens.astype(F32) + branch
 
     normed2_f, pull_ffn_norm = jax.vjp(rms_norm, middle, gain_ffn)
     normed_ffn = swap_features(normed2_f.astype(BF), row, rows)
-    ring_normed = jnp.concatenate(ring_gather(normed_ffn, "ring"))
-
-    def feature_blocks(value):
-        return [value[:, k * feat : (k + 1) * feat] for k in range(rows)]
-
-    h2_blocks = feature_blocks(ring_normed)
-    dy_blocks = feature_blocks(ring_upstream)
-    gate_up = sum(mm_nt(h, w) for h, w in zip(h2_blocks, gate_up_w))
-    grad_hidden = sum(mm_nt(d, w) for d, w in zip(dy_blocks, down_ffn_w))
-
-    def gated_unit(both):
-        return jax.nn.silu(both[:, :hidden_units]) * both[:, hidden_units:]
-
-    hidden_f, pull_gated = jax.vjp(gated_unit, gate_up)
-    hidden = hidden_f.astype(BF)
-    grad_gate_up = pull_gated(grad_hidden)[0].astype(BF)
-
-    def ring_parts(blocks):
-        whole = jnp.concatenate(blocks, axis=1)
-        return [whole[k * count_local : (k + 1) * count_local] for k in range(rings)]
-
-    grad_normed_ffn = ring_scatter(ring_parts([mm(grad_gate_up, w) for w in gate_up_w]), "ring")
+    normed_ffn = after(normed_ffn, *ring_upstream)
+    ring_normed = ring_gather(normed_ffn, "ring")
+    done = []
+    chunk = 2
+    for first in range(0, rings, chunk):
+        h_part = jnp.concatenate(ring_normed[first : first + chunk])
+        dy_part = jnp.concatenate(ring_upstream[first : first + chunk])
+        done.append((h_part, dy_part) + tuple(feed_forward(h_part, dy_part, gate_up_w, down_ffn_w)))
+
+    def ring_parts(values):
+        return [
+            values[k // chunk][(k % chunk) * count_local : (k % chunk + 1) * count_local]
+            for k in range(rings)
+        ]
+
+    grad_normed_ffn = ring_scatter(ring_parts([d[4] for d in done]), "ring")
+    outs = after(tuple(d[5] for d in done), grad_normed_ffn)
     grad_normed_ffn = swap_features(grad_normed_ffn, row, rows)
-    output = ring_scatter(ring_parts([mm(hidden, w) for w in down_ffn_w]), "ring")
+    output = ring_scatter(ring_parts(outs), "ring")
     output = middle + swap_features(output, row, rows)
 
-    ffn_grad = [
-        jnp.concatenate([mm_tn(grad_gate_up, h), mm_tn(hidden, d)])
-        for h, d in zip(h2_blocks, dy_blocks)
-    ]
-    ffn_grad = ring_scatter(ffn_grad, "rows")
-    ffn_grad = ffn_grad.reshape(3, PLANE, hidden_units // PLANE, feat)
-    ffn_grad = plane_scatter([ffn_grad[:, k] for k in range(PLANE)], axis=1)
-    gate_grad = jnp.transpose(ffn_grad[0])
-    up_grad = jnp.transpose(ffn_grad[1])
-    down_grad = ffn_grad[2]
+    ring_h, ring_dy, hidden, grad_gate_up = (
+        jnp.concatenate([d[k] for d in done]) for k in range(4)
+    )
+
+    def ffn_gradient(left, right, count):
+        blocks = [
+            mm_tn(left, right[:, k * feat : (k + 1) * feat]).astype(BF) for k in range(rows)
+        ]
+        total = ring_scatter([b.astype(F32) for b in blocks], "rows").astype(BF)
+        total = total.reshape(count, PLANE, -1, feat)
+        return plane_scatter(
+            [total[:, k].reshape(-1, feat).astype(F32) for k in range(PLANE)]
+        )
+
+    down_grad = ffn_gradient(hidden, ring_dy, 1)
+    both_grad = ffn_gradient(grad_gate_up, ring_h, 2)
+    gate_grad, up_grad = (jnp.transpose(g) for g in halves(both_grad))
 
     grad_middle_norm, grad_gain_ffn = pull_ffn_norm(grad_normed_ffn)
     grad_middle = upstream_f + grad_middle_norm
@@ -339,28 +561,23 @@
     branch_grad = plane_order(plane_gather(grad_middle.astype(BF)), plane)
     grad_out_w = plane_ring_gradient(mm_tn(branch_grad, attended), spot)
     grad_out_w = jnp.transpose(jnp.concatenate(grad_out_w, axis=1))
-    grad_attended = mm(branch_grad, out_proj).astype(BF).reshape(group * heads, HD)
-    scores = masked_scores()
-    probs_f = jnp.exp(scores - log_total)
-    probs_again = probs_f.astype(BF).reshape(group * heads, row_length)
-    grad_probs = mm_nt(grad_attended, all_values).reshape(group, heads, row_length)
-    grad_scores = probs_f * (grad_probs - jnp.sum(grad_probs * probs_f, axis=-1, keepdims=True))
-    grad_scores = grad_scores.astype(BF).reshape(group * heads, row_length)
-    grad_queries = mm(grad_scores, all_keys) * score_scale
-    key_part = mm_tn(grad_scores, queries) * score_scale
-    value_part = mm_tn(probs_again, grad_attended)
-    key_part = rotate(key_part, key_cos, -key_sin)
-    kv_parts = jnp.stack(
-        [key_part[:, :kv_width], key_part[:, kv_width:]]
-        + [value_part[:, :kv_width], value_part[:, kv_width:]]
-    )
-    kv_grad = plane_scatter([pick(kv_parts, plane ^ k) for k in range(PLANE)])
+    grad_attended = mm(branch_grad, out_proj).astype(BF)
+    grad_query_raw, kv_parts = attend_back(
+        scal,
+        queries,
+        all_keys,
+        all_values,
+        log_total,
+        attended,
+        grad_attended,
+        key_cos,
+        key_sin,
+    )
+    kv_grad = plane_scatter([kv_parts[k] for k in range(PLANE)])
     kv_grad = ring_scatter(
         [block_of(kv_grad, (ring - k) % rings, group) for k in range(rings)], "ring"
     )
 
-    grad_query_raw = rotate(grad_queries.reshape(group, heads, HD), cosine, -sine_table)
-    grad_query_raw = grad_query_raw.reshape(group, heads * HD).astype(BF)
     grad_up_query = plane_ring_gradient(mm_tn(latent_normed, grad_query_raw), spot)
     grad_latent_normed = mm_nt(grad_query_raw, up_query)
     grad_latent_normed = plane_scatter(

time: 913 us -> 741 us (0.81)
  local copies, waits for them, and re-layouts: 163 us -> 51.6 us
  matrix products: 126 us -> 43.3 us
  Pallas kernels: 0 us -> 75.8 us
  other arithmetic: 125 us -> 83.2 us
  waiting for transfers between devices: 348 us -> 311 us
  starting transfers between devices: 138 us -> 160 us
    pallas_call x0 -> x4, Pallas kernels: none -> 75.8 us  [the longest x2 48 us: feed_forward(): pl.pallas_call(lambda *refs: ffn_kernel(blocks, *refs), grid=(count // ti...]
    dot_general x9 -> x3, matrix products: 64.2 us -> 8.28 us  [mm_nt(): return jnp.einsum('ik,jk->ij', left, right, preferred_element_type=F32)]
    reshape x5 -> x0, local copies, waits for them, and re-layouts: 38.4 us -> none  [the longest x1 19 us: masked_scores(): raw_scores.reshape(group, heads, row_length)]
    ppermute x68 -> x78, waiting for transfers between devices: 129 us -> 97.1 us  [flip(): return lax.ppermute(value, 'px' if by == 1 else 'py', [(0, 1), (1, 0)])]
    dot_general x9 -> x3, matrix products: 33.8 us -> 7.34 us  [mm(): return jnp.dot(left, right, preferred_element_type=F32)]
    convert_element_type x4 -> x3, other arithmetic: 32.2 us -> 8.9 us  [the longest x1 7.29 us: ffn_gradient(): total = ring_scatter([b.astype(F32) for b in blocks], 'rows').astype(BF)]
    convert_element_type x3 -> x1, local copies, waits for them, and re-layouts: 22.9 us -> 1.13 us  [plane_scatter(): got_ya = flip(y_a.astype(BF), 2)]
    ppermute x52 -> x54, starting transfers between devices: 41.8 us -> 63.2 us  [shift(): lax.ppermute(value, axis, [(i, (i + by) % count) for i in range(count)])]
  transfers between devices with their start and end apart: 129 -> 141, of which waited for: 62 -> 66; matrix products, arithmetic and copies ran while one was open for 25% -> 23% of each run, Pallas kernels for 0% -> 7%
where the time goes in v2:
time: 741 us; the launch traced here: 729 us
  waiting for transfers between devices  311 us (42%)
  starting transfers between devices  160 us (22%)
  other arithmetic  83.2 us (11%)
  Pallas kernels  75.8 us (10%)
  local copies, waits for them, and re-layouts  51.6 us (7%)
  matrix products  43.3 us (6%)
    ppermute x54, waiting for transfers between devices, shift(): lax.ppermute(value, axis, [(i, (i + by) % count) for i in range(count)])  201 us
    ppermute x78, waiting for transfers between devices, flip(): return lax.ppermute(value, 'px' if by == 1 else 'py', [(0, 1), (1, 0)])  97.1 us
    ppermute x78, starting transfers between devices, flip(): return lax.ppermute(value, 'px' if by == 1 else 'py', [(0, 1), (1, 0)])  86.4 us
    ppermute x54, starting transfers between devices, shift(): lax.ppermute(value, axis, [(i, (i + by) % count) for i in range(count)])  63.2 us
    pallas_call x2, Pallas kernels, feed_forward(): pl.pallas_call(lambda *refs: ffn_kernel(blocks, *refs), grid=(count // ti...  48 us
    dot_general x7, matrix products, mm_tn(): return jnp.einsum('ki,kj->ij', left, right, preferred_element_type=F32)  27.6 us
    unnamed x215, local copies, waits for them, and re-layouts  15.4 us
    pallas_call x1, Pallas kernels, attend_back(): pl.pallas_call(lambda *refs: attend_back_kernel(scal.shape[0] - 2, *refs)...  15 us
  transfers between devices with their start and end apart: 141, of which 66 were waited for; matrix products, arithmetic and copies ran while one was open for 23% of the time, Pallas kernels for 7%

profile of v2, /device:TPU:0, one launch (start us, length us, event | category | flops | bytes accessed | tf_op | source)
XLA Modules:
  0.0 729.3 jit_solution(13284551246335938187)
XLA Ops:
  15.1 5.5 multiply_sine_fusion
  62.9 12.6 %collective-permute-done.15 = bf16[256,384]{1,0:T(8,128)(2,1)S(1)} collective-permute-done((bf16[256,384]{1,0:T(8,128)(2,1)S(1)}, bf16[256,384]{1,0:T(8,128)(2,1)S(1)}, u32[]{:S(2)}, u32[]{:S(2)}) %collective-permute-start.15) | collective-permute-done | bytes 196640 | tf_op jit(solution)/shard_map/ppermute | solution.py:53
  83.6 27.2 %collective-permute-done.26 = bf16[128,1024]{1,0:T(8,128)(2,1)S(1)} collective-permute-done((bf16[128,1024]{1,0:T(8,128)(2,1)S(1)}, bf16[128,1024]{1,0:T(8,128)(2,1)S(1)}, u32[]{:S(2)}, u32[]{:S(2)}) %collective-permute-start.26) | collective-permute-done | bytes 262176 | tf_op jit(solution)/shard_map/ppermute | solution.py:53
  116.3 11.4 %collective-permute-done.40 = bf16[256,1024]{1,0:T(8,128)(2,1)S(1)} collective-permute-done((bf16[256,1024]{1,0:T(8,128)(2,1)S(1)}, bf16[256,1024]{1,0:T(8,128)(2,1)S(1)}, u32[]{:S(2)}, u32[]{:S(2)}) %collective-permute-start.40) | collective-permute-done | bytes 524320 | tf_op jit(solution)/shard_map/ppermute | solution.py:53
  127.7 7.9 %collective-permute-done.41 = bf16[256,1024]{1,0:T(8,128)(2,1)S(1)} collective-permute-done((bf16[256,1024]{1,0:T(8,128)(2,1)S(1)}, bf16[256,1024]{1,0:T(8,128)(2,1)S(1)}, u32[]{:S(2)}, u32[]{:S(2)}) %collective-permute-start.41) | collective-permute-done | bytes 524320 | tf_op jit(solution)/shard_map/ppermute | solution.py:53
  166.5 21.2 %collective-permute-done.20 = bf16[256,256]{1,0:T(8,128)(2,1)S(1)} collective-permute-done((bf16[256,256]{1,0:T(8,128)(2,1)S(1)}, bf16[256,256]{1,0:T(8,128)(2,1)S(1)}, u32[]{:S(2)}, u32[]{:S(2)}) %collective-permute-start.20) | collective-permute-done | bytes 131104 | tf_op jit(solution)/shard_map/ppermute | solution.py:77
  190.2 9.2 %collective-permute-done.32.refs_3_ = bf16[2048,128]{1,0:T(8,128)(2,1)S(1)} collective-permute-done((bf16[2048,128]{1,0:T(8,128)(2,1)S(1)}, bf16[2048,128]{1,0:T(8,128)(2,1)S(1)}, u32[]{:S(2)}, u32[]{:S(2)}) %collective-permute-start.32) | collective-permute-done | bytes 524320 | tf_op jit(solution)/shard_map/ppermute | solution.py:77
  210.2 8.0 %collective-permute-start.49 = (bf16[128,2048]{1,0:T(8,128)(2,1)}, bf16[128,2048]{1,0:T(8,128)(2,1)S(1)}, u32[]{:S(2)}, u32[]{:S(2)}) collective-permute-start(bf16[128,2048]{1,0:T(8,128)(2,1)} %pad_maximum_fusion.36), channel_id=1, source_target_pairs={{0,4},{4,8},{8,12},{12,0},{1,5},{5,9},{9,13},{13,1},{2,6},{6,10},{... | collective-permute-start | bytes 1572872 | tf_op jit(solution)/shard_map/ppermute | solution.py:53
  219.7 12.7 %attend.1 = (bf16[512,1024]{1,0:T(8,128)(2,1)}, bf16[512,1024]{1,0:T(8,128)(2,1)}, f32[512,512]{1,0:T(8,128)}, bf16[2048,256]{1,0:T(8,128)(2,1)}, bf16[2048,256]{1,0:T(8,128)(2,1)}) custom-call(s32[4]{0:T(128)} %pad_add_fusion.refs_0_, f32[512,1024]{1,0:T(8,128)} %fusion.21.refs_1_, bf16[2048,128]{1,0:T(8,128)(2,1)} %copy-done.67, ...), custom_call_target="tpu_custom_call" | custom-call | flops 4294967296 | bytes 8388608 | tf_op jit(solution)/shard_map/attend/pallas_call | solution.py:264
  244.0 10.4 %maximum_maximum_fusion = bf16[2,1408,1024]{2,1,0:T(8,128)(2,1)} fusion(bf16[1,352,1024]{2,1,0:T(8,128)(2,1)S(1)} %collective-permute-done.56, bf16[1,352,1024]{2,1,0:T(8,128)(2,1)} %collective-permute-done.55, bf16[2,352,1024]{2,1,0:T(8,128)(2,1)S(1)} %copy-done.9, bf16[2,352,1024]{2,1,0:T(8,128)(2,1)S(1)} %collective-permute-done.53, ...), kind=kLoop, calls=%fused_computation.4 | loop fusion | flops 34603008 | bytes 11534336 | tf_op jit(solution)/shard_map/concatenate | solution.py:491
  261.5 7.4 %collective-permute-start.50 = (bf16[128,2048]{1,0:T(8,128)(2,1)S(1)}, bf16[128,2048]{1,0:T(8,128)(2,1)S(1)}, u32[]{:S(2)}, u32[]{:S(2)}) collective-permute-start(bf16[128,2048]{1,0:T(8,128)(2,1)S(1)} %collective-permute-done.49), channel_id=1, source_target_pairs={{0,4},{4,8},{8,12},{12,0},{1,5},{5,9},{9,13},{13,1},{2,6},{6,10},{... | collective-permute-start | bytes 1572872 | tf_op jit(solution)/shard_map/ppermute | solution.py:53
  291.9 7.7 %collective-permute-done.51 = bf16[128,2048]{1,0:T(8,128)(2,1)S(1)} collective-permute-done((bf16[128,2048]{1,0:T(8,128)(2,1)S(1)}, bf16[128,2048]{1,0:T(8,128)(2,1)S(1)}, u32[]{:S(2)}, u32[]{:S(2)}) %collective-permute-start.51) | collective-permute-done | bytes 524320 | tf_op jit(solution)/shard_map/ppermute | solution.py:53
  303.2 10.1 %collective-permute-done.52 = bf16[128,2048]{1,0:T(8,128)(2,1)S(1)} collective-permute-done((bf16[128,2048]{1,0:T(8,128)(2,1)S(1)}, bf16[128,2048]{1,0:T(8,128)(2,1)S(1)}, u32[]{:S(2)}, u32[]{:S(2)}) %collective-permute-start.52) | collective-permute-done | bytes 524320 | tf_op jit(solution)/shard_map/ppermute | solution.py:53
  316.8 9.7 %collective-permute-done.63 = bf16[128,2048]{1,0:T(8,128)(2,1)S(1)} collective-permute-done((bf16[128,2048]{1,0:T(8,128)(2,1)S(1)}, bf16[128,2048]{1,0:T(8,128)(2,1)S(1)}, u32[]{:S(2)}, u32[]{:S(2)}) %collective-permute-start.63) | collective-permute-done | bytes 524320 | tf_op jit(solution)/shard_map/ppermute | solution.py:53
  327.7 10.8 %collective-permute-done.64 = bf16[128,2048]{1,0:T(8,128)(2,1)S(1)} collective-permute-done((bf16[128,2048]{1,0:T(8,128)(2,1)S(1)}, bf16[128,2048]{1,0:T(8,128)(2,1)S(1)}, u32[]{:S(2)}, u32[]{:S(2)}) %collective-permute-start.64) | collective-permute-done | bytes 524320 | tf_op jit(solution)/shard_map/ppermute | solution.py:53
  341.3 24.0 %feed_forward.2 = (bf16[256,1408]{1,0:T(8,128)(2,1)}, bf16[256,2816]{1,0:T(8,128)(2,1)}, f32[256,2048]{1,0:T(8,128)}, f32[256,2048]{1,0:T(8,128)}) custom-call(bf16[256,2048]{1,0:T(8,128)(2,1)} %pad_maximum_fusion.21.refs_0_, bf16[256,2048]{1,0:T(8,128)(2,1)} %pad_maximum_fusion.22.refs_1_, bf16[2816,1024]{1,0:T(8,128)(2,1)} %bitcast.122.refs_2_, ...), custom_call_target="tpu_custom_call" | custom-call | flops 8858370048 | bytes 25165824 | tf_op jit(solution)/shard_map/feed_forward/pallas_call | solution.py:402
  366.8 24.0 %feed_forward.3 = (bf16[256,1408]{1,0:T(8,128)(2,1)}, bf16[256,2816]{1,0:T(8,128)(2,1)}, f32[256,2048]{1,0:T(8,128)}, f32[256,2048]{1,0:T(8,128)}) custom-call(bf16[256,2048]{1,0:T(8,128)(2,1)} %pad_maximum_fusion.23.refs_0_, bf16[256,2048]{1,0:T(8,128)(2,1)} %pad_maximum_fusion.24.refs_1_, bf16[2816,1024]{1,0:T(8,128)(2,1)} %bitcast.122.refs_2_, ...), custom_call_target="tpu_custom_call" | custom-call | flops 8858370048 | bytes 25165824 | tf_op jit(solution)/shard_map/feed_forward/pallas_call | solution.py:402
  395.9 8.7 %collective-permute-done.66 = bf16[128,2048]{1,0:T(8,128)(2,1)S(1)} collective-permute-done((bf16[128,2048]{1,0:T(8,128)(2,1)S(1)}, bf16[128,2048]{1,0:T(8,128)(2,1)S(1)}, u32[]{:S(2)}, u32[]{:S(2)}) %collective-permute-start.66) | collective-permute-done | bytes 524320 | tf_op jit(solution)/shard_map/ppermute | solution.py:53
  405.0 10.7 %collective-permute-done.67 = bf16[128,2048]{1,0:T(8,128)(2,1)S(1)} collective-permute-done((bf16[128,2048]{1,0:T(8,128)(2,1)S(1)}, bf16[128,2048]{1,0:T(8,128)(2,1)S(1)}, u32[]{:S(2)}, u32[]{:S(2)}) %collective-permute-start.67) | collective-permute-done | bytes 524320 | tf_op jit(solution)/shard_map/ppermute | solution.py:53
  442.1 7.8 %collective-permute-done.69 = bf16[128,2048]{1,0:T(8,128)(2,1)} collective-permute-done((bf16[128,2048]{1,0:T(8,128)(2,1)}, bf16[128,2048]{1,0:T(8,128)(2,1)}, u32[]{:S(2)}, u32[]{:S(2)}) %collective-permute-start.69) | collective-permute-done | bytes 524320 | tf_op jit(solution)/shard_map/ppermute | solution.py:53
  465.8 5.6 fusion.67
  474.8 15.0 %attend_back.1 = (bf16[512,1024]{1,0:T(8,128)(2,1)}, f32[4,2048,128]{2,1,0:T(8,128)}) custom-call(s32[4]{0:T(128)} %pad_add_fusion.refs_0_, bf16[512,1024]{1,0:T(8,128)(2,1)} %get-tuple-element.39.refs_1_, bf16[2048,256]{1,0:T(8,128)(2,1)} %get-tuple-element.40.refs_2_, bf16[2048,256]{1,0:T(8,128)(2,1)} %get-tuple-element.41.refs_3_, ...), custom_call_target="tpu_custom_call" | custom-call | flops 10737418240 | bytes 12582912 | tf_op jit(solution)/shard_map/attend_back/pallas_call | solution.py:345
  494.1 5.4 dynamic-slice_convert_fusion
  600.2 6.8 collective-permute-done.115
  608.1 8.1 %collective-permute-done.116 = bf16[128,1024]{1,0:T(8,128)(2,1)S(1)} collective-permute-done((bf16[128,1024]{1,0:T(8,128)(2,1)S(1)}, bf16[128,1024]{1,0:T(8,128)(2,1)S(1)}, u32[]{:S(2)}, u32[]{:S(2)}) %collective-permute-start.116) | collective-permute-done | bytes 262176 | tf_op jit(solution)/shard_map/ppermute | solution.py:53
  637.8 7.5 %collective-permute-done.108 = bf16[256,384]{1,0:T(8,128)(2,1)S(1)} collective-permute-done((bf16[256,384]{1,0:T(8,128)(2,1)S(1)}, bf16[256,384]{1,0:T(8,128)(2,1)S(1)}, u32[]{:S(2)}, u32[]{:S(2)}) %collective-permute-start.108) | collective-permute-done | bytes 196640 | tf_op jit(solution)/shard_map/ppermute | solution.py:53
  646.6 8.3 %collective-permute-done.109 = bf16[256,384]{1,0:T(8,128)(2,1)S(1)} collective-permute-done((bf16[256,384]{1,0:T(8,128)(2,1)S(1)}, bf16[256,384]{1,0:T(8,128)(2,1)S(1)}, u32[]{:S(2)}, u32[]{:S(2)}) %collective-permute-start.109) | collective-permute-done | bytes 196640 | tf_op jit(solution)/shard_map/ppermute | solution.py:53
  664.2 7.3 add_convert_fusion
  671.5 6.7 collective-permute-done.122
  685.3 5.6 collective-permute-done.123
  702.0 12.5 %collective-permute-done.124 = bf16[64,1024]{1,0:T(8,128)(2,1)S(1)} collective-permute-done((bf16[64,1024]{1,0:T(8,128)(2,1)S(1)}, bf16[64,1024]{1,0:T(8,128)(2,1)S(1)}, u32[]{:S(2)}, u32[]{:S(2)}) %collective-permute-start.124) | collective-permute-done | bytes 131104 | tf_op jit(solution)/shard_map/ppermute | solution.py:77
  717.8 8.0 %collective-permute-done.130 = bf16[352,1024]{1,0:T(8,128)(2,1)S(1)} collective-permute-done((bf16[352,1024]{1,0:T(8,128)(2,1)S(1)}, bf16[352,1024]{1,0:T(8,128)(2,1)S(1)}, u32[]{:S(2)}, u32[]{:S(2)}) %collective-permute-start.130) | collective-permute-done | bytes 720928 | tf_op jit(solution)/shard_map/ppermute | solution.py:77
  (705 shorter events, 381.6 us)
Async XLA Ops:
  0.6 110.6 %collective-permute-start = (bf16[128,2048]{1,0:T(8,128)(2,1)}, bf16[128,2048]{1,0:T(8,128)(2,1)S(1)}, u32[]{:S(2)}, u32[]{:S(2)}) collective-permute-start(bf16[128,2048]{1,0:T(8,128)(2,1)} %bitcast.441), channel_id=1, source_target_pairs={{0,1},{1,0},{2,3},{3,2},{4,5},{5,4},{6,7},{7,6},{8,9},{9,8},{10,11... | collective-permute-start | bytes 1572872 | tf_op jit(solution)/shard_map/ppermute | solution.py:77
  3.6 109.2 %collective-permute-start.1 = (bf16[128,2048]{1,0:T(8,128)(2,1)}, bf16[128,2048]{1,0:T(8,128)(2,1)}, u32[]{:S(2)}, u32[]{:S(2)}) collective-permute-start(bf16[128,2048]{1,0:T(8,128)(2,1)} %bitcast.442), channel_id=1, source_target_pairs={{0,2},{2,0},{1,3},{3,1},{4,6},{6,4},{5,7},{7,5},{8,10},{10,8},{9,1... | collective-permute-start | bytes 1572872 | tf_op jit(solution)/shard_map/ppermute | solution.py:77
  75.5 35.3 %collective-permute-start.26 = (bf16[128,1024]{1,0:T(8,128)(2,1)S(1)}, bf16[128,1024]{1,0:T(8,128)(2,1)S(1)}, u32[]{:S(2)}, u32[]{:S(2)}) collective-permute-start(bf16[128,1024]{1,0:T(8,128)(2,1)S(1)} %get-tuple-element.184), channel_id=1, source_target_pairs={{0,8},{4,12},{8,0},{12,4},{1,9},{5,13},{9,1},{13,5},{2,10},{6,14},... | collective-permute-start | bytes 786440 | tf_op jit(solution)/shard_map/ppermute | solution.py:53
  75.6 35.3 %collective-permute-start.27 = (bf16[128,1024]{1,0:T(8,128)(2,1)S(1)}, bf16[128,1024]{1,0:T(8,128)(2,1)S(1)}, u32[]{:S(2)}, u32[]{:S(2)}) collective-permute-start(bf16[128,1024]{1,0:T(8,128)(2,1)S(1)} %get-tuple-element.184), channel_id=1, source_target_pairs={{0,12},{4,0},{8,4},{12,8},{1,13},{5,1},{9,5},{13,9},{2,14},{6,2},{... | collective-permute-start | bytes 786440 | tf_op jit(solution)/shard_map/ppermute | solution.py:53
  78.3 37.1 %collective-permute-start.39 = (bf16[256,1024]{1,0:T(8,128)(2,1)S(1)}, bf16[256,1024]{1,0:T(8,128)(2,1)S(1)}, u32[]{:S(2)}, u32[]{:S(2)}) collective-permute-start(bf16[256,1024]{1,0:T(8,128)(2,1)S(1)} %get-tuple-element.148), channel_id=1, source_target_pairs={{0,4},{4,8},{8,12},{12,0},{1,5},{5,9},{9,13},{13,1},{2,6},{6,10},{... | collective-permute-start | bytes 1572872 | tf_op jit(solution)/shard_map/ppermute | solution.py:53
  110.8 24.8 %collective-permute-start.41 = (bf16[256,1024]{1,0:T(8,128)(2,1)S(1)}, bf16[256,1024]{1,0:T(8,128)(2,1)S(1)}, u32[]{:S(2)}, u32[]{:S(2)}) collective-permute-start(bf16[256,1024]{1,0:T(8,128)(2,1)S(1)} %get-tuple-element.148), channel_id=1, source_target_pairs={{0,12},{4,0},{8,4},{12,8},{1,13},{5,1},{9,5},{13,9},{2,14},{6,2},{... | collective-permute-start | bytes 1572872 | tf_op jit(solution)/shard_map/ppermute | solution.py:53
  111.3 24.7 %collective-permute-start.2 = (bf16[64,2048]{1,0:T(8,128)(2,1)S(1)}, bf16[64,2048]{1,0:T(8,128)(2,1)S(1)}, u32[]{:S(2)}, u32[]{:S(2)}) collective-permute-start(bf16[64,2048]{1,0:T(8,128)(2,1)S(1)} %slice.532), channel_id=1, source_target_pairs={{0,2},{2,0},{1,3},{3,1},{4,6},{6,4},{5,7},{7,5},{8,10},{10,8},{9,1... | collective-permute-start | bytes 786440 | tf_op jit(solution)/shard_map/ppermute | solution.py:77
  115.4 89.8 %collective-permute-start.53 = (bf16[2,352,1024]{2,1,0:T(8,128)(2,1)S(1)}, bf16[2,352,1024]{2,1,0:T(8,128)(2,1)S(1)}, u32[]{:S(2)}, u32[]{:S(2)}) collective-permute-start(bf16[2,352,1024]{2,1,0:T(8,128)(2,1)S(1)} %copy-done.45), channel_id=1, source_target_pairs={{0,1},{1,0},{2,3},{3,2},{4,5},{5,4},{6,7},{7,6},{8,9},{9,8},{10,11... | collective-permute-start | bytes 4325384 | tf_op jit(solution)/shard_map/ppermute | solution.py:77
  135.6 25.7 %collective-permute-start.28 = (bf16[512,1024]{1,0:T(8,128)(2,1)S(1)}, bf16[512,1024]{1,0:T(8,128)(2,1)S(1)}, u32[]{:S(2)}, u32[]{:S(2)}) collective-permute-start(bf16[512,1024]{1,0:T(8,128)(2,1)S(1)} %get-tuple-element.119), channel_id=1, source_target_pairs={{0,16},{16,0},{1,17},{17,1},{2,18},{18,2},{3,19},{19,3},{4,20},{20... | collective-permute-start | bytes 3145736 | tf_op jit(solution)/shard_map/ppermute | solution.py:53
  152.7 55.5 %collective-permute-start.54 = (bf16[2,352,1024]{2,1,0:T(8,128)(2,1)S(1)}, bf16[2,352,1024]{2,1,0:T(8,128)(2,1)S(1)}, u32[]{:S(2)}, u32[]{:S(2)}) collective-permute-start(bf16[2,352,1024]{2,1,0:T(8,128)(2,1)S(1)} %copy-done.45), channel_id=1, source_target_pairs={{0,2},{2,0},{1,3},{3,1},{4,6},{6,4},{5,7},{7,5},{8,10},{10,8},{9,1... | collective-permute-start | bytes 4325384 | tf_op jit(solution)/shard_map/ppermute | solution.py:77
  157.1 75.3 %collective-permute-start.42 = (bf16[1024,1024]{1,0:T(8,128)(2,1)}, bf16[1024,1024]{1,0:T(8,128)(2,1)}, u32[]{:S(2)}, u32[]{:S(2)}) collective-permute-start(bf16[1024,1024]{1,0:T(8,128)(2,1)} %get-tuple-element.94), channel_id=1, source_target_pairs={{0,16},{16,0},{1,17},{17,1},{2,18},{18,2},{3,19},{19,3},{4,20},{20... | collective-permute-start | bytes 6291464 | tf_op jit(solution)/shard_map/ppermute | solution.py:53
  161.3 26.4 %collective-permute-start.20 = (bf16[256,256]{1,0:T(8,128)(2,1)S(1)}, bf16[256,256]{1,0:T(8,128)(2,1)S(1)}, u32[]{:S(2)}, u32[]{:S(2)}) collective-permute-start(bf16[256,256]{1,0:T(8,128)(2,1)S(1)} %slice.536), channel_id=1, source_target_pairs={{0,2},{2,0},{1,3},{3,1},{4,6},{6,4},{5,7},{7,5},{8,10},{10,8},{9,1... | collective-permute-start | bytes 393224 | tf_op jit(solution)/shard_map/ppermute | solution.py:77
  165.6 23.5 %collective-permute-start.21 = (bf16[256,256]{1,0:T(8,128)(2,1)S(1)}, bf16[256,256]{1,0:T(8,128)(2,1)S(1)}, u32[]{:S(2)}, u32[]{:S(2)}) collective-permute-start(bf16[256,256]{1,0:T(8,128)(2,1)S(1)} %slice.537), channel_id=1, source_target_pairs={{0,1},{1,0},{2,3},{3,2},{4,5},{5,4},{6,7},{7,6},{8,9},{9,8},{10,11... | collective-permute-start | bytes 393224 | tf_op jit(solution)/shard_map/ppermute | solution.py:77
  205.2 52.2 %collective-permute-start.58 = (bf16[352,1024]{1,0:T(8,128)(2,1)}, bf16[352,1024]{1,0:T(8,128)(2,1)}, u32[]{:S(2)}, u32[]{:S(2)}) collective-permute-start(bf16[352,1024]{1,0:T(8,128)(2,1)} %param.27), channel_id=1, source_target_pairs={{0,1},{1,0},{2,3},{3,2},{4,5},{5,4},{6,7},{7,6},{8,9},{9,8},{10,11... | collective-permute-start | bytes 2162696 | tf_op jit(solution)/shard_map/ppermute | solution.py:77
  208.2 53.3 %collective-permute-start.59 = (bf16[352,1024]{1,0:T(8,128)(2,1)}, bf16[352,1024]{1,0:T(8,128)(2,1)}, u32[]{:S(2)}, u32[]{:S(2)}) collective-permute-start(bf16[352,1024]{1,0:T(8,128)(2,1)} %param.27), channel_id=1, source_target_pairs={{0,2},{2,0},{1,3},{3,1},{4,6},{6,4},{5,7},{7,5},{8,10},{10,8},{9,1... | collective-permute-start | bytes 2162696 | tf_op jit(solution)/shard_map/ppermute | solution.py:77
  210.2 45.8 %collective-permute-start.49 = (bf16[128,2048]{1,0:T(8,128)(2,1)}, bf16[128,2048]{1,0:T(8,128)(2,1)S(1)}, u32[]{:S(2)}, u32[]{:S(2)}) collective-permute-start(bf16[128,2048]{1,0:T(8,128)(2,1)} %pad_maximum_fusion.36), channel_id=1, source_target_pairs={{0,4},{4,8},{8,12},{12,0},{1,5},{5,9},{9,13},{13,1},{2,6},{6,10},{... | collective-permute-start | bytes 1572872 | tf_op jit(solution)/shard_map/ppermute | solution.py:53
  254.4 86.9 %collective-permute-start.57 = (bf16[2816,1024]{1,0:T(8,128)(2,1)}, bf16[2816,1024]{1,0:T(8,128)(2,1)}, u32[]{:S(2)}, u32[]{:S(2)}) collective-permute-start(bf16[2816,1024]{1,0:T(8,128)(2,1)} %bitcast.122.refs_2_), channel_id=1, source_target_pairs={{0,16},{16,0},{1,17},{17,1},{2,18},{18,2},{3,19},{19,3},{4,20},{20... | collective-permute-start | bytes 17301512 | tf_op jit(solution)/shard_map/ppermute | solution.py:53
  289.7 50.0 %collective-permute-start.62 = (bf16[1408,1024]{1,0:T(8,128)(2,1)S(1)}, bf16[1408,1024]{1,0:T(8,128)(2,1)S(1)}, u32[]{:S(2)}, u32[]{:S(2)}) collective-permute-start(bf16[1408,1024]{1,0:T(8,128)(2,1)S(1)} %constant_dynamic-update-slice_fusion.refs_4_), channel_id=1, source_target_pairs={{0,16},{16,0},{1,17},{17,1},{2,18},{18,2},{3,19},{19,3},{4,20},{20... | collective-permute-start | bytes 8650760 | tf_op jit(solution)/shard_map/ppermute | solution.py:53
  366.6 24.3 %collective-permute-start.65 = (bf16[128,2048]{1,0:T(8,128)(2,1)S(1)}, bf16[128,2048]{1,0:T(8,128)(2,1)S(1)}, u32[]{:S(2)}, u32[]{:S(2)}) collective-permute-start(bf16[128,2048]{1,0:T(8,128)(2,1)S(1)} %slice.664), channel_id=1, source_target_pairs={{0,4},{4,8},{8,12},{12,0},{1,5},{5,9},{9,13},{13,1},{2,6},{6,10},{... | collective-permute-start | bytes 1572872 | tf_op jit(solution)/shard_map/ppermute | solution.py:53
  395.9 55.6 %collective-permute-start.134 = (bf16[1408,1024]{1,0:T(8,128)(2,1)}, bf16[1408,1024]{1,0:T(8,128)(2,1)}, u32[]{:S(2)}, u32[]{:S(2)}) collective-permute-start(bf16[1408,1024]{1,0:T(8,128)(2,1)} %convolution_convert_fusion.2), channel_id=1, source_target_pairs={{0,16},{16,0},{1,17},{17,1},{2,18},{18,2},{3,19},{19,3},{4,20},{20... | collective-permute-start | bytes 8650760 | tf_op jit(solution)/shard_map/ppermute | solution.py:53
  456.6 49.4 %collective-permute-start.136 = (bf16[176,1024]{1,0:T(8,128)(2,1)}, bf16[176,1024]{1,0:T(8,128)(2,1)}, u32[]{:S(2)}, u32[]{:S(2)}) collective-permute-start(bf16[176,1024]{1,0:T(8,128)(2,1)} %get-tuple-element.77), channel_id=1, source_target_pairs={{0,2},{2,0},{1,3},{3,1},{4,6},{6,4},{5,7},{7,5},{8,10},{10,8},{9,1... | collective-permute-start | bytes 1081352 | tf_op jit(solution)/shard_map/ppermute | solution.py:77
  457.2 50.9 %collective-permute-start.139 = (bf16[176,1024]{1,0:T(8,128)(2,1)}, bf16[176,1024]{1,0:T(8,128)(2,1)}, u32[]{:S(2)}, u32[]{:S(2)}) collective-permute-start(bf16[176,1024]{1,0:T(8,128)(2,1)} %get-tuple-element.75), channel_id=1, source_target_pairs={{0,1},{1,0},{2,3},{3,2},{4,5},{5,4},{6,7},{7,6},{8,9},{9,8},{10,11... | collective-permute-start | bytes 1081352 | tf_op jit(solution)/shard_map/ppermute | solution.py:77
  458.9 76.8 %collective-permute-start.135 = (bf16[176,1024]{1,0:T(8,128)(2,1)}, bf16[176,1024]{1,0:T(8,128)(2,1)}, u32[]{:S(2)}, u32[]{:S(2)}) collective-permute-start(bf16[176,1024]{1,0:T(8,128)(2,1)} %get-tuple-element.74), channel_id=1, source_target_pairs={{0,2},{2,0},{1,3},{3,1},{4,6},{6,4},{5,7},{7,5},{8,10},{10,8},{9,1... | collective-permute-start | bytes 1081352 | tf_op jit(solution)/shard_map/ppermute | solution.py:77
  510.5 26.5 %collective-permute-start.138 = (bf16[176,1024]{1,0:T(8,128)(2,1)S(1)}, bf16[176,1024]{1,0:T(8,128)(2,1)}, u32[]{:S(2)}, u32[]{:S(2)}) collective-permute-start(bf16[176,1024]{1,0:T(8,128)(2,1)S(1)} %copy-done.71), channel_id=1, source_target_pairs={{0,1},{1,0},{2,3},{3,2},{4,5},{5,4},{6,7},{7,6},{8,9},{9,8},{10,11... | collective-permute-start | bytes 1081352 | tf_op jit(solution)/shard_map/ppermute | solution.py:77
  534.1 130.2 %collective-permute-start.127 = (bf16[2816,1024]{1,0:T(8,128)(2,1)}, bf16[2816,1024]{1,0:T(8,128)(2,1)}, u32[]{:S(2)}, u32[]{:S(2)}) collective-permute-start(bf16[2816,1024]{1,0:T(8,128)(2,1)} %convolution_convert_fusion), channel_id=1, source_target_pairs={{0,16},{16,0},{1,17},{17,1},{2,18},{18,2},{3,19},{19,3},{4,20},{20... | collective-permute-start | bytes 17301512 | tf_op jit(solution)/shard_map/ppermute | solution.py:53
  536.9 33.2 %collective-permute-start.113 = (bf16[512,1024]{1,0:T(8,128)(2,1)S(1)}, bf16[512,1024]{1,0:T(8,128)(2,1)S(1)}, u32[]{:S(2)}, u32[]{:S(2)}) collective-permute-start(bf16[512,1024]{1,0:T(8,128)(2,1)S(1)} %copy-done.58), channel_id=1, source_target_pairs={{0,16},{16,0},{1,17},{17,1},{2,18},{18,2},{3,19},{19,3},{4,20},{20... | collective-permute-start | bytes 3145736 | tf_op jit(solution)/shard_map/ppermute | solution.py:53
  538.1 22.2 %collective-permute-start.81 = (bf16[128,256]{1,0:T(8,128)(2,1)S(1)}, bf16[128,256]{1,0:T(8,128)(2,1)S(1)}, u32[]{:S(2)}, u32[]{:S(2)}) collective-permute-start(bf16[128,256]{1,0:T(8,128)(2,1)S(1)} %get-tuple-element.180), channel_id=1, source_target_pairs={{0,1},{1,0},{2,3},{3,2},{4,5},{5,4},{6,7},{7,6},{8,9},{9,8},{10,11... | collective-permute-start | bytes 196616 | tf_op jit(solution)/shard_map/ppermute | solution.py:77
  570.5 23.9 %collective-permute-start.114 = (bf16[128,1024]{1,0:T(8,128)(2,1)S(1)}, bf16[128,1024]{1,0:T(8,128)(2,1)S(1)}, u32[]{:S(2)}, u32[]{:S(2)}) collective-permute-start(bf16[128,1024]{1,0:T(8,128)(2,1)S(1)} %dynamic-slice_convert_fusion.10), channel_id=1, source_target_pairs={{0,4},{4,8},{8,12},{12,0},{1,5},{5,9},{9,13},{13,1},{2,6},{6,10},{... | collective-permute-start | bytes 786440 | tf_op jit(solution)/shard_map/ppermute | solution.py:53
  590.3 39.6 %collective-permute-start.106 = (bf16[1024,384]{1,0:T(8,128)(2,1)S(1)}, bf16[1024,384]{1,0:T(8,128)(2,1)S(1)}, u32[]{:S(2)}, u32[]{:S(2)}) collective-permute-start(bf16[1024,384]{1,0:T(8,128)(2,1)S(1)} %dynamic-slice_convert_fusion.2), channel_id=1, source_target_pairs={{0,16},{16,0},{1,17},{17,1},{2,18},{18,2},{3,19},{19,3},{4,20},{20... | collective-permute-start | bytes 2359304 | tf_op jit(solution)/shard_map/ppermute | solution.py:53
  682.0 35.8 %collective-permute-start.128 = (bf16[352,1024]{1,0:T(8,128)(2,1)S(1)}, bf16[352,1024]{1,0:T(8,128)(2,1)S(1)}, u32[]{:S(2)}, u32[]{:S(2)}) collective-permute-start(bf16[352,1024]{1,0:T(8,128)(2,1)S(1)} %get-tuple-element.59), channel_id=1, source_target_pairs={{0,2},{2,0},{1,3},{3,1},{4,6},{6,4},{5,7},{7,5},{8,10},{10,8},{9,1... | collective-permute-start | bytes 2162696 | tf_op jit(solution)/shard_map/ppermute | solution.py:77
  683.5 34.3 %collective-permute-start.131 = (bf16[352,1024]{1,0:T(8,128)(2,1)S(1)}, bf16[352,1024]{1,0:T(8,128)(2,1)S(1)}, u32[]{:S(2)}, u32[]{:S(2)}) collective-permute-start(bf16[352,1024]{1,0:T(8,128)(2,1)S(1)} %get-tuple-element.56), channel_id=1, source_target_pairs={{0,1},{1,0},{2,3},{3,2},{4,5},{5,4},{6,7},{7,6},{8,9},{9,8},{10,11... | collective-permute-start | bytes 2162696 | tf_op jit(solution)/shard_map/ppermute | solution.py:77
  692.3 22.2 %collective-permute-start.124 = (bf16[64,1024]{1,0:T(8,128)(2,1)S(1)}, bf16[64,1024]{1,0:T(8,128)(2,1)S(1)}, u32[]{:S(2)}, u32[]{:S(2)}) collective-permute-start(bf16[64,1024]{1,0:T(8,128)(2,1)S(1)} %get-tuple-element.138), channel_id=1, source_target_pairs={{0,1},{1,0},{2,3},{3,2},{4,5},{5,4},{6,7},{7,6},{8,9},{9,8},{10,11... | collective-permute-start | bytes 393224 | tf_op jit(solution)/shard_map/ppermute | solution.py:77
  (208 other events, 2602.4 us)

commit v3 on v2

v3 whole, which is shorter than its diff:
```python
import jax
import jax.numpy as jnp
import numpy as np
from jax import lax
from jax.experimental import pallas as pl
from jax.experimental.pallas import tpu as pltpu
from jax.sharding import Mesh, PartitionSpec as P

HEADS = 16
HD = 256
PLANE = 4
EXTRA = 16

masked = -1e30
epsilon = 1e-05
BF = jnp.bfloat16
F32 = jnp.float32


def rms_norm(values, gain_vec):
    return (
        values * lax.rsqrt(jnp.mean(values * values, axis=-1, keepdims=True) + epsilon) * gain_vec
    )


def rope_tables(relative, half_dim):
    frequency = 1.0 / 10000.0 ** (jnp.arange(half_dim, dtype=F32) / half_dim)
    angles = relative.astype(F32)[..., None] * frequency
    return (jnp.cos(angles), jnp.sin(angles))


def doc_layout(lengths, positions):
    doc_ends = jnp.cumsum(lengths)
    passed = positions[:, None] >= doc_ends[None, :]
    segment = jnp.sum(passed.astype(jnp.int32), axis=1)
    doc_start = jnp.sum(jnp.where(passed, lengths[None, :], 0), axis=1)
    return (segment, positions - doc_start)


def mm(left, right):
    return jnp.dot(left, right, preferred_element_type=F32)


def mm_nt(left, right):
    return jnp.einsum("ik,jk->ij", left, right, preferred_element_type=F32)


def mm_tn(left, right):
    return jnp.einsum("ki,kj->ij", left, right, preferred_element_type=F32)


def shift(value, axis, by=1):
    count = lax.axis_size(axis)
    return lax.ppermute(value, axis, [(i, (i + by) % count) for i in range(count)])


def ring_gather(value, axis):
    pieces = [value]
    for _ in range(lax.axis_size(axis) - 1):
        pieces.append(shift(pieces[-1], axis))
    return pieces


def ring_spread(value, axis):
    return [value] + [shift(value, axis, k) for k in range(1, lax.axis_size(axis))]


def ring_scatter(parts, axis):
    total = parts[1]
    for k in range(2, len(parts) + 1):
        total = shift(total.astype(BF), axis).astype(F32) + parts[k % len(parts)]
    return total


def flip(value, by):
    if by == 3:
        return lax.ppermute(value, ("py", "px"), [(i, i ^ 3) for i in range(PLANE)])
    return lax.ppermute(value, "px" if by == 1 else "py", [(0, 1), (1, 0)])


def halves(value, axis=0):
    half = value.shape[axis] // 2
    return (
        lax.slice_in_dim(value, 0, half, axis=axis),
        lax.slice_in_dim(value, half, 2 * half, axis=axis),
    )


def plane_spread(value):
    return [value] + [flip(value, k) for k in range(1, PLANE)]


def plane_sum(parts):
    got = [flip(parts[k].astype(BF), k) for k in range(1, PLANE)]
    return sum((g.astype(F32) for g in got), parts[0].astype(F32))


def token_of(started):
    return shift(started[:8, :128], "rows")


def plane_swap(parts):
    return [parts[0]] + [flip(parts[k], k) for k in range(1, PLANE)]


def pick(stacked, index):
    return lax.dynamic_index_in_dim(stacked, index, 0, keepdims=False)


def place(items, count, unit=None, split=None):
    unit = unit or items[0][0].shape[0]
    columns = items[0][0].shape[1]
    pieces = [v.reshape(-1, unit, columns) for v, _ in items]
    number = len(pieces)
    cuts = [(0, unit)] if split is None else [(0, split), (split, unit)]

    def kernel(slots, *refs):
        outs, sems = refs[number:-1], refs[-1]
        copies = []
        for i in range(number):
            span = pl.ds(slots[i], pieces[i].shape[0])
            for j, (start, stop) in enumerate(cuts):
                source = refs[i] if split is None else refs[i].at[:, pl.ds(start, stop - start)]
                copies.append(pltpu.make_async_copy(source, outs[j].at[span], sems.at[i, j]))
        for copy in copies:
            copy.start()
        for copy in copies:
            copy.wait()

    shapes = [(count, stop - start, columns) for start, stop in cuts]
    outs = pl.pallas_call(
        kernel,
        grid_spec=pltpu.PrefetchScalarGridSpec(
            num_scalar_prefetch=1,
            grid=(1,),
            in_specs=[pl.BlockSpec(memory_space=pl.ANY)] * number,
            out_specs=[pl.BlockSpec(shape, lambda i, s: (0, 0, 0)) for shape in shapes],
            scratch_shapes=[pltpu.SemaphoreType.DMA((number, len(cuts)))],
        ),
        out_shape=[jax.ShapeDtypeStruct(shape, pieces[0].dtype) for shape in shapes],
        compiler_params=params(),
        cost_estimate=pl.CostEstimate(
            flops=0, bytes_accessed=4 * count * unit * columns, transcendentals=0
        ),
        name="place",
    )(jnp.stack([jnp.asarray(slot, jnp.int32) for _, slot in items]), *pieces)
    if split is None:
        return outs[0].reshape(-1, columns)
    return outs


def plane_place(blocks, index):
    return place([(p, index ^ k) for k, p in enumerate(blocks)], PLANE)


def ring_place(pieces, index):
    count = len(pieces)
    return place([(p, (index - k) % count) for k, p in enumerate(pieces)], count)


def block_of(value, index, size, axis=0):
    return lax.dynamic_slice_in_dim(value, index * size, size, axis)


def column_swap(weight, index):
    size = weight.shape[1] // PLANE
    parts = [block_of(weight, index ^ k, size, 1) for k in range(PLANE)]
    return place([(p, index ^ k) for k, p in enumerate(plane_swap(parts))], PLANE)


def rows_place(pieces, row, ring, split=None):
    rings, rows = len(pieces), lax.axis_size("rows")
    unit = pieces[0].shape[0] // PLANE
    own = ring_place(pieces, ring)
    items = [
        (got, (row - j) % rows * rings * PLANE) for j, got in enumerate(ring_spread(own, "rows"))
    ]
    return place(items, rings * rows * PLANE, unit, split)


def row_blocks(left, right, spot, extra=None):
    row, rows = spot[0], lax.axis_size("rows")
    size = left.shape[1] // rows

    def block(k):
        index = (row - k) % rows
        result = mm_tn(block_of(left, index, size, 1), right)
        if extra is not None:
            more = pick(extra, index)
            result = result.reshape(more.shape[0], -1, result.shape[1])
            result = jnp.concatenate([result, more], axis=1).reshape(-1, result.shape[2])
        return result

    return block


def over_rows(block):
    rows = lax.axis_size("rows")
    total = block(1).astype(BF) if rows > 1 else block(0)
    for k in range(2, rows + 1):
        total = shift(total, "rows").astype(F32) + block(k % rows)
        total = total.astype(BF)
    return total


def over_ring(total, spot, pending=()):
    ring, rings = spot[1], lax.axis_size("ring")
    size = total.shape[0] // rings
    total, pending = ring_scatter_bf(
        [block_of(total, (ring - k) % rings, size) for k in range(rings)], pending
    )
    return total.astype(BF), pending


def over_plane(total, spot):
    plane = spot[2]
    size = total.shape[0] // PLANE
    got = plane_swap([block_of(total, plane ^ k, size) for k in range(PLANE)])
    return place([(g, plane ^ k) for k, g in enumerate(got)], PLANE)


def ring_scatter_bf(parts, pending=()):
    count = len(parts)
    total = parts[1]
    for k in range(2, count + 1):
        total = shift(total, "ring").astype(F32) + parts[k % count].astype(F32)
        if k < count:
            total = total.astype(BF)
        if k == 2 and pending:
            total, *pending = tie(total, *pending)
    return total, pending


def tie(value, *deps):
    return lax.optimization_barrier((value,) + deps)


def params():
    return pltpu.CompilerParams(vmem_limit_bytes=56 * 1024 * 1024)


def dot_nn(left, right):
    return lax.dot_general(left, right, (((1,), (0,)), ((), ())), preferred_element_type=F32)


def dot_nt(left, right):
    return lax.dot_general(left, right, (((1,), (1,)), ((), ())), preferred_element_type=F32)


def dot_tn(left, right):
    return lax.dot_general(left, right, (((0,), (0,)), ((), ())), preferred_element_type=F32)


QB = 256
KB = 512
HALF = HD // 2


def query_bounds(scal, ndoc, block):
    first = scal[1] + block * QB
    positions = first + lax.broadcasted_iota(jnp.int32, (QB, 1), 0)
    starts = jnp.zeros((QB, 1), jnp.int32)
    low_start, end = 0, 0
    for n in range(ndoc):
        end = end + scal[2 + n]
        starts = jnp.where(positions >= end, end, starts)
        low_start = jnp.where(first >= end, end, low_start)
    return positions, starts, lax.div(low_start, KB), lax.div(first + QB - 1, KB) + 1


def attend_kernel(ndoc, scal, q_raw, p0, p1, p2, p3, cos, sin, att, q_out, lse, keys, values):
    head, block = pl.program_id(0), pl.program_id(1)

    @pl.when((head == 0) & (block == 0))
    def _():
        plane = scal[0]
        for i in range(PLANE):
            dest = keys if i < 2 else values
            side = slice((i % 2) * HALF, (i % 2 + 1) * HALF)
            for j, piece in enumerate((p0, p1, p2, p3)):

                @pl.when(plane == (i ^ j))
                def _(dest=dest, side=side, piece=piece):
                    dest[:, side] = piece[...]

        front, back = keys[:, :HALF].astype(F32), keys[:, HALF:].astype(F32)
        keys[:, :HALF] = (front * cos[...] - back * sin[...]).astype(BF)
        keys[:, HALF:] = (back * cos[...] + front * sin[...]).astype(BF)

    rows = pl.ds(pl.multiple_of(scal[1] + block * QB, QB), QB)
    q_cos, q_sin = cos[rows, :], sin[rows, :]
    front, back = q_raw[:, :HALF], q_raw[:, HALF:]
    query = jnp.concatenate(
        [front * q_cos - back * q_sin, back * q_cos + front * q_sin], axis=1
    ).astype(BF)
    query = query * jnp.asarray(HD**-0.5, BF)
    q_out[...] = query
    positions, starts, low, high = query_bounds(scal, ndoc, block)

    def step(kb, carry):
        peak, total, mixed = carry
        span = pl.ds(pl.multiple_of(kb * KB, KB), KB)
        scores = dot_nt(query, keys[span, :])
        where = kb * KB + lax.broadcasted_iota(jnp.int32, (QB, KB), 1)
        scores = jnp.where((where <= positions) & (where >= starts), scores, masked)
        new_peak = jnp.maximum(peak, jnp.max(scores, axis=1, keepdims=True))
        weights = jnp.exp(scores - new_peak)
        keep = jnp.exp(peak - new_peak)
        total = total * keep + jnp.sum(weights, axis=1, keepdims=True)
        mixed = mixed * keep + dot_nn(weights.astype(BF), values[span, :])
        return new_peak, total, mixed

    peak, total, mixed = lax.fori_loop(
        low,
        high,
        step,
        (jnp.full((QB, 1), -3e38, F32), jnp.zeros((QB, 1), F32), jnp.zeros((QB, HD), F32)),
    )
    att[...] = (mixed / total).astype(BF)
    lse[...] = jnp.broadcast_to(peak + jnp.log(total), (QB, 128))


def attend(scal, query_raw, pieces, cos, sin):
    group, wide = query_raw.shape
    length = cos.shape[0]
    heads = wide // HD
    whole = pl.BlockSpec((length, HALF), lambda h, i, s: (0, 0))
    token = pl.BlockSpec((QB, HD), lambda h, i, s: (i, h))
    return pl.pallas_call(
        lambda *refs: attend_kernel(scal.shape[0] - 2, *refs),
        grid_spec=pltpu.PrefetchScalarGridSpec(
            num_scalar_prefetch=1,
            grid=(heads, group // QB),
            in_specs=[token] + [whole] * 6,
            out_specs=[
                token,
                token,
                pl.BlockSpec((QB, 128), lambda h, i, s: (i, h)),
                pl.BlockSpec((length, HD), lambda h, i, s: (0, 0)),
                pl.BlockSpec((length, HD), lambda h, i, s: (0, 0)),
            ],
        ),
        out_shape=[
            jax.ShapeDtypeStruct((group, wide), BF),
            jax.ShapeDtypeStruct((group, wide), BF),
            jax.ShapeDtypeStruct((group, heads * 128), F32),
            jax.ShapeDtypeStruct((length, HD), BF),
            jax.ShapeDtypeStruct((length, HD), BF),
        ],
        compiler_params=params(),
        cost_estimate=pl.CostEstimate(
            flops=4 * group * wide * length, bytes_accessed=8 << 20, transcendentals=0
        ),
        name="attend",
    )(scal, query_raw, *pieces, cos, sin)


def attend_back_kernel(
    ndoc, scal, query, keys, values, lse, att, d_att, cos, sin, dep, d_raw, parts, d_keys, d_values
):
    head, block = pl.program_id(0), pl.program_id(1)

    @pl.when((head == 0) & (block == 0))
    def _():
        d_keys[...] = jnp.zeros_like(d_keys)
        d_values[...] = jnp.zeros_like(d_values)

    positions, starts, low, high = query_bounds(scal, ndoc, block)
    peak = lse[:, :1]
    grad = d_att[...]
    shared = jnp.sum(grad.astype(F32) * att[...].astype(F32), axis=1, keepdims=True)

    def step(kb, d_query):
        span = pl.ds(pl.multiple_of(kb * KB, KB), KB)
        key, value = keys[span, :], values[span, :]
        scores = dot_nt(query[...], key)
        where = kb * KB + lax.broadcasted_iota(jnp.int32, (QB, KB), 1)
        scores = jnp.where((where <= positions) & (where >= starts), scores, masked)
        probs = jnp.exp(scores - peak)
        d_probs = dot_nt(grad, value)
        d_scores = (probs * (d_probs - shared)).astype(BF)
        d_keys[span, :] += dot_tn(d_scores, query[...])
        d_values[span, :] += dot_tn(probs.astype(BF), grad)
        return d_query + dot_nn(d_scores, key)

    d_query = lax.fori_loop(low, high, step, jnp.zeros((QB, HD), F32)) * HD**-0.5
    rows = pl.ds(pl.multiple_of(scal[1] + block * QB, QB), QB)
    q_cos, q_sin = cos[rows, :], sin[rows, :]
    front, back = d_query[:, :HALF], d_query[:, HALF:]
    d_raw[:, :HALF] = (front * q_cos + back * q_sin).astype(BF)
    d_raw[:, HALF:] = (back * q_cos - front * q_sin).astype(BF)

    @pl.when((head == pl.num_programs(0) - 1) & (block == pl.num_programs(1) - 1))
    def _():
        plane = scal[0]
        front, back = d_keys[:, :HALF], d_keys[:, HALF:]
        parts[plane] = (front * cos[...] + back * sin[...]).astype(BF)
        parts[plane ^ 1] = (back * cos[...] - front * sin[...]).astype(BF)
        parts[plane ^ 2] = d_values[:, :HALF].astype(BF)
        parts[plane ^ 3] = d_values[:, HALF:].astype(BF)


def attend_back(scal, query, keys, values, lse, att, d_att, cos, sin, dep):
    group, wide = query.shape
    length = cos.shape[0]
    heads = wide // HD
    token = pl.BlockSpec((QB, HD), lambda h, i, s: (i, h))
    table = pl.BlockSpec((length, HALF), lambda h, i, s: (0, 0))
    whole = pl.BlockSpec((length, HD), lambda h, i, s: (0, 0))
    return pl.pallas_call(
        lambda *refs: attend_back_kernel(scal.shape[0] - 2, *refs),
        grid_spec=pltpu.PrefetchScalarGridSpec(
            num_scalar_prefetch=1,
            grid=(heads, group // QB),
            in_specs=[token, whole, whole, pl.BlockSpec((QB, 128), lambda h, i, s: (i, h))]
            + [token, token, table, table, pl.BlockSpec(memory_space=pl.ANY)],
            out_specs=[token, pl.BlockSpec((PLANE, length, HALF), lambda h, i, s: (0, 0, 0))],
            scratch_shapes=[pltpu.VMEM((length, HD), F32), pltpu.VMEM((length, HD), F32)],
        ),
        out_shape=[
            jax.ShapeDtypeStruct((group, wide), BF),
            jax.ShapeDtypeStruct((PLANE, length, HALF), BF),
        ],
        compiler_params=params(),
        cost_estimate=pl.CostEstimate(
            flops=10 * group * wide * length, bytes_accessed=12 << 20, transcendentals=0
        ),
        name="attend_back",
    )(scal, query, keys, values, lse, att, d_att, cos, sin, dep)


def ffn_kernel(chunk, count, blocks, slots, *refs):
    h_refs, dy_ref, w_ref, refs = refs[:count], refs[count], refs[count + 1], refs[count + 2 :]
    if chunk:
        refs = refs[3:]
    acts, h_all, dy_all = refs[:3]
    d_h, out = refs[3 : 3 + count], refs[3 + count : 3 + 2 * count]
    gate_up, down, sems, dy_sems = refs[3 + 2 * count :]
    units = down.shape[1]
    own = units // PLANE
    rows = h_refs[0].shape[0]
    copies = []
    for block in range(blocks):
        for k in range(PLANE):
            at = block * PLANE + k
            for part in range(3):
                source = w_ref.at[pl.ds((3 * at + part) * own, own)]
                if part < 2:
                    dest = gate_up.at[block, pl.ds(part * units + k * own, own)]
                else:
                    dest = down.at[block, pl.ds(k * own, own)]
                copies.append((part, pltpu.make_async_copy(source, dest, sems.at[at, part])))
    for k in range(count):
        source = dy_ref.at[pl.ds(pl.multiple_of(slots[k] * rows, rows), rows)]
        dest = dy_all.at[pl.ds(k * rows, rows)]
        copies.append((2, pltpu.make_async_copy(source, dest, dy_sems.at[k])))
    for part in range(3):
        for kind, copy in copies:
            if kind == part:
                copy.start()
    for k in range(count):
        h_all[k * rows : (k + 1) * rows, :] = h_refs[k][...]
    feat = h_all.shape[1] // blocks

    def cols(ref, k):
        return ref[:, k * feat : (k + 1) * feat]

    def wait(part):
        for kind, copy in copies:
            if kind == part:
                copy.wait()

    wait(0)
    gate = sum(dot_nt(cols(h_all, k), gate_up[k, :units, :]) for k in range(blocks))
    wait(1)
    up = sum(dot_nt(cols(h_all, k), gate_up[k, units:, :]) for k in range(blocks))
    sig = 1.0 / (1.0 + jnp.exp(-gate))
    silu = gate * sig
    hid = (silu * up).astype(BF)
    acts[2] = hid
    wait(2)
    d_hidden = sum(dot_nt(cols(dy_all, k), down[k]) for k in range(blocks))
    d_gate = (d_hidden * up * (sig + silu * (1.0 - sig))).astype(BF)
    d_up = (d_hidden * silu).astype(BF)
    acts[0] = d_gate
    acts[1] = d_up
    for k in range(blocks):
        span = slice(k * feat, (k + 1) * feat)
        grad = dot_nn(d_gate, gate_up[k, :units, :]) + dot_nn(d_up, gate_up[k, units:, :])
        result = dot_nn(hid, down[k])
        for j in range(count):
            d_h[j][:, span] = grad[j * rows : (j + 1) * rows].astype(BF)
            out[j][:, span] = result[j * rows : (j + 1) * rows].astype(BF)


def feed_forward(chunk, chunks, slots, h, dy, weights, held):
    count = len(h)
    rows, width = h[0].shape
    feat = weights.shape[1]
    blocks = width // feat
    units = weights.shape[0] // blocks // 3
    total = rows * count
    whole = pl.BlockSpec((rows, width), lambda i, s: (0, 0))
    anywhere = pl.BlockSpec(memory_space=pl.ANY)
    return pl.pallas_call(
        lambda *refs: ffn_kernel(chunk, count, blocks, *refs),
        grid_spec=pltpu.PrefetchScalarGridSpec(
            num_scalar_prefetch=1,
            grid=(1,),
            in_specs=[whole] * count + [anywhere] * (2 + len(held)),
            out_specs=[pl.BlockSpec((3, total, units), lambda i, s: (0, chunk, 0))]
            + [pl.BlockSpec((total, width), lambda i, s: (chunk, 0))] * 2
            + [whole] * (2 * count),
            scratch_shapes=[
                pltpu.VMEM((blocks, 2 * units, feat), BF),
                pltpu.VMEM((blocks, units, feat), BF),
                pltpu.SemaphoreType.DMA((blocks * PLANE, 3)),
                pltpu.SemaphoreType.DMA((count,)),
            ],
        ),
        out_shape=[jax.ShapeDtypeStruct((3, total * chunks, units), BF)]
        + [jax.ShapeDtypeStruct((total * chunks, width), BF)] * 2
        + [jax.ShapeDtypeStruct((rows, width), BF)] * (2 * count),
        input_output_aliases={3 + count + i: i for i in range(len(held))},
        compiler_params=params(),
        cost_estimate=pl.CostEstimate(
            flops=12 * total * width * units, bytes_accessed=24 << 20, transcendentals=0
        ),
        name="feed_forward",
    )(slots, *h, dy, weights, *held)


def ffn_gradient(acts, h, dy, blocks, dep):
    count, width = h.shape
    units = acts.shape[2]
    feat = width // blocks

    def kernel(left, h_ref, dy_ref, dep_ref, out):
        def store(right):
            result = dot_tn(left[0], right).astype(BF)
            for k in range(PLANE):
                out[0, k, 0] = result[k * (units // PLANE) : (k + 1) * (units // PLANE)]

        part = pl.program_id(1)

        @pl.when(part < 2)
        def _():
            store(h_ref[...])

        @pl.when(part == 2)
        def _():
            store(dy_ref[...])

    right = pl.BlockSpec((count, feat), lambda k, part: (0, k))
    out = pl.pallas_call(
        kernel,
        grid=(blocks, 3),
        in_specs=[pl.BlockSpec((1, count, units), lambda k, part: (part, 0, 0)), right, right]
        + [pl.BlockSpec(memory_space=pl.ANY)],
        out_specs=pl.BlockSpec(
            (1, PLANE, 1, units // PLANE, feat), lambda k, part: (k, 0, part, 0, 0)
        ),
        out_shape=jax.ShapeDtypeStruct((blocks, PLANE, 3, units // PLANE, feat), BF),
        compiler_params=params(),
        cost_estimate=pl.CostEstimate(
            flops=6 * count * width * units, bytes_accessed=24 << 20, transcendentals=0
        ),
        name="ffn_gradient",
    )(acts, h, dy, dep)
    return out.reshape(-1, feat)


def shards(
    tokens,
    out_grad,
    doc_lengths,
    norm_attn,
    w_qdown,
    norm_query,
    w_qup,
    w_key,
    w_value,
    w_out,
    norm_ffn,
    w_gate,
    w_up,
    w_down,
):
    rows, rings = lax.axis_size("rows"), lax.axis_size("ring")
    devices = rows * rings * PLANE
    row = lax.axis_index("rows")
    ring = lax.axis_index("ring")
    plane = lax.axis_index("py") * 2 + lax.axis_index("px")
    spot = (row, ring, plane)
    own_tokens = tokens[0]
    count_local, width = own_tokens.shape
    group = count_local * PLANE
    row_length = group * rings

    latent_width = w_qdown.shape[1] // PLANE
    kv_width = 2 * HD // PLANE
    kv_w = jnp.concatenate([w_key, w_value], axis=1)
    down_w = jnp.concatenate(
        [
            piece
            for i in range(PLANE)
            for piece in (
                w_qdown[:, i * latent_width : (i + 1) * latent_width],
                kv_w[:, i * kv_width : (i + 1) * kv_width],
            )
        ],
        axis=1,
    )
    part_a, part_q = norm_attn.shape[0], norm_query.shape[0]
    gains = jnp.concatenate([norm_attn, norm_query, norm_ffn])
    gain_count = gains.shape[0]
    lanes = latent_width + kv_width
    gains = jnp.tile(jnp.pad(gains, (0, lanes - gain_count)), PLANE)
    gains = jnp.pad(gains[None], ((0, EXTRA - 1), (0, 0)))
    block_rows = down_w.shape[0]
    hidden_axes = ("rows", "py", "px")
    ffn_w = jnp.concatenate([jnp.transpose(w_gate), jnp.transpose(w_up), w_down])
    ffn_w = lax.all_gather(ffn_w, hidden_axes, axis=0, tiled=True)

    down_w = column_swap(jnp.concatenate([down_w, gains]), plane)
    token_blocks = plane_spread(own_tokens)
    down_ring = ring_spread(down_w, "ring")
    other_w = column_swap(jnp.concatenate([w_qup, jnp.transpose(w_out)]), plane)
    other_w = other_w.reshape(PLANE, -1, other_w.shape[1])
    up_rows = w_qup.shape[0]
    up_query = other_w[:, :up_rows].reshape(-1, other_w.shape[2])
    out_proj = other_w[:, up_rows:].reshape(-1, other_w.shape[2])
    up_query, *down_ring = tie(up_query, *down_ring)
    up_ring = ring_gather(up_query, "ring")
    out_proj, *up_ring = tie(out_proj, *up_ring)
    out_proj = rows_place(ring_gather(out_proj, "ring"), row, ring)
    up_query = rows_place(up_ring, row, ring)
    upstream = out_grad[0]
    ring_upstream, ffn_w = tie(upstream, ffn_w)
    ring_upstream = lax.all_gather(ring_upstream, "ring", axis=0, tiled=True)
    down_w, gains = rows_place(down_ring, row, ring, block_rows)
    down_w = down_w.reshape(-1, lanes)
    gains = gains[:, 0, :gain_count].astype(F32)
    gain_attn = gains[:, :part_a].reshape(-1)
    gain_query = gains[:, part_a : part_a + part_q].reshape(-1)
    gain_ffn = gains[:, part_a + part_q :].reshape(-1)

    key_positions = jnp.arange(row_length, dtype=jnp.int32)
    key_relative = doc_layout(doc_lengths[0], key_positions)[1]
    key_cos, key_sin = rope_tables(key_relative, HD // 2)
    scal = jnp.concatenate([jnp.stack([plane, ring * group]), doc_lengths[0]]).astype(jnp.int32)

    group_tokens = plane_place(token_blocks, plane).astype(F32)
    normed = rms_norm(group_tokens, gain_attn).astype(BF)
    projected = mm(normed, down_w).astype(BF)

    key_value = ring_gather(projected[:, latent_width:], "ring")
    latent = plane_spread(projected[:, :latent_width])
    key_value, *latent = tie(ring_place(key_value, ring), *latent)
    latent = jnp.stack(latent)
    latent = jnp.concatenate([pick(latent, plane ^ i) for i in range(PLANE)], axis=1).astype(F32)
    latent_normed = rms_norm(latent, gain_query).astype(BF)
    query_raw = mm(latent_normed, up_query)

    key_value = plane_spread(key_value)
    attended, queries, log_total, all_keys, all_values = attend(
        scal, query_raw, key_value, key_cos, key_sin
    )
    branch = mm_nt(attended, out_proj)
    branch = plane_sum([block_of(branch, plane ^ k, count_local) for k in range(PLANE)])
    middle = own_tokens.astype(F32) + branch

    normed2_f, pull_ffn_norm = jax.vjp(rms_norm, middle, gain_ffn)
    normed_ffn = normed2_f.astype(BF)
    chunk = 2
    chunks = rings // chunk
    held = []
    grad_parts, out_parts = [], []
    ring_normed = [normed_ffn]
    for k in range(1, rings):
        last = ring_normed[-1]
        if k > 1 and k % chunk == chunk - 1:
            last, *held = tie(last, *held)
        ring_normed.append(shift(last, "ring"))
        if k % chunk != chunk - 1:
            continue
        some = slice(k - chunk + 1, k + 1)
        slots = (ring - jnp.arange(k - chunk + 1, k + 1)) % rings
        results = feed_forward(
            k // chunk, chunks, slots, ring_normed[some], ring_upstream, ffn_w, held
        )
        held = results[:3]
        grad_parts += results[3 : 3 + chunk]
        out_parts += results[3 + chunk :]
    grad_normed_ffn, _ = ring_scatter_bf(grad_parts)
    grad_normed_ffn, *out_parts = tie(grad_normed_ffn, *out_parts)
    out_total = out_parts[1]
    for k in range(2, rings):
        out_total = shift(out_total, "ring").astype(F32) + out_parts[k].astype(F32)
        out_total = out_total.astype(BF)
    output = shift(out_total, "ring").astype(F32) + out_parts[0].astype(F32)

    upstream_f = upstream.astype(F32)
    grad_middle_norm, grad_gain_ffn = pull_ffn_norm(grad_normed_ffn)
    grad_middle = upstream_f + grad_middle_norm

    branch_grad = grad_middle.astype(BF)
    branch_blocks = plane_spread(branch_grad)
    ffn_grad = ffn_gradient(*held, rows, token_of(branch_grad))
    ffn_grad = lax.psum_scatter(ffn_grad, hidden_axes, scatter_dimension=0, tiled=True)
    branch_grad = plane_place(branch_blocks, plane)
    grad_attended = mm(branch_grad, out_proj).astype(BF)
    out_block = row_blocks(branch_grad, attended, spot)
    grad_query_raw, kv_parts = attend_back(
        scal,
        queries,
        all_keys,
        all_values,
        log_total,
        attended,
        grad_attended,
        key_cos,
        key_sin,
        out_total,
    )
    grad_out_w = over_rows(out_block)
    kv_parts, output = tie(kv_parts, output)
    grad_out_w, output = tie(grad_out_w, output)
    grad_out_w, _ = over_ring(grad_out_w, spot)
    output = middle + output
    kv_grad = plane_sum([kv_parts[k] for k in range(PLANE)]).astype(BF)
    grad_latent_normed = mm_nt(grad_query_raw, up_query)
    grad_latent_normed, kv_grad = tie(grad_latent_normed, kv_grad)
    kv_grad = ring_scatter(
        [block_of(kv_grad, (ring - k) % rings, group).astype(F32) for k in range(rings)], "ring"
    )
    grad_up_query = over_rows(row_blocks(latent_normed, grad_query_raw, spot))
    grad_up_query, _ = over_ring(grad_up_query, spot)
    grad_latent_normed = plane_sum(
        [block_of(grad_latent_normed, plane ^ k, count_local) for k in range(PLANE)]
    )
    own_latent = block_of(latent, plane, count_local)
    pull_latent = jax.vjp(rms_norm, own_latent, gain_query)[1]
    grad_latent, grad_gain_query = pull_latent(grad_latent_normed)
    grad_latent = grad_latent.astype(BF)
    grad_latent = plane_swap(
        [block_of(grad_latent, plane ^ k, latent_width, 1) for k in range(PLANE)]
    )
    grad_latent = place([(g, plane ^ k) for k, g in enumerate(grad_latent)], PLANE)
    grad_projected = jnp.concatenate([grad_latent, kv_grad.astype(BF)], axis=1)
    grad_projected, grad_out_w, grad_up_query = tie(grad_projected, grad_out_w, grad_up_query)
    grad_normed = mm_nt(grad_projected, down_w)
    pull_attn_norm = jax.vjp(rms_norm, own_tokens.astype(F32), gain_attn)[1]
    scale = lax.rsqrt(jnp.mean(group_tokens * group_tokens, axis=-1, keepdims=True) + epsilon)
    grad_gain_attn = jnp.sum(grad_normed * group_tokens * scale, axis=0)
    gain_grads = jnp.concatenate(
        [g.reshape(devices, -1) for g in (grad_gain_attn, grad_gain_query, grad_gain_ffn)], axis=1
    )
    gain_grads = jnp.pad(gain_grads[:, None], ((0, 0), (0, EXTRA - 1), (0, lanes - gain_count)))
    gain_grads = gain_grads.reshape(rows, rings * PLANE, EXTRA, lanes)
    grad_down = over_rows(row_blocks(normed, grad_projected, spot, gain_grads))
    grad_down, (grad_up_query, grad_out_w) = over_ring(
        grad_down, spot, (grad_up_query, grad_out_w)
    )
    grad_up_query = beside(over_plane(grad_up_query, spot)).astype(F32)
    grad_out_w = jnp.transpose(beside(over_plane(grad_out_w, spot)).astype(F32))
    grad_down = over_plane(grad_down, spot)
    grad_down = grad_down.reshape(PLANE, -1, grad_down.shape[1]).astype(F32)
    grad_gains = jnp.sum(grad_down[:, block_rows, :gain_count], axis=0)
    grad_down = grad_down[:, :block_rows]
    grad_down_query = jnp.concatenate([p[:, :latent_width] for p in grad_down], axis=1)
    grad_kv_w = jnp.concatenate([p[:, latent_width:] for p in grad_down], axis=1)
    grad_normed = plane_sum(
        [block_of(grad_normed, plane ^ k, count_local) for k in range(PLANE)]
    )
    grad_input = grad_middle + pull_attn_norm(grad_normed)[0]
    ffn_grad = ffn_grad.astype(F32).reshape(3, -1, ffn_grad.shape[1])
    gate_grad, up_grad, down_grad = jnp.transpose(ffn_grad[0]), jnp.transpose(ffn_grad[1]), ffn_grad[2]

    return (
        output.astype(BF)[None],
        grad_input.astype(BF)[None],
        grad_gains[:part_a],
        grad_down_query,
        grad_gains[part_a : part_a + part_q],
        grad_up_query,
        grad_kv_w[:, :HD],
        grad_kv_w[:, HD:],
        grad_out_w,
        grad_gains[part_a + part_q :],
        gate_grad,
        up_grad,
        down_grad,
    )


def beside(stacked):
    blocks = stacked.reshape(PLANE, -1, stacked.shape[1])
    return jnp.concatenate(list(blocks), axis=1)


def solution(mesh):
    rows = mesh.shape["rows"]
    chips = mesh.shape["seq"]
    inner = Mesh(
        np.asarray(mesh.devices).reshape(rows, chips // PLANE, 2, 2), ("rows", "ring", "py", "px")
    )
    seq = ("ring", "py", "px")
    every = ("rows",) + seq
    placed = (
        P("rows", seq, None),
        P("rows", seq, None),
        P("rows", None),
        P(every),
        P(every, None),
        P(every),
        P(every, None),
        P(every, None),
        P(every, None),
        P(None, every),
        P(every),
        P("rows", seq),
        P("rows", seq),
        P(seq, "rows"),
    )
    return jax.shard_map(
        shards,
        mesh=inner,
        in_specs=placed,
        out_specs=(
            P("rows", seq, None),
            P("rows", seq, None),
            P(every),
            P(every, None),
            P(every),
            P(every, None),
            P(every, None),
            P(every, None),
            P(None, every),
            P(every),
            P("rows", seq),
            P("rows", seq),
            P(seq, "rows"),
        ),
        check_vma=False,
    )
```

time: 741 us -> 637 us (0.86)
  starting transfers between devices: 160 us -> 76 us
  Pallas kernels: 75.8 us -> 125 us
  other arithmetic: 83.2 us -> 54.3 us
  waiting for transfers between devices: 311 us -> 283 us
  local copies, waits for them, and re-layouts: 51.6 us -> 39 us
  between operations: 3.82 us -> 15.9 us
  matrix products: 43.3 us -> 33.5 us
    ppermute x54 -> x40, waiting for transfers between devices: 201 us -> 137 us  [shift(): lax.ppermute(value, axis, [(i, (i + by) % count) for i in range(count)])]
    ppermute x78 -> x28, starting transfers between devices: 86.4 us -> 30 us  [flip(): return lax.ppermute(value, 'px' if by == 1 else 'py', [(0, 1), (1, 0)])]
    pallas_call x2 -> x18, Pallas kernels: 48 us -> 97.9 us  [the longest x15 45.9 us: place(): pl.pallas_call(kernel, grid_spec=pltpu.PrefetchScalarGridSpec(num_scalar_...]
    ppermute x54 -> x40, starting transfers between devices: 63.2 us -> 23.8 us  [shift(): lax.ppermute(value, axis, [(i, (i + by) % count) for i in range(count)])]
    ppermute x9 -> x14, waiting for transfers between devices: 13.3 us -> 48.1 us  [flip(): return lax.ppermute(value, ('py', 'px'), [(i, i ^ 3) for i in range(PLANE)])]
    concatenate x17 -> x7, other arithmetic: 23.6 us -> 4.27 us  [the longest x1 3.16 us: shards(): jnp.concatenate([jnp.transpose(w_gate), jnp.transpose(w_up), w_down])]
    dot_general x7 -> x6, matrix products: 27.6 us -> 13.5 us  [mm_tn(): return jnp.einsum('ki,kj->ij', left, right, preferred_element_type=F32)]
    ppermute x9 -> x14, starting transfers between devices: 10.7 us -> 21.6 us  [flip(): return lax.ppermute(value, ('py', 'px'), [(i, i ^ 3) for i in range(PLANE)])]
  transfers between devices with their start and end apart: 141 -> 85, of which waited for: 66 -> 43; matrix products, arithmetic and copies ran while one was open for 23% -> 15% of each run, Pallas kernels for 7% -> 17%
where the time goes in v3:
time: 637 us; the launch traced here: 627 us
  waiting for transfers between devices  283 us (44%)
  Pallas kernels  125 us (20%)
  starting transfers between devices  76 us (12%)
  other arithmetic  54.3 us (9%)
  local copies, waits for them, and re-layouts  39 us (6%)
  matrix products  33.5 us (5%)
  between operations  15.9 us (2%)
    ppermute x40, waiting for transfers between devices, shift(): lax.ppermute(value, axis, [(i, (i + by) % count) for i in range(count)])  137 us
    ppermute x28, waiting for transfers between devices, flip(): return lax.ppermute(value, 'px' if by == 1 else 'py', [(0, 1), (1, 0)])  97.4 us
    ppermute x14, waiting for transfers between devices, flip(): return lax.ppermute(value, ('py', 'px'), [(i, i ^ 3) for i in range(PLANE)])  48.1 us
    pallas_call x15, Pallas kernels, place(): pl.pallas_call(kernel, grid_spec=pltpu.PrefetchScalarGridSpec(num_scalar_...  45.9 us
    pallas_call x2, Pallas kernels, feed_forward(): pl.pallas_call(lambda *refs: ffn_kernel(chunk, count, blocks, *refs), gri...  36 us
    ppermute x28, starting transfers between devices, flip(): return lax.ppermute(value, 'px' if by == 1 else 'py', [(0, 1), (1, 0)])  30 us
    ppermute x40, starting transfers between devices, shift(): lax.ppermute(value, axis, [(i, (i + by) % count) for i in range(count)])  23.8 us
    ppermute x14, starting transfers between devices, flip(): return lax.ppermute(value, ('py', 'px'), [(i, i ^ 3) for i in range(PLANE)])  21.6 us
  transfers between devices with their start and end apart: 85, of which 43 were waited for; matrix products, arithmetic and copies ran while one was open for 15% of the time, Pallas kernels for 17%

profile of v3, /device:TPU:0, one launch (start us, length us, event | category | flops | bytes accessed | tf_op | source)
XLA Modules:
  0.0 626.6 jit_solution(4457857692193819761)
XLA Ops:
  35.4 11.7 %collective-permute-done.4 = bf16[96,1024]{1,0:T(8,128)(2,1)S(1)} collective-permute-done((bf16[96,1024]{1,0:T(8,128)(2,1)S(1)}, bf16[96,1024]{1,0:T(8,128)(2,1)S(1)}, u32[]{:S(2)}, u32[]{:S(2)}) %collective-permute-start.4) | collective-permute-done | bytes 196640 | tf_op jit(solution)/shard_map/ppermute | solution.py:78
  64.8 14.9 %collective-permute-done.1 = bf16[128,2048]{1,0:T(8,128)(2,1)S(1)} collective-permute-done((bf16[128,2048]{1,0:T(8,128)(2,1)S(1)}, bf16[128,2048]{1,0:T(8,128)(2,1)S(1)}, u32[]{:S(2)}, u32[]{:S(2)}) %collective-permute-start.1) | collective-permute-done | bytes 524320 | tf_op jit(solution)/shard_map/ppermute | solution.py:78
  88.9 4.4 collective-permute-done.21
  100.3 6.7 %collective-permute-done.26 = bf16[256,1024]{1,0:T(8,128)(2,1)S(1)} collective-permute-done((bf16[256,1024]{1,0:T(8,128)(2,1)S(1)}, bf16[256,1024]{1,0:T(8,128)(2,1)S(1)}, u32[]{:S(2)}, u32[]{:S(2)}) %collective-permute-start.26) | collective-permute-done | bytes 524320 | tf_op jit(solution)/shard_map/ppermute | solution.py:54
  109.0 12.7 %collective-permute-done.27 = bf16[256,1024]{1,0:T(8,128)(2,1)} collective-permute-done((bf16[256,1024]{1,0:T(8,128)(2,1)S(1)}, bf16[256,1024]{1,0:T(8,128)(2,1)}, u32[]{:S(2)}, u32[]{:S(2)}) %collective-permute-start.27) | collective-permute-done | bytes 524320 | tf_op jit(solution)/shard_map/ppermute | solution.py:54
  124.7 12.1 %collective-permute-done.14 = bf16[512,128]{1,0:T(8,128)(2,1)} collective-permute-done((bf16[512,128]{1,0:T(8,128)(2,1)S(1)}, bf16[512,128]{1,0:T(8,128)(2,1)}, u32[]{:S(2)}, u32[]{:S(2)}) %collective-permute-start.14) | collective-permute-done | bytes 131104 | tf_op jit(solution)/shard_map/ppermute | solution.py:54
  147.0 5.5 multiply_sine_fusion
  171.0 12.0 %collective-permute-done.24.refs_4_ = bf16[2048,128]{1,0:T(8,128)(2,1)} collective-permute-done((bf16[2048,128]{1,0:T(8,128)(2,1)}, bf16[2048,128]{1,0:T(8,128)(2,1)}, u32[]{:S(2)}, u32[]{:S(2)}) %collective-permute-start.24) | collective-permute-done | bytes 524320 | tf_op jit(solution)/shard_map/ppermute | solution.py:78
  183.0 12.7 %attend.1 = (bf16[512,1024]{1,0:T(8,128)(2,1)}, bf16[512,1024]{1,0:T(8,128)(2,1)}, f32[512,512]{1,0:T(8,128)}, bf16[2048,256]{1,0:T(8,128)(2,1)}, bf16[2048,256]{1,0:T(8,128)(2,1)}) custom-call(s32[4]{0:T(128)} %pad_add_fusion.refs_0_, f32[512,1024]{1,0:T(8,128)} %fusion.62.refs_1_, bf16[2048,128]{1,0:T(8,128)(2,1)} %bitcast.258, ...), custom_call_target="tpu_custom_call" | custom-call | flops 4294967296 | bytes 8388608 | tf_op jit(solution)/shard_map/attend/pallas_call | solution.py:329
  195.7 5.1 place.24
  200.8 4.6 fusion.63
  212.1 12.5 %collective-permute-done.32 = bf16[128,2048]{1,0:T(8,128)(2,1)S(1)} collective-permute-done((bf16[128,2048]{1,0:T(8,128)(2,1)}, bf16[128,2048]{1,0:T(8,128)(2,1)S(1)}, u32[]{:S(2)}, u32[]{:S(2)}) %collective-permute-start.32) | collective-permute-done | bytes 524320 | tf_op jit(solution)/shard_map/ppermute | solution.py:77
  224.6 9.5 %collective-permute-done.31 = bf16[128,2048]{1,0:T(8,128)(2,1)S(1)} collective-permute-done((bf16[128,2048]{1,0:T(8,128)(2,1)}, bf16[128,2048]{1,0:T(8,128)(2,1)S(1)}, u32[]{:S(2)}, u32[]{:S(2)}) %collective-permute-start.31) | collective-permute-done | bytes 524320 | tf_op jit(solution)/shard_map/ppermute | solution.py:78
  241.3 16.6 %collective-permute-done.33.refs_2_ = bf16[128,2048]{1,0:T(8,128)(2,1)} collective-permute-done((bf16[128,2048]{1,0:T(8,128)(2,1)S(1)}, bf16[128,2048]{1,0:T(8,128)(2,1)}, u32[]{:S(2)}, u32[]{:S(2)}) %collective-permute-start.33) | collective-permute-done | bytes 524320 | tf_op jit(solution)/shard_map/ppermute | solution.py:54
  258.1 18.0 %feed_forward.2 = (bf16[3,512,1408]{2,1,0:T(8,128)(2,1)}, bf16[512,2048]{1,0:T(8,128)(2,1)}, bf16[512,2048]{1,0:T(8,128)(2,1)}, bf16[128,2048]{1,0:T(8,128)(2,1)...) custom-call(s32[2]{0:T(128)} %and_select_fusion.1.refs_0_, ...), custom_call_target="tpu_custom_call" | custom-call | flops 8858370048 | bytes 25165824 | tf_op jit(solution)/shard_map/feed_forward/pallas_call | solution.py:505
  279.7 13.3 %collective-permute-done.36.refs_2_ = bf16[128,2048]{1,0:T(8,128)(2,1)S(1)} collective-permute-done((bf16[128,2048]{1,0:T(8,128)(2,1)}, bf16[128,2048]{1,0:T(8,128)(2,1)S(1)}, u32[]{:S(2)}, u32[]{:S(2)}) %collective-permute-start.36) | collective-permute-done | bytes 524320 | tf_op jit(solution)/shard_map/ppermute | solution.py:54
  293.8 18.0 %feed_forward.3 = (bf16[3,512,1408]{2,1,0:T(8,128)(2,1)}, bf16[512,2048]{1,0:T(8,128)(2,1)}, bf16[512,2048]{1,0:T(8,128)(2,1)}, bf16[128,2048]{1,0:T(8,128)(2,1)...) custom-call(s32[2]{0:T(128)} %and_select_fusion.refs_0_, ...), custom_call_target="tpu_custom_call", output_to_operand_aliasing={{0}: (5, {}), {1}: (6, {}), {2}: (7, {})} | custom-call | flops 8858370048 | bytes 25165824 | tf_op jit(solution)/shard_map/feed_forward/pallas_call | solution.py:505
  313.1 11.8 %collective-permute-done.37 = bf16[128,2048]{1,0:T(8,128)(2,1)S(1)} collective-permute-done((bf16[128,2048]{1,0:T(8,128)(2,1)S(1)}, bf16[128,2048]{1,0:T(8,128)(2,1)S(1)}, u32[]{:S(2)}, u32[]{:S(2)}) %collective-permute-start.37) | collective-permute-done | bytes 524320 | tf_op jit(solution)/shard_map/ppermute | solution.py:54
  326.4 11.0 %collective-permute-done.38 = bf16[128,2048]{1,0:T(8,128)(2,1)S(1)} collective-permute-done((bf16[128,2048]{1,0:T(8,128)(2,1)S(1)}, bf16[128,2048]{1,0:T(8,128)(2,1)S(1)}, u32[]{:S(2)}, u32[]{:S(2)}) %collective-permute-start.38) | collective-permute-done | bytes 524320 | tf_op jit(solution)/shard_map/ppermute | solution.py:54
  341.4 16.0 %ffn_gradient.1 = bf16[2,4,3,352,1024]{4,3,2,1,0:T(8,128)(2,1)} custom-call(bf16[3,512,1408]{2,1,0:T(8,128)(2,1)} %get-tuple-element.132.left, bf16[512,2048]{1,0:T(8,128)(2,1)} %get-tuple-element.133.h_ref, bf16[512,2048]{1,0:T(8,128)(2,1)} %get-tuple-element.134.dy_ref, bf16[8,128]{1,0:T(8,128)(2,1)} %copy-done.96), custom_call_target="tpu_custom_call" | custom-call | flops 8858370048 | bytes 25165824 | tf_op jit(solution)/shard_map/ffn_gradient/pallas_call | solution.py:555
  364.2 9.4 %collective-permute-done.43 = bf16[128,2048]{1,0:T(8,128)(2,1)} collective-permute-done((bf16[128,2048]{1,0:T(8,128)(2,1)}, bf16[128,2048]{1,0:T(8,128)(2,1)}, u32[]{:S(2)}, u32[]{:S(2)}) %collective-permute-start.43) | collective-permute-done | bytes 524320 | tf_op jit(solution)/shard_map/ppermute | solution.py:54
  375.0 8.6 %collective-permute-done.40 = bf16[128,2048]{1,0:T(8,128)(2,1)S(1)} collective-permute-done((bf16[128,2048]{1,0:T(8,128)(2,1)}, bf16[128,2048]{1,0:T(8,128)(2,1)S(1)}, u32[]{:S(2)}, u32[]{:S(2)}) %collective-permute-start.40) | collective-permute-done | bytes 524320 | tf_op jit(solution)/shard_map/ppermute | solution.py:78
  396.5 14.3 %attend_back.1 = (bf16[512,1024]{1,0:T(8,128)(2,1)}, bf16[4,2048,128]{2,1,0:T(8,128)(2,1)}) custom-call(s32[4]{0:T(128)} %pad_add_fusion.refs_0_, bf16[512,1024]{1,0:T(8,128)(2,1)} %get-tuple-element.110.refs_1_, bf16[2048,256]{1,0:T(8,128)(2,1)} %get-tuple-element.111.refs_2_, bf16[2048,256]{1,0:T(8,128)(2,1)} %get-tuple-element.112.refs_3_, ...), custom_call_target="tpu_custom_call" | custom-call | flops 10737418240 | bytes 12582912 | tf_op jit(solution)/shard_map/attend_back/pallas_call | solution.py:410
  424.6 19.3 %collective-permute-done.48 = bf16[2048,128]{1,0:T(8,128)(2,1)} collective-permute-done((bf16[2048,128]{1,0:T(8,128)(2,1)}, bf16[2048,128]{1,0:T(8,128)(2,1)}, u32[]{:S(2)}, u32[]{:S(2)}) %collective-permute-start.48) | collective-permute-done | bytes 524320 | tf_op jit(solution)/shard_map/ppermute | solution.py:77
  443.9 11.0 %collective-permute-done.47 = bf16[2048,128]{1,0:T(8,128)(2,1)} collective-permute-done((bf16[2048,128]{1,0:T(8,128)(2,1)}, bf16[2048,128]{1,0:T(8,128)(2,1)}, u32[]{:S(2)}, u32[]{:S(2)}) %collective-permute-start.47) | collective-permute-done | bytes 524320 | tf_op jit(solution)/shard_map/ppermute | solution.py:78
  454.9 7.3 %collective-permute-done.46 = bf16[2048,128]{1,0:T(8,128)(2,1)} collective-permute-done((bf16[2048,128]{1,0:T(8,128)(2,1)}, bf16[2048,128]{1,0:T(8,128)(2,1)}, u32[]{:S(2)}, u32[]{:S(2)}) %collective-permute-start.46) | collective-permute-done | bytes 524320 | tf_op jit(solution)/shard_map/ppermute | solution.py:78
  489.9 5.8 collective-permute-done.49
  521.2 4.6 collective-permute-done.64
  527.5 7.2 %collective-permute-done.60 = bf16[256,1024]{1,0:T(8,128)(2,1)S(1)} collective-permute-done((bf16[256,1024]{1,0:T(8,128)(2,1)S(1)}, bf16[256,1024]{1,0:T(8,128)(2,1)S(1)}, u32[]{:S(2)}, u32[]{:S(2)}) %collective-permute-start.60) | collective-permute-done | bytes 524320 | tf_op jit(solution)/shard_map/ppermute | solution.py:54
  551.1 8.3 %collective-permute-done.67 = bf16[128,2048]{1,0:T(8,128)(2,1)} collective-permute-done((bf16[128,2048]{1,0:T(8,128)(2,1)}, bf16[128,2048]{1,0:T(8,128)(2,1)}, u32[]{:S(2)}, u32[]{:S(2)}) %collective-permute-start.67) | collective-permute-done | bytes 524320 | tf_op jit(solution)/shard_map/ppermute | solution.py:77
  559.4 7.7 %collective-permute-done.66 = bf16[128,2048]{1,0:T(8,128)(2,1)} collective-permute-done((bf16[128,2048]{1,0:T(8,128)(2,1)}, bf16[128,2048]{1,0:T(8,128)(2,1)}, u32[]{:S(2)}, u32[]{:S(2)}) %collective-permute-start.66) | collective-permute-done | bytes 524320 | tf_op jit(solution)/shard_map/ppermute | solution.py:78
  574.0 4.7 collective-permute-done.69
  (501 shorter events, 273.5 us)
Async XLA Ops:
  7.2 161.9 %all-gather.3.cloned.1.call-start = ((), (), s32[]{:S(2)}) async-start(), calls=%async_computation.1 | async-start | bytes 19464192 | tf_op jit(solution)/shard_map/all_gather | solution.py:623
  10.5 247.6 %all-gather.5.cloned.1.call-start = ((), (), s32[]{:S(2)}) async-start(), calls=%async_computation.2 | async-start | bytes 2621440 | tf_op jit(solution)/shard_map/all_gather | solution.py:640
  12.2 20.8 %collective-permute-start.3 = (bf16[96,1024]{1,0:T(8,128)(2,1)S(1)}, bf16[96,1024]{1,0:T(8,128)(2,1)S(1)}, u32[]{:S(2)}, u32[]{:S(2)}) collective-permute-start(bf16[96,1024]{1,0:T(8,128)(2,1)S(1)} %get-tuple-element.168), channel_id=1, source_target_pairs={{0,1},{1,0},{2,3},{3,2},{4,5},{5,4},{6,7},{7,6},{8,9},{9,8},{10,11... | collective-permute-start | bytes 589832 | tf_op jit(solution)/shard_map/ppermute | solution.py:78
  26.9 26.4 %collective-permute-start.9 = (bf16[320,384]{1,0:T(8,128)(2,1)}, bf16[320,384]{1,0:T(8,128)(2,1)S(1)}, u32[]{:S(2)}, u32[]{:S(2)}) collective-permute-start(bf16[320,384]{1,0:T(8,128)(2,1)} %bitcast.239), channel_id=1, source_target_pairs={{0,4},{4,8},{8,12},{12,0},{1,5},{5,9},{9,13},{13,1},{2,6},{6,10},{... | collective-permute-start | bytes 737288 | tf_op jit(solution)/shard_map/ppermute | solution.py:54
  28.5 26.1 %collective-permute-start.10 = (bf16[320,384]{1,0:T(8,128)(2,1)}, bf16[320,384]{1,0:T(8,128)(2,1)S(1)}, u32[]{:S(2)}, u32[]{:S(2)}) collective-permute-start(bf16[320,384]{1,0:T(8,128)(2,1)} %bitcast.240), channel_id=1, source_target_pairs={{0,8},{4,12},{8,0},{12,4},{1,9},{5,13},{9,1},{13,5},{2,10},{6,14},... | collective-permute-start | bytes 737288 | tf_op jit(solution)/shard_map/ppermute | solution.py:54
  31.1 23.5 %collective-permute-start.11 = (bf16[320,384]{1,0:T(8,128)(2,1)}, bf16[320,384]{1,0:T(8,128)(2,1)S(1)}, u32[]{:S(2)}, u32[]{:S(2)}) collective-permute-start(bf16[320,384]{1,0:T(8,128)(2,1)} %bitcast.241), channel_id=1, source_target_pairs={{0,12},{4,0},{8,4},{12,8},{1,13},{5,1},{9,5},{13,9},{2,14},{6,2},{... | collective-permute-start | bytes 737288 | tf_op jit(solution)/shard_map/ppermute | solution.py:54
  48.6 31.1 %collective-permute-start.1 = (bf16[128,2048]{1,0:T(8,128)(2,1)S(1)}, bf16[128,2048]{1,0:T(8,128)(2,1)S(1)}, u32[]{:S(2)}, u32[]{:S(2)}) collective-permute-start(bf16[128,2048]{1,0:T(8,128)(2,1)S(1)} %bitcast.210), channel_id=1, source_target_pairs={{0,2},{2,0},{1,3},{3,1},{4,6},{6,4},{5,7},{7,5},{8,10},{10,8},{9,1... | collective-permute-start | bytes 1572872 | tf_op jit(solution)/shard_map/ppermute | solution.py:78
  53.3 26.4 %collective-permute-start.2 = (bf16[128,2048]{1,0:T(8,128)(2,1)S(1)}, bf16[128,2048]{1,0:T(8,128)(2,1)}, u32[]{:S(2)}, u32[]{:S(2)}) collective-permute-start(bf16[128,2048]{1,0:T(8,128)(2,1)S(1)} %bitcast.211), channel_id=1, source_target_pairs={{0,3},{1,2},{2,1},{3,0},{4,7},{5,6},{6,5},{7,4},{8,11},{9,10},{10,... | collective-permute-start | bytes 1572872 | tf_op jit(solution)/shard_map/ppermute | solution.py:77
  59.0 35.0 %collective-permute-start.12 = (bf16[1280,384]{1,0:T(8,128)(2,1)}, bf16[1280,384]{1,0:T(8,128)(2,1)}, u32[]{:S(2)}, u32[]{:S(2)}) collective-permute-start(bf16[1280,384]{1,0:T(8,128)(2,1)} %bitcast.220), channel_id=1, source_target_pairs={{0,16},{16,0},{1,17},{17,1},{2,18},{18,2},{3,19},{19,3},{4,20},{20... | collective-permute-start | bytes 2949128 | tf_op jit(solution)/shard_map/ppermute | solution.py:54
  62.9 21.1 %collective-permute-start.20 = (bf16[128,1024]{1,0:T(8,128)(2,1)}, bf16[128,1024]{1,0:T(8,128)(2,1)}, u32[]{:S(2)}, u32[]{:S(2)}) collective-permute-start(bf16[128,1024]{1,0:T(8,128)(2,1)} %collective-permute-done.19), channel_id=1, source_target_pairs={{0,4},{4,8},{8,12},{12,0},{1,5},{5,9},{9,13},{13,1},{2,6},{6,10},{... | collective-permute-start | bytes 786440 | tf_op jit(solution)/shard_map/ppermute | solution.py:54
  121.7 19.8 %collective-permute-start.28 = (bf16[256,1024]{1,0:T(8,128)(2,1)}, bf16[256,1024]{1,0:T(8,128)(2,1)S(1)}, u32[]{:S(2)}, u32[]{:S(2)}) collective-permute-start(bf16[256,1024]{1,0:T(8,128)(2,1)} %collective-permute-done.27), channel_id=1, source_target_pairs={{0,4},{4,8},{8,12},{12,0},{1,5},{5,9},{9,13},{13,1},{2,6},{6,10},{... | collective-permute-start | bytes 1572872 | tf_op jit(solution)/shard_map/ppermute | solution.py:54
  139.7 21.6 %collective-permute-start.22 = (bf16[512,1024]{1,0:T(8,128)(2,1)}, bf16[512,1024]{1,0:T(8,128)(2,1)}, u32[]{:S(2)}, u32[]{:S(2)}) collective-permute-start(bf16[512,1024]{1,0:T(8,128)(2,1)} %bitcast.216), channel_id=1, source_target_pairs={{0,16},{16,0},{1,17},{17,1},{2,18},{18,2},{3,19},{19,3},{4,20},{20... | collective-permute-start | bytes 3145736 | tf_op jit(solution)/shard_map/ppermute | solution.py:54
  146.9 48.8 %collective-permute-start.29 = (bf16[1024,1024]{1,0:T(8,128)(2,1)}, bf16[1024,1024]{1,0:T(8,128)(2,1)}, u32[]{:S(2)}, u32[]{:S(2)}) collective-permute-start(bf16[1024,1024]{1,0:T(8,128)(2,1)} %bitcast.212), channel_id=1, source_target_pairs={{0,16},{16,0},{1,17},{17,1},{2,18},{18,2},{3,19},{19,3},{4,20},{20... | collective-permute-start | bytes 6291464 | tf_op jit(solution)/shard_map/ppermute | solution.py:54
  157.4 25.6 %collective-permute-start.24 = (bf16[2048,128]{1,0:T(8,128)(2,1)}, bf16[2048,128]{1,0:T(8,128)(2,1)}, u32[]{:S(2)}, u32[]{:S(2)}) collective-permute-start(bf16[2048,128]{1,0:T(8,128)(2,1)} %bitcast.256), channel_id=1, source_target_pairs={{0,2},{2,0},{1,3},{3,1},{4,6},{6,4},{5,7},{7,5},{8,10},{10,8},{9,1... | collective-permute-start | bytes 1572872 | tf_op jit(solution)/shard_map/ppermute | solution.py:78
  157.6 25.4 %collective-permute-start.25 = (bf16[2048,128]{1,0:T(8,128)(2,1)}, bf16[2048,128]{1,0:T(8,128)(2,1)}, u32[]{:S(2)}, u32[]{:S(2)}) collective-permute-start(bf16[2048,128]{1,0:T(8,128)(2,1)} %bitcast.257), channel_id=1, source_target_pairs={{0,3},{1,2},{2,1},{3,0},{4,7},{5,6},{6,5},{7,4},{8,11},{9,10},{10,... | collective-permute-start | bytes 1572872 | tf_op jit(solution)/shard_map/ppermute | solution.py:77
  169.1 444.8 %reduce-scatter.2.cloned.1.call-start = ((), (), s32[]{:S(2)}) async-start(), calls=%async_computation.3 | async-start | bytes 19464192 | tf_op jit(solution)/shard_map/reduce_scatter | solution.py:710
  209.8 24.4 %collective-permute-start.31 = (bf16[128,2048]{1,0:T(8,128)(2,1)}, bf16[128,2048]{1,0:T(8,128)(2,1)S(1)}, u32[]{:S(2)}, u32[]{:S(2)}) collective-permute-start(bf16[128,2048]{1,0:T(8,128)(2,1)} %get-tuple-element.151), channel_id=1, source_target_pairs={{0,2},{2,0},{1,3},{3,1},{4,6},{6,4},{5,7},{7,5},{8,10},{10,8},{9,1... | collective-permute-start | bytes 1572872 | tf_op jit(solution)/shard_map/ppermute | solution.py:78
  210.6 24.3 %collective-permute-start.30 = (bf16[128,2048]{1,0:T(8,128)(2,1)}, bf16[128,2048]{1,0:T(8,128)(2,1)}, u32[]{:S(2)}, u32[]{:S(2)}) collective-permute-start(bf16[128,2048]{1,0:T(8,128)(2,1)} %get-tuple-element.149), channel_id=1, source_target_pairs={{0,1},{1,0},{2,3},{3,2},{4,5},{5,4},{6,7},{7,6},{8,9},{9,8},{10,11... | collective-permute-start | bytes 1572872 | tf_op jit(solution)/shard_map/ppermute | solution.py:78
  276.9 34.9 %collective-permute-start.34 = (bf16[128,2048]{1,0:T(8,128)(2,1)}, bf16[128,2048]{1,0:T(8,128)(2,1)S(1)}, u32[]{:S(2)}, u32[]{:S(2)}) collective-permute-start(bf16[128,2048]{1,0:T(8,128)(2,1)} %get-tuple-element.94), channel_id=1, source_target_pairs={{0,4},{4,8},{8,12},{12,0},{1,5},{5,9},{9,13},{13,1},{2,6},{6,10},{... | collective-permute-start | bytes 1572872 | tf_op jit(solution)/shard_map/ppermute | solution.py:54
  358.4 25.2 %collective-permute-start.40 = (bf16[128,2048]{1,0:T(8,128)(2,1)}, bf16[128,2048]{1,0:T(8,128)(2,1)S(1)}, u32[]{:S(2)}, u32[]{:S(2)}) collective-permute-start(bf16[128,2048]{1,0:T(8,128)(2,1)} %copy-done.19), channel_id=1, source_target_pairs={{0,2},{2,0},{1,3},{3,1},{4,6},{6,4},{5,7},{7,5},{8,10},{10,8},{9,1... | collective-permute-start | bytes 1572872 | tf_op jit(solution)/shard_map/ppermute | solution.py:78
  359.8 23.8 %collective-permute-start.41 = (bf16[128,2048]{1,0:T(8,128)(2,1)}, bf16[128,2048]{1,0:T(8,128)(2,1)S(1)}, u32[]{:S(2)}, u32[]{:S(2)}) collective-permute-start(bf16[128,2048]{1,0:T(8,128)(2,1)} %copy-done.19), channel_id=1, source_target_pairs={{0,3},{1,2},{2,1},{3,0},{4,7},{5,6},{6,5},{7,4},{8,11},{9,10},{10,... | collective-permute-start | bytes 1572872 | tf_op jit(solution)/shard_map/ppermute | solution.py:77
  374.9 20.7 %collective-permute-start.44 = (bf16[128,2048]{1,0:T(8,128)(2,1)S(1)}, bf16[128,2048]{1,0:T(8,128)(2,1)S(1)}, u32[]{:S(2)}, u32[]{:S(2)}) collective-permute-start(bf16[128,2048]{1,0:T(8,128)(2,1)S(1)} %add_convert_fusion.7), channel_id=1, source_target_pairs={{0,4},{4,8},{8,12},{12,0},{1,5},{5,9},{9,13},{13,1},{2,6},{6,10},{... | collective-permute-start | bytes 1572872 | tf_op jit(solution)/shard_map/ppermute | solution.py:54
  392.3 85.1 %collective-permute-start.42 = (bf16[1024,1024]{1,0:T(8,128)(2,1)}, bf16[1024,1024]{1,0:T(8,128)(2,1)}, u32[]{:S(2)}, u32[]{:S(2)}) collective-permute-start(bf16[1024,1024]{1,0:T(8,128)(2,1)} %convolution_convert_fusion), channel_id=1, source_target_pairs={{0,16},{16,0},{1,17},{17,1},{2,18},{18,2},{3,19},{19,3},{4,20},{20... | collective-permute-start | bytes 6291464 | tf_op jit(solution)/shard_map/ppermute | solution.py:54
  414.0 51.6 %collective-permute-start.61 = (bf16[512,1024]{1,0:T(8,128)(2,1)}, bf16[512,1024]{1,0:T(8,128)(2,1)}, u32[]{:S(2)}, u32[]{:S(2)}) collective-permute-start(bf16[512,1024]{1,0:T(8,128)(2,1)} %convolution_convert_fusion.1), channel_id=1, source_target_pairs={{0,16},{16,0},{1,17},{17,1},{2,18},{18,2},{3,19},{19,3},{4,20},{20... | collective-permute-start | bytes 3145736 | tf_op jit(solution)/shard_map/ppermute | solution.py:54
  416.7 27.2 %collective-permute-start.48 = (bf16[2048,128]{1,0:T(8,128)(2,1)}, bf16[2048,128]{1,0:T(8,128)(2,1)}, u32[]{:S(2)}, u32[]{:S(2)}) collective-permute-start(bf16[2048,128]{1,0:T(8,128)(2,1)} %get-tuple-element.158), channel_id=1, source_target_pairs={{0,3},{1,2},{2,1},{3,0},{4,7},{5,6},{6,5},{7,4},{8,11},{9,10},{10,... | collective-permute-start | bytes 1572872 | tf_op jit(solution)/shard_map/ppermute | solution.py:77
  418.2 36.8 %collective-permute-start.47 = (bf16[2048,128]{1,0:T(8,128)(2,1)}, bf16[2048,128]{1,0:T(8,128)(2,1)}, u32[]{:S(2)}, u32[]{:S(2)}) collective-permute-start(bf16[2048,128]{1,0:T(8,128)(2,1)} %get-tuple-element.159), channel_id=1, source_target_pairs={{0,2},{2,0},{1,3},{3,1},{4,6},{6,4},{5,7},{7,5},{8,10},{10,8},{9,1... | collective-permute-start | bytes 1572872 | tf_op jit(solution)/shard_map/ppermute | solution.py:78
  419.7 42.6 %collective-permute-start.46 = (bf16[2048,128]{1,0:T(8,128)(2,1)}, bf16[2048,128]{1,0:T(8,128)(2,1)}, u32[]{:S(2)}, u32[]{:S(2)}) collective-permute-start(bf16[2048,128]{1,0:T(8,128)(2,1)} %get-tuple-element.157), channel_id=1, source_target_pairs={{0,1},{1,0},{2,3},{3,2},{4,5},{5,4},{6,7},{7,6},{8,9},{9,8},{10,11... | collective-permute-start | bytes 1572872 | tf_op jit(solution)/shard_map/ppermute | solution.py:78
  472.3 23.5 %collective-permute-start.49 = (bf16[128,1024]{1,0:T(8,128)(2,1)S(1)}, bf16[128,1024]{1,0:T(8,128)(2,1)S(1)}, u32[]{:S(2)}, u32[]{:S(2)}) collective-permute-start(bf16[128,1024]{1,0:T(8,128)(2,1)S(1)} %get-tuple-element.154), channel_id=1, source_target_pairs={{0,1},{1,0},{2,3},{3,2},{4,5},{5,4},{6,7},{7,6},{8,9},{9,8},{10,11... | collective-permute-start | bytes 786440 | tf_op jit(solution)/shard_map/ppermute | solution.py:78
  477.3 26.3 %collective-permute-start.56 = (bf16[512,128]{1,0:T(8,128)(2,1)S(1)}, bf16[512,128]{1,0:T(8,128)(2,1)S(1)}, u32[]{:S(2)}, u32[]{:S(2)}) collective-permute-start(bf16[512,128]{1,0:T(8,128)(2,1)S(1)} %add_convert_fusion.18), channel_id=1, source_target_pairs={{0,4},{4,8},{8,12},{12,0},{1,5},{5,9},{9,13},{13,1},{2,6},{6,10},{... | collective-permute-start | bytes 393224 | tf_op jit(solution)/shard_map/ppermute | solution.py:54
  477.4 34.0 %collective-permute-start.63 = (bf16[128,1024]{1,0:T(8,128)(2,1)S(1)}, bf16[128,1024]{1,0:T(8,128)(2,1)}, u32[]{:S(2)}, u32[]{:S(2)}) collective-permute-start(bf16[128,1024]{1,0:T(8,128)(2,1)S(1)} %add_convert_fusion.12), channel_id=1, source_target_pairs={{0,4},{4,8},{8,12},{12,0},{1,5},{5,9},{9,13},{13,1},{2,6},{6,10},{... | collective-permute-start | bytes 786440 | tf_op jit(solution)/shard_map/ppermute | solution.py:54
  544.7 22.4 %collective-permute-start.66 = (bf16[128,2048]{1,0:T(8,128)(2,1)}, bf16[128,2048]{1,0:T(8,128)(2,1)}, u32[]{:S(2)}, u32[]{:S(2)}) collective-permute-start(bf16[128,2048]{1,0:T(8,128)(2,1)} %get-tuple-element.148), channel_id=1, source_target_pairs={{0,2},{2,0},{1,3},{3,1},{4,6},{6,4},{5,7},{7,5},{8,10},{10,8},{9,1... | collective-permute-start | bytes 1572872 | tf_op jit(solution)/shard_map/ppermute | solution.py:78
  546.1 21.0 %collective-permute-start.65 = (bf16[128,2048]{1,0:T(8,128)(2,1)}, bf16[128,2048]{1,0:T(8,128)(2,1)}, u32[]{:S(2)}, u32[]{:S(2)}) collective-permute-start(bf16[128,2048]{1,0:T(8,128)(2,1)} %get-tuple-element.146), channel_id=1, source_target_pairs={{0,1},{1,0},{2,3},{3,2},{4,5},{5,4},{6,7},{7,6},{8,9},{9,8},{10,11... | collective-permute-start | bytes 1572872 | tf_op jit(solution)/shard_map/ppermute | solution.py:78
  (154 other events, 1563.9 us)
Sparse Core Ops, SparseCore 0:
  10.6 125.1 all-gather.2
  169.3 46.4 all-gather.4
  357.5 149.3 reduce-scatter.1
